TPU v7x, 512 devices: a whole 4x4x16 slice. The times are simulated.
512 devices in a mesh: slab: 128 (over y, z, core), rep: 4 (over x).
Axes of the slice: x: 4, y: 4, z: 16, core: 2. Of those that a mesh axis runs over, the one named last changes fastest.
Arguments:
- camera_rows: float32 [655360, 128], P(('slab', 'rep')), may hold values from 0.1 to 4
- blend: float32 [655360], P(('slab', 'rep')), may hold values from 0.2 to 5
- route: int32 [655360], P(('slab', 'rep')), may hold values from 0 to 3, as said below
- line: int32 [655360], P(('slab', 'rep')), may hold values from 0 to 1023, as said below
- start: float32 [128, 1024, 512], P('slab', None, 'rep'), may hold values from 0.5 to 2
- psf_xy: float32 [31], replicated, may hold values from 0.05 to 1
- psf_z: float32 [63], replicated, may hold values from 0.05 to 1
Outputs:
- estimate: float32 [128, 1024, 512], P('slab', None, 'rep')
Inputs may be any that keep to these rules, and one draw needn't show every extreme that they name: `route`: of the rows of one device, exactly 512 go to one owner, the same owner for all devices of one slab index, and exactly 256 to each other owner. A line is z * 1024 + x for local plane z of the owner. Every line of every owner is named by at least one row of its slab index.
All inputs are finite; a program needn't handle non-finite values.
Results may differ from a plain program's by a relative error of at most 0.0001.
Values sent between devices are 32-bit elements; how exact they have to be, the bound alone decides.
No kernel may reach another device: no remote copies, remote signals or barrier semaphores. Data moves between devices by JAX's collectives and lax.ppermute only.
A program may use at most 128 MiB of HBM per device.

v0:
```python
import functools

import jax
import jax.numpy as jnp
from jax import lax
from jax.experimental import pallas as pl
from jax.experimental.pallas import tpu as pltpu
from jax.sharding import PartitionSpec as P

F32 = jnp.float32
BF16 = jnp.bfloat16
LANES = 128
SIDE = 32
TAPS = 31
RIM = TAPS // 2
OWNERS = 4
CAPACITY = 512
META = 8
LINES = 1024
Z = 128
VMEM_LIMIT = 40 * 1024 * 1024


def call(kernel, out_shapes, scratch, *args, smem=0):
    specs = [
        pl.BlockSpec(memory_space=pltpu.SMEM if i < smem else pltpu.VMEM)
        for i in range(len(args))
    ]
    outs = tuple(jax.ShapeDtypeStruct(s, F32) for s in out_shapes)
    return pl.pallas_call(
        kernel,
        out_shape=outs,
        in_specs=specs,
        out_specs=tuple(pl.BlockSpec(memory_space=pltpu.VMEM) for _ in outs),
        scratch_shapes=[pltpu.VMEM(s, d) for s, d in scratch],
        compiler_params=pltpu.CompilerParams(vmem_limit_bytes=VMEM_LIMIT),
        name=kernel.func.__name__ if isinstance(kernel, functools.partial) else kernel.__name__,
    )(*args)


def halves(value):
    high = value.astype(BF16)
    return high, (value - high.astype(F32)).astype(BF16)


def thirds(value):
    high, rest = halves(value)
    low = (value - high.astype(F32) - rest.astype(F32)).astype(BF16)
    return high, rest, low


def lane_blocks(groups):
    block = lax.broadcasted_iota(jnp.int32, groups[0].shape, 2) // SIDE
    outs = []
    for sub in range(4):
        out = groups[sub]
        for j in range(4):
            if j != sub:
                moved = pltpu.roll(groups[j], (SIDE * (j - sub)) % LANES, axis=2)
                out = jnp.where(block == j, moved, out)
        outs.append(out)
    return outs


def store_tiles(plane, out_ref):
    cube = plane.reshape(32, SIDE, LANES)
    for sub, out in enumerate(lane_blocks([cube[:, 8 * j : 8 * j + 8, :] for j in range(4)])):
        out_ref[32 * sub : 32 * sub + 32] = out


def tiles_of_start(start_ref, taps_ref, out_ref, band_ref):
    store_tiles(start_ref[...], out_ref)
    rows = jnp.broadcast_to(taps_ref[...], (Z, LANES))
    rolled = pltpu.roll(rows, LANES - 31, axis=1, stride=1, stride_axis=0)
    j = lax.broadcasted_iota(jnp.int32, (Z, LANES), 0)
    z = lax.broadcasted_iota(jnp.int32, (Z, LANES), 1)
    band_ref[...] = jnp.where(jnp.abs(j - z) <= 31, rolled, 0.0)


def pack_rows(rows_ref, blend_ref, route_ref, line_ref, out_ref, split_ref, hot_ref):
    chunks = rows_ref.shape[0] // LANES
    blend = blend_ref[...]
    route = route_ref[...]
    line = line_ref[...]
    i = lax.broadcasted_iota(jnp.int32, (LANES, LANES), 0)
    j = lax.broadcasted_iota(jnp.int32, (LANES, LANES), 1)
    upto = (i <= j).astype(BF16)
    ones = jnp.ones((LANES, LANES), BF16)
    ci = lax.broadcasted_iota(jnp.int32, (16, 16), 0)
    cj = lax.broadcasted_iota(jnp.int32, (16, 16), 1)
    before = (cj < ci).astype(BF16)
    key = route * CAPACITY
    for owner in range(OWNERS):
        mine = (route == owner).astype(F32)
        mine16 = jnp.concatenate([mine, jnp.zeros((16 - chunks, LANES), F32)], axis=0).astype(BF16)
        upto_here = jnp.dot(mine16, upto, preferred_element_type=F32)
        totals = jnp.dot(mine16, ones, preferred_element_type=F32).astype(BF16)
        offset = jnp.dot(before, totals, preferred_element_type=F32)
        rank = (upto_here + offset)[:chunks] - 1.0
        key = key + jnp.where(route == owner, rank, 0.0).astype(jnp.int32)
    square = jnp.concatenate([blend, jnp.zeros((LANES - chunks, LANES), F32)], axis=0)
    columns = square.T
    for c in range(chunks):
        weighted = rows_ref[c * LANES : (c + 1) * LANES, :] * columns[:, c : c + 1]
        high, low = halves(weighted)
        split_ref[c * LANES : (c + 1) * LANES, :LANES] = high
        split_ref[c * LANES : (c + 1) * LANES, LANES:] = low
    first, second, third = thirds(blend)
    upper = line // 32
    parts = [first, second, third, upper.astype(BF16), (line - upper * 32).astype(BF16)]
    notes = jnp.concatenate(
        [
            jnp.concatenate(
                [p.astype(F32)[c : c + 1] for p in parts] + [jnp.zeros((3, LANES), F32)], axis=0
            )
            for c in range(chunks)
        ],
        axis=1,
    ).astype(BF16)
    for owner in range(OWNERS):
        slot = lax.broadcasted_iota(jnp.int32, (CAPACITY, LANES), 0) + owner * CAPACITY
        for c in range(chunks):
            hot = jnp.where(slot == key[c : c + 1, :], 1.0, 0.0)
            hot_ref[:, c * LANES : (c + 1) * LANES] = hot.astype(BF16)
        hot = hot_ref[...]
        both = jnp.dot(hot, split_ref[...], preferred_element_type=F32)
        out_ref[owner, :CAPACITY, :] = both[:, :LANES] + both[:, LANES:]
        meta = lax.dot_general(
            notes, hot, (((1,), (1,)), ((), ())), preferred_element_type=F32
        )
        weight = meta[0:1] + meta[1:2] + meta[2:3]
        where = meta[3:4] * 32.0 + meta[4:5]
        out_ref[owner, CAPACITY:, :] = jnp.concatenate(
            [weight[:, q * LANES : (q + 1) * LANES] for q in range(4)]
            + [where[:, q * LANES : (q + 1) * LANES] for q in range(4)],
            axis=0,
        )


def observe(got_ref, out_ref, hot_ref):
    total = jnp.zeros((LINES, 2 * LANES), F32)
    weights = jnp.zeros((LINES, 8), F32)
    at = lax.broadcasted_iota(jnp.int32, (LINES, LANES), 0)
    for source in range(OWNERS):
        meta = got_ref[source, CAPACITY:, :]
        where = meta[4:8].astype(jnp.int32)
        for q in range(4):
            hot = jnp.where(at == where[q : q + 1, :], 1.0, 0.0)
            hot_ref[:, q * LANES : (q + 1) * LANES] = hot.astype(BF16)
        hot = hot_ref[...]
        high, low = halves(got_ref[source, :CAPACITY, :])
        total += jnp.dot(hot, jnp.concatenate([high, low], axis=1), preferred_element_type=F32)
        weight = jnp.concatenate([meta[q : q + 1] for q in range(4)], axis=1)
        parts = [p.astype(F32) for p in thirds(weight)]
        stacked = jnp.concatenate(parts + [jnp.zeros((5, CAPACITY), F32)], axis=0).astype(BF16)
        weights += lax.dot_general(
            hot, stacked, (((1,), (1,)), ((), ())), preferred_element_type=F32
        )
    weight_sum = weights[:, 0:1] + weights[:, 1:2] + weights[:, 2:3]
    store_tiles((total[:, :LANES] + total[:, LANES:]) / weight_sum, out_ref)


def columns_from(got_ref, out_ref):
    for i in range(8):
        turned = got_ref[pl.ds(i, Z, stride=8), :].T
        for j in range(4):
            out_ref[8 * j + i] = turned[SIDE * j : SIDE * j + SIDE, :]


def arrive(got_ref, out_ref, low_ref, high_ref):
    columns_from(got_ref, out_ref)
    low_ref[...] = out_ref[:RIM]
    high_ref[...] = out_ref[SIDE - RIM :]


def convolve(taps_ref, flip, low_ref, mid_ref, high_ref, wide_ref, flat_ref):
    wide_ref[:RIM] = low_ref[...]
    wide_ref[RIM : RIM + SIDE] = mid_ref[...]
    wide_ref[RIM + SIDE :] = high_ref[...]
    taps = [taps_ref[TAPS - 1 - k if flip else k] for k in range(TAPS)]

    def block(index, carry):
        lead = (index // 4) * 8
        row = pl.multiple_of((index % 4) * 8, 8)
        total = taps[0] * wide_ref[pl.ds(lead, 8), pl.ds(row, 8), :]
        for k in range(1, TAPS):
            total = total + taps[k] * wide_ref[pl.ds(lead + k, 8), pl.ds(row, 8), :]
        for i in range(8):
            flat_ref[pl.ds(pl.multiple_of((lead + i) * SIDE + row, 8), 8), :] = total[i]
        return carry

    lax.fori_loop(0, 16, block, 0)


def along_x(flip, taps_ref, low_ref, mid_ref, high_ref, out_ref, first_ref, last_ref, wide_ref, flat_ref):
    convolve(taps_ref, flip, low_ref, mid_ref, high_ref, wide_ref, flat_ref)
    for y in range(SIDE):
        out_ref[y] = flat_ref[pl.ds(y, SIDE, stride=SIDE), :]
    first_ref[...] = out_ref[:RIM]
    last_ref[...] = out_ref[SIDE - RIM :]


def along_y(taps_ref, flip, low_ref, mid_ref, high_ref, wide_ref, flat_ref, out_ref):
    convolve(taps_ref, flip, low_ref, mid_ref, high_ref, wide_ref, flat_ref)
    for x in range(SIDE):
        out_ref[SIDE * x : SIDE * x + SIDE, :] = flat_ref[pl.ds(x, SIDE, stride=SIDE), :]


def axial(value, band, back):
    return lax.dot_general(
        value,
        band,
        (((1,), (1 if back else 0,)), ((), ())),
        precision=lax.Precision.HIGHEST,
        preferred_element_type=F32,
    )


def blur(taps_ref, low_ref, mid_ref, high_ref, band_ref, out_ref, wide_ref, flat_ref, cols_ref):
    along_y(taps_ref, False, low_ref, mid_ref, high_ref, wide_ref, flat_ref, cols_ref)
    out_ref[...] = axial(cols_ref[...], band_ref[...], False)


def back_axial(ratio, band_ref, out_ref, first_ref, last_ref):
    back = axial(ratio, band_ref[...], True)
    out_ref[...] = back.reshape(SIDE, SIDE, Z)
    first_ref[...] = back[: RIM * SIDE].reshape(RIM, SIDE, Z)
    last_ref[...] = back[(SIDE - RIM) * SIDE :].reshape(RIM, SIDE, Z)


def first_ratio(got_ref, blurred_ref, band_ref, seen_ref, out_ref, first_ref, last_ref):
    columns_from(got_ref, seen_ref)
    ratio = seen_ref[...].reshape(SIDE * SIDE, Z) / blurred_ref[...]
    back_axial(ratio, band_ref, out_ref, first_ref, last_ref)


def blur_ratio(
    taps_ref, low_ref, mid_ref, high_ref, band_ref, seen_ref, out_ref, first_ref, last_ref, wide_ref, flat_ref, cols_ref
):
    along_y(taps_ref, False, low_ref, mid_ref, high_ref, wide_ref, flat_ref, cols_ref)
    blurred = axial(cols_ref[...], band_ref[...], False)
    back_axial(seen_ref[...].reshape(SIDE * SIDE, Z) / blurred, band_ref, out_ref, first_ref, last_ref)


def update(
    taps_ref, low_ref, mid_ref, high_ref, estimate_ref, out_ref, first_ref, last_ref, wide_ref, flat_ref, cols_ref
):
    along_y(taps_ref, True, low_ref, mid_ref, high_ref, wide_ref, flat_ref, cols_ref)
    out_ref[...] = estimate_ref[...] * cols_ref[...].reshape(SIDE, SIDE, Z)
    first_ref[...] = out_ref[:RIM]
    last_ref[...] = out_ref[SIDE - RIM :]


def last_update(
    taps_ref, low_ref, mid_ref, high_ref, estimate_ref, out_ref, wide_ref, flat_ref, cols_ref
):
    along_y(taps_ref, True, low_ref, mid_ref, high_ref, wide_ref, flat_ref, cols_ref)
    for i in range(8):
        block = jnp.concatenate(
            [
                estimate_ref[8 * j + i] * cols_ref[SIDE * (8 * j + i) : SIDE * (8 * j + i) + SIDE, :]
                for j in range(4)
            ],
            axis=0,
        )
        out_ref[pl.ds(i, Z, stride=8), :] = block.T


def plane_of(got_ref, out_ref):
    outs = lane_blocks([got_ref[32 * sub : 32 * sub + 32] for sub in range(4)])
    for j, out in enumerate(outs):
        out_ref[:, 8 * j : 8 * j + 8, :] = out


TILE = (SIDE, SIDE, Z)
EDGE = (RIM, SIDE, Z)
PIECES = (Z, 8, LANES)
FLAT = (SIDE * SIDE, Z)
SCRATCH = [((SIDE + 2 * RIM, SIDE, Z), F32), (FLAT, F32), (FLAT, F32)]


def exchange(first, last, pairs, axes):
    low = lax.ppermute(last, axes, pairs)
    high = lax.ppermute(first, axes, [(b, a) for a, b in pairs])
    return low, high


def shards(camera_rows, blend, route, line, start, psf_xy, psf_z):
    slabs, reps = lax.axis_size("slab"), lax.axis_size("rep")
    x_tiles = LINES // SIDE
    y_tiles = slabs // x_tiles
    chunks = camera_rows.shape[0] // LANES
    x_pairs = [(t, t + 1) for t in range(slabs) if t % x_tiles != x_tiles - 1]
    y_pairs = []
    for t in range(slabs):
        for r in range(reps):
            y = r * y_tiles + t // x_tiles + 1
            if y < y_tiles * reps:
                up = (y % y_tiles) * x_tiles + t % x_tiles
                y_pairs.append((t * reps + r, up * reps + y // y_tiles))

    def rims_x(first, last):
        return exchange(first, last, x_pairs, "slab")

    def rims_y(first, last):
        return exchange(first, last, y_pairs, ("slab", "rep"))

    def turn(pieces):
        return lax.all_to_all(pieces, "slab", split_axis=0, concat_axis=0, tiled=True)

    taps = psf_xy / jnp.sum(psf_xy)
    taps_z = jnp.pad((psf_z / jnp.sum(psf_z))[::-1], (0, LANES - psf_z.shape[0]))[None, :]

    sent = call(
        pack_rows,
        [(OWNERS, CAPACITY + META, LANES)],
        [((chunks * LANES, 2 * LANES), BF16), ((CAPACITY, chunks * LANES), BF16)],
        camera_rows,
        blend.reshape(chunks, LANES),
        route.reshape(chunks, LANES),
        line.reshape(chunks, LANES),
    )[0]
    got = lax.all_to_all(sent, "rep", split_axis=0, concat_axis=0, tiled=True)
    pieces, band = call(
        tiles_of_start, [PIECES, (Z, LANES)], [], start.reshape(LINES, LANES), taps_z
    )
    arrived = turn(pieces)
    seen_pieces = call(observe, [PIECES], [((LINES, CAPACITY), BF16)], got)[0]
    seen_arrived = turn(seen_pieces)

    estimate, first, last = call(
        arrive, [TILE, EDGE, EDGE], [], arrived.reshape(Z * 8, LANES)
    )

    def lateral_x(flip, value, first, last):
        low, high = rims_x(first, last)
        value, first, last = call(
            functools.partial(along_x, flip), [TILE, EDGE, EDGE], SCRATCH[:2], taps, low, value, high, smem=1
        )
        low, high = rims_y(first, last)
        return low, value, high

    wide = lateral_x(False, estimate, first, last)
    blurred = call(blur, [FLAT], SCRATCH, taps, *wide, band, smem=1)[0]
    seen, back, first, last = call(
        first_ratio, [TILE, TILE, EDGE, EDGE], [], seen_arrived.reshape(Z * 8, LANES), blurred, band
    )
    wide = lateral_x(True, back, first, last)
    estimate, first, last = call(
        update, [TILE, EDGE, EDGE], SCRATCH, taps, *wide, estimate, smem=1
    )
    wide = lateral_x(False, estimate, first, last)
    back, first, last = call(
        blur_ratio, [TILE, EDGE, EDGE], SCRATCH, taps, *wide, band, seen, smem=1
    )
    wide = lateral_x(True, back, first, last)
    pieces = call(last_update, [(Z * 8, LANES)], SCRATCH, taps, *wide, estimate, smem=1)[0]
    done = turn(pieces.reshape(PIECES))
    plane = call(plane_of, [(LINES // SIDE, SIDE, LANES)], [], done)[0]
    return plane.reshape(1, LINES, LANES)


def solution(mesh):
    in_specs = (
        P(("slab", "rep"), None),
        P(("slab", "rep")),
        P(("slab", "rep")),
        P(("slab", "rep")),
        P("slab", None, "rep"),
        P(),
        P(),
    )
    out_specs = P("slab", None, "rep")
    return jax.shard_map(shards, mesh=mesh, in_specs=in_specs, out_specs=out_specs, check_vma=False)
```

profile of v0, /device:TPU:1, one launch (start us, length us, event | category | flops | bytes accessed | tf_op | source)
XLA Modules:
  0.0 273.2 jit_solution(16087251644264991382)
XLA Ops:
  0.0 1.1 copy-done
  1.1 0.7 copy-done.2
  1.8 0.7 copy-done.3
  2.5 0.7 copy-done.4
  3.2 4.9 %pack_rows.1 = f32[4,520,128]{2,1,0:T(8,128)} custom-call(f32[1280,128]{1,0:T(8,128)S(1)} %copy-done, f32[10,128]{1,0:T(8,128)S(1)} %bitcast.14, s32[10,128]{1,0:T(8,128)S(1)} %bitcast.15, s32[10,128]{1,0:T(8,128)S(1)} %bitcast.16), custom_call_target="tpu_custom_call" | custom-call | tf_op jit(solution)/shard_map/pack_rows/pallas_call | solution.py:30
  8.1 5.0 %all-to-all-start = ((f32[4,520,128]{2,1,0:T(8,128)}), f32[4,520,128]{2,1,0:T(8,128)S(1)}, u32[]{:S(2)}, u32[]{:S(2)}) async-start(f32[4,520,128]{2,1,0:T(8,128)} %pack_rows.1), calls=%async_computation | async-start | bytes 2129920 | tf_op jit(solution)/shard_map/all_to_all | solution.py:323
  13.1 0.1 reverse.3
  13.1 0.6 reduce_sum.19
  13.7 0.6 broadcast_divide_fusion
  14.4 0.0 copy-done.1
  14.4 1.3 tiles_of_start.1
  15.7 7.2 %all-to-all-done.got_ref = f32[4,520,128]{2,1,0:T(8,128)S(1)} async-done(((f32[4,520,128]{2,1,0:T(8,128)}), f32[4,520,128]{2,1,0:T(8,128)S(1)}, u32[]{:S(2)}, u32[]{:S(2)}) %all-to-all-start) | async-done | bytes 1064992 | tf_op jit(solution)/shard_map/all_to_all | solution.py:323
  22.9 25.5 %all-to-all-start.2 = ((f32[128,8,128]{2,1,0:T(8,128)}), f32[128,8,128]{2,1,0:T(8,128)S(1)}, u32[]{:S(2)}, u32[]{:S(2)}) async-start(f32[128,8,128]{2,1,0:T(8,128)} %get-tuple-element.32), calls=%async_computation.2 | async-start | bytes 1048576 | tf_op jit(solution)/shard_map/all_to_all | solution.py:309
  48.3 4.3 %observe.1 = f32[128,8,128]{2,1,0:T(8,128)} custom-call(f32[4,520,128]{2,1,0:T(8,128)S(1)} %all-to-all-done.got_ref), custom_call_target="tpu_custom_call" | custom-call | tf_op jit(solution)/shard_map/observe/pallas_call | solution.py:30
  52.6 29.0 %all-to-all-done.2 = f32[128,8,128]{2,1,0:T(8,128)S(1)} async-done(((f32[128,8,128]{2,1,0:T(8,128)}), f32[128,8,128]{2,1,0:T(8,128)S(1)}, u32[]{:S(2)}, u32[]{:S(2)}) %all-to-all-start.2) | async-done | bytes 524320 | tf_op jit(solution)/shard_map/all_to_all | solution.py:309
  81.6 7.2 %all-to-all-start.1 = ((f32[128,8,128]{2,1,0:T(8,128)}), f32[128,8,128]{2,1,0:T(8,128)S(1)}, u32[]{:S(2)}, u32[]{:S(2)}) async-start(f32[128,8,128]{2,1,0:T(8,128)} %observe.1), calls=%async_computation.1 | async-start | bytes 1048576 | tf_op jit(solution)/shard_map/all_to_all | solution.py:309
  88.7 0.2 arrive.1
  88.9 3.5 %collective-permute-start = (f32[15,32,128]{2,1,0:T(8,128)S(1)}, f32[15,32,128]{2,1,0:T(8,128)S(1)}, u32[]{:S(2)}, u32[]{:S(2)}) collective-permute-start(f32[15,32,128]{2,1,0:T(8,128)S(1)} %get-tuple-element.33), channel_id=1, source_target_pairs={{0,4},{4,8},{8,12},{12,16},{16,20},{20,24},{24,28},{28,32},{32,36}... | collective-permute-start | bytes 737288 | tf_op jit(solution)/shard_map/ppermute | solution.py:283
  92.5 1.9 collective-permute-start.1
  94.4 0.0 copy-done.6
  94.4 0.6 reduce_sum.18
  95.0 0.6 broadcast_divide_fusion.1.taps_ref
  95.6 17.6 %collective-permute-done.low_ref = f32[15,32,128]{2,1,0:T(8,128)S(1)} collective-permute-done((f32[15,32,128]{2,1,0:T(8,128)S(1)}, f32[15,32,128]{2,1,0:T(8,128)S(1)}, u32[]{:S(2)}, u32[]{:S(2)}) %collective-permute-start) | collective-permute-done | bytes 245792 | tf_op jit(solution)/shard_map/ppermute | solution.py:283
  113.2 2.6 collective-permute-done.1.high_ref
  115.8 2.4 along_x.4
  118.2 3.2 %collective-permute-start.2 = (f32[15,32,128]{2,1,0:T(8,128)S(1)}, f32[15,32,128]{2,1,0:T(8,128)S(1)}, u32[]{:S(2)}, u32[]{:S(2)}) collective-permute-start(f32[15,32,128]{2,1,0:T(8,128)S(1)} %get-tuple-element.36), channel_id=1, source_target_pairs={{0,128},{1,129},{2,130},{3,131},{4,132},{5,133},{6,134},{7,135},{8... | collective-permute-start | bytes 737288 | tf_op jit(solution)/shard_map/ppermute | solution.py:283
  121.4 1.5 collective-permute-start.3
  122.9 1.6 collective-permute-done.2.low_ref
  124.5 3.8 %collective-permute-done.3.high_ref = f32[15,32,128]{2,1,0:T(8,128)S(1)} collective-permute-done((f32[15,32,128]{2,1,0:T(8,128)S(1)}, f32[15,32,128]{2,1,0:T(8,128)S(1)}, u32[]{:S(2)}, u32[]{:S(2)}) %collective-permute-start.3) | collective-permute-done | bytes 245792 | tf_op jit(solution)/shard_map/ppermute | solution.py:284
  128.4 2.9 %blur.1.blurred_ref = f32[1024,128]{1,0:T(8,128)S(1)} custom-call(f32[31]{0:T(128)S(1)} %broadcast_divide_fusion.1.taps_ref, f32[15,32,128]{2,1,0:T(8,128)S(1)} %collective-permute-done.2.low_ref, f32[32,32,128]{2,1,0:T(8,128)S(1)} %get-tuple-element.37.mid_ref, f32[15,32,128]{2,1,0:T(8,128)S(1)} %collective-permute-done.3.high_ref, ...), custom_call_target="tpu_custom_call" | custom-call | tf_op jit(solution)/shard_map/blur/pallas_call | solution.py:30
  131.3 0.0 all-to-all-done.1
  131.3 0.7 first_ratio.1
  132.0 6.0 %collective-permute-start.4 = (f32[15,32,128]{2,1,0:T(8,128)S(1)}, f32[15,32,128]{2,1,0:T(8,128)S(1)}, u32[]{:S(2)}, u32[]{:S(2)}) collective-permute-start(f32[15,32,128]{2,1,0:T(8,128)S(1)} %get-tuple-element.40), channel_id=1, source_target_pairs={{0,4},{4,8},{8,12},{12,16},{16,20},{20,24},{24,28},{28,32},{32,36}... | collective-permute-start | bytes 737288 | tf_op jit(solution)/shard_map/ppermute | solution.py:283
  138.0 1.9 collective-permute-start.5
  139.9 1.2 collective-permute-done.4.low_ref
  141.1 4.4 %collective-permute-done.5.high_ref = f32[15,32,128]{2,1,0:T(8,128)S(1)} collective-permute-done((f32[15,32,128]{2,1,0:T(8,128)S(1)}, f32[15,32,128]{2,1,0:T(8,128)S(1)}, u32[]{:S(2)}, u32[]{:S(2)}) %collective-permute-start.5) | collective-permute-done | bytes 245792 | tf_op jit(solution)/shard_map/ppermute | solution.py:284
  145.5 2.4 along_x.5
  147.9 3.3 %collective-permute-start.6 = (f32[15,32,128]{2,1,0:T(8,128)S(1)}, f32[15,32,128]{2,1,0:T(8,128)S(1)}, u32[]{:S(2)}, u32[]{:S(2)}) collective-permute-start(f32[15,32,128]{2,1,0:T(8,128)S(1)} %get-tuple-element.43), channel_id=1, source_target_pairs={{0,128},{1,129},{2,130},{3,131},{4,132},{5,133},{6,134},{7,135},{8... | collective-permute-start | bytes 737288 | tf_op jit(solution)/shard_map/ppermute | solution.py:283
  151.3 1.3 collective-permute-start.7
  152.6 1.8 collective-permute-done.6.low_ref
  154.4 3.8 %collective-permute-done.7.high_ref = f32[15,32,128]{2,1,0:T(8,128)S(1)} collective-permute-done((f32[15,32,128]{2,1,0:T(8,128)S(1)}, f32[15,32,128]{2,1,0:T(8,128)S(1)}, u32[]{:S(2)}, u32[]{:S(2)}) %collective-permute-start.7) | collective-permute-done | bytes 245792 | tf_op jit(solution)/shard_map/ppermute | solution.py:284
  158.2 2.4 update.1
  160.6 5.6 %collective-permute-start.8 = (f32[15,32,128]{2,1,0:T(8,128)S(1)}, f32[15,32,128]{2,1,0:T(8,128)S(1)}, u32[]{:S(2)}, u32[]{:S(2)}) collective-permute-start(f32[15,32,128]{2,1,0:T(8,128)S(1)} %get-tuple-element.46), channel_id=1, source_target_pairs={{0,4},{4,8},{8,12},{12,16},{16,20},{20,24},{24,28},{28,32},{32,36}... | collective-permute-start | bytes 737288 | tf_op jit(solution)/shard_map/ppermute | solution.py:283
  166.2 1.9 collective-permute-start.9
  168.2 1.2 collective-permute-done.8.low_ref
  169.3 4.4 %collective-permute-done.9.high_ref = f32[15,32,128]{2,1,0:T(8,128)S(1)} collective-permute-done((f32[15,32,128]{2,1,0:T(8,128)S(1)}, f32[15,32,128]{2,1,0:T(8,128)S(1)}, u32[]{:S(2)}, u32[]{:S(2)}) %collective-permute-start.9) | collective-permute-done | bytes 245792 | tf_op jit(solution)/shard_map/ppermute | solution.py:284
  173.7 2.4 along_x.6
  176.2 3.0 %collective-permute-start.10 = (f32[15,32,128]{2,1,0:T(8,128)S(1)}, f32[15,32,128]{2,1,0:T(8,128)S(1)}, u32[]{:S(2)}, u32[]{:S(2)}) collective-permute-start(f32[15,32,128]{2,1,0:T(8,128)S(1)} %get-tuple-element.49), channel_id=1, source_target_pairs={{0,128},{1,129},{2,130},{3,131},{4,132},{5,133},{6,134},{7,135},{8... | collective-permute-start | bytes 737288 | tf_op jit(solution)/shard_map/ppermute | solution.py:283
  179.1 1.3 collective-permute-start.11
  180.4 1.8 collective-permute-done.10.low_ref
  182.3 4.3 %collective-permute-done.11.high_ref = f32[15,32,128]{2,1,0:T(8,128)S(1)} collective-permute-done((f32[15,32,128]{2,1,0:T(8,128)S(1)}, f32[15,32,128]{2,1,0:T(8,128)S(1)}, u32[]{:S(2)}, u32[]{:S(2)}) %collective-permute-start.11) | collective-permute-done | bytes 245792 | tf_op jit(solution)/shard_map/ppermute | solution.py:284
  186.6 4.1 %blur_ratio.1 = (f32[32,32,128]{2,1,0:T(8,128)S(1)}, f32[15,32,128]{2,1,0:T(8,128)S(1)}, f32[15,32,128]{2,1,0:T(8,128)S(1)}) custom-call(f32[31]{0:T(128)S(1)} %broadcast_divide_fusion.1.taps_ref, f32[15,32,128]{2,1,0:T(8,128)S(1)} %collective-permute-done.10.low_ref, f32[32,32,128]{2,1,0:T(8,128)S(1)} %get-tuple-element.50.mid_ref, ...), custom_call_target="tpu_custom_call" | custom-call | tf_op jit(solution)/shard_map/blur_ratio/pallas_call | solution.py:30
  190.7 5.2 %collective-permute-start.12 = (f32[15,32,128]{2,1,0:T(8,128)S(1)}, f32[15,32,128]{2,1,0:T(8,128)S(1)}, u32[]{:S(2)}, u32[]{:S(2)}) collective-permute-start(f32[15,32,128]{2,1,0:T(8,128)S(1)} %get-tuple-element.53), channel_id=1, source_target_pairs={{0,4},{4,8},{8,12},{12,16},{16,20},{20,24},{24,28},{28,32},{32,36}... | collective-permute-start | bytes 737288 | tf_op jit(solution)/shard_map/ppermute | solution.py:283
  195.9 1.9 collective-permute-start.13
  197.8 1.2 collective-permute-done.12.low_ref
  199.0 4.4 %collective-permute-done.13.high_ref = f32[15,32,128]{2,1,0:T(8,128)S(1)} collective-permute-done((f32[15,32,128]{2,1,0:T(8,128)S(1)}, f32[15,32,128]{2,1,0:T(8,128)S(1)}, u32[]{:S(2)}, u32[]{:S(2)}) %collective-permute-start.13) | collective-permute-done | bytes 245792 | tf_op jit(solution)/shard_map/ppermute | solution.py:284
  203.4 2.4 along_x.7
  205.9 3.9 %collective-permute-start.14 = (f32[15,32,128]{2,1,0:T(8,128)S(1)}, f32[15,32,128]{2,1,0:T(8,128)S(1)}, u32[]{:S(2)}, u32[]{:S(2)}) collective-permute-start(f32[15,32,128]{2,1,0:T(8,128)S(1)} %get-tuple-element.56), channel_id=1, source_target_pairs={{0,128},{1,129},{2,130},{3,131},{4,132},{5,133},{6,134},{7,135},{8... | collective-permute-start | bytes 737288 | tf_op jit(solution)/shard_map/ppermute | solution.py:283
  209.7 1.3 collective-permute-start.15
  211.0 1.8 collective-permute-done.14.low_ref
  212.8 4.1 %collective-permute-done.15.high_ref = f32[15,32,128]{2,1,0:T(8,128)S(1)} collective-permute-done((f32[15,32,128]{2,1,0:T(8,128)S(1)}, f32[15,32,128]{2,1,0:T(8,128)S(1)}, u32[]{:S(2)}, u32[]{:S(2)}) %collective-permute-start.15) | collective-permute-done | bytes 245792 | tf_op jit(solution)/shard_map/ppermute | solution.py:284
  216.9 2.5 last_update.1
  219.4 52.5 %all_to_all.20.got_ref = f32[128,8,128]{2,1,0:T(8,128)S(1)} all-to-all(f32[128,8,128]{2,1,0:T(8,128)S(1)} %bitcast.10), channel_id=1, replica_groups=mesh['slab'=128,'rep'=4] {'slab'}, dimensions={0} | all-to-all | bytes 1048576 | tf_op jit(solution)/shard_map/all_to_all | solution.py:309
  271.9 1.3 plane_of.1
  (9 shorter events, 0.0 us)
Async XLA Ops:
  0.0 1.1 copy-start
  1.1 0.7 copy-start.2
  1.8 0.7 copy-start.3
  2.5 0.7 copy-start.4
  8.1 5.0 %copy-start.5 = (f32[63]{0:T(128)S(1)}, f32[63]{0:T(128)}, u32[]{:S(2)}) copy-start(f32[63]{0:T(128)} %param.13) | copy-start | bytes 760
  8.1 6.3 %copy-start.1 = (f32[1,1024,128]{2,1,0:T(8,128)S(1)}, f32[1,1024,128]{2,1,0:T(8,128)}, u32[]{:S(2)}) copy-start(f32[1,1024,128]{2,1,0:T(8,128)} %param.11) | copy-start | bytes 1572868
  8.1 14.8 %all-to-all-start = ((f32[4,520,128]{2,1,0:T(8,128)}), f32[4,520,128]{2,1,0:T(8,128)S(1)}, u32[]{:S(2)}, u32[]{:S(2)}) async-start(f32[4,520,128]{2,1,0:T(8,128)} %pack_rows.1), calls=%async_computation | async-start | bytes 2129920 | tf_op jit(solution)/shard_map/all_to_all | solution.py:323
  22.9 58.7 %all-to-all-start.2 = ((f32[128,8,128]{2,1,0:T(8,128)}), f32[128,8,128]{2,1,0:T(8,128)S(1)}, u32[]{:S(2)}, u32[]{:S(2)}) async-start(f32[128,8,128]{2,1,0:T(8,128)} %get-tuple-element.32), calls=%async_computation.2 | async-start | bytes 1048576 | tf_op jit(solution)/shard_map/all_to_all | solution.py:309
  52.6 41.8 %copy-start.6 = (f32[31]{0:T(128)S(1)}, f32[31]{0:T(128)}, u32[]{:S(2)}) copy-start(f32[31]{0:T(128)} %param.12) | copy-start | bytes 376
  81.6 49.7 %all-to-all-start.1 = ((f32[128,8,128]{2,1,0:T(8,128)}), f32[128,8,128]{2,1,0:T(8,128)S(1)}, u32[]{:S(2)}, u32[]{:S(2)}) async-start(f32[128,8,128]{2,1,0:T(8,128)} %observe.1), calls=%async_computation.1 | async-start | bytes 1048576 | tf_op jit(solution)/shard_map/all_to_all | solution.py:309
  88.9 24.3 %collective-permute-start = (f32[15,32,128]{2,1,0:T(8,128)S(1)}, f32[15,32,128]{2,1,0:T(8,128)S(1)}, u32[]{:S(2)}, u32[]{:S(2)}) collective-permute-start(f32[15,32,128]{2,1,0:T(8,128)S(1)} %get-tuple-element.33), channel_id=1, source_target_pairs={{0,4},{4,8},{8,12},{12,16},{16,20},{20,24},{24,28},{28,32},{32,36}... | collective-permute-start | bytes 737288 | tf_op jit(solution)/shard_map/ppermute | solution.py:283
  92.5 23.3 %collective-permute-start.1 = (f32[15,32,128]{2,1,0:T(8,128)S(1)}, f32[15,32,128]{2,1,0:T(8,128)S(1)}, u32[]{:S(2)}, u32[]{:S(2)}) collective-permute-start(f32[15,32,128]{2,1,0:T(8,128)S(1)} %get-tuple-element.35), channel_id=1, source_target_pairs={{4,0},{8,4},{12,8},{16,12},{20,16},{24,20},{28,24},{32,28},{36,32}... | collective-permute-start | bytes 737288 | tf_op jit(solution)/shard_map/ppermute | solution.py:284
  118.2 6.3 %collective-permute-start.2 = (f32[15,32,128]{2,1,0:T(8,128)S(1)}, f32[15,32,128]{2,1,0:T(8,128)S(1)}, u32[]{:S(2)}, u32[]{:S(2)}) collective-permute-start(f32[15,32,128]{2,1,0:T(8,128)S(1)} %get-tuple-element.36), channel_id=1, source_target_pairs={{0,128},{1,129},{2,130},{3,131},{4,132},{5,133},{6,134},{7,135},{8... | collective-permute-start | bytes 737288 | tf_op jit(solution)/shard_map/ppermute | solution.py:283
  121.4 6.9 %collective-permute-start.3 = (f32[15,32,128]{2,1,0:T(8,128)S(1)}, f32[15,32,128]{2,1,0:T(8,128)S(1)}, u32[]{:S(2)}, u32[]{:S(2)}) collective-permute-start(f32[15,32,128]{2,1,0:T(8,128)S(1)} %get-tuple-element.38), channel_id=1, source_target_pairs={{128,0},{129,1},{130,2},{131,3},{132,4},{133,5},{134,6},{135,7},{1... | collective-permute-start | bytes 737288 | tf_op jit(solution)/shard_map/ppermute | solution.py:284
  132.0 9.1 %collective-permute-start.4 = (f32[15,32,128]{2,1,0:T(8,128)S(1)}, f32[15,32,128]{2,1,0:T(8,128)S(1)}, u32[]{:S(2)}, u32[]{:S(2)}) collective-permute-start(f32[15,32,128]{2,1,0:T(8,128)S(1)} %get-tuple-element.40), channel_id=1, source_target_pairs={{0,4},{4,8},{8,12},{12,16},{16,20},{20,24},{24,28},{28,32},{32,36}... | collective-permute-start | bytes 737288 | tf_op jit(solution)/shard_map/ppermute | solution.py:283
  138.0 7.5 %collective-permute-start.5 = (f32[15,32,128]{2,1,0:T(8,128)S(1)}, f32[15,32,128]{2,1,0:T(8,128)S(1)}, u32[]{:S(2)}, u32[]{:S(2)}) collective-permute-start(f32[15,32,128]{2,1,0:T(8,128)S(1)} %get-tuple-element.42), channel_id=1, source_target_pairs={{4,0},{8,4},{12,8},{16,12},{20,16},{24,20},{28,24},{32,28},{36,32}... | collective-permute-start | bytes 737288 | tf_op jit(solution)/shard_map/ppermute | solution.py:284
  147.9 6.4 %collective-permute-start.6 = (f32[15,32,128]{2,1,0:T(8,128)S(1)}, f32[15,32,128]{2,1,0:T(8,128)S(1)}, u32[]{:S(2)}, u32[]{:S(2)}) collective-permute-start(f32[15,32,128]{2,1,0:T(8,128)S(1)} %get-tuple-element.43), channel_id=1, source_target_pairs={{0,128},{1,129},{2,130},{3,131},{4,132},{5,133},{6,134},{7,135},{8... | collective-permute-start | bytes 737288 | tf_op jit(solution)/shard_map/ppermute | solution.py:283
  151.3 6.9 %collective-permute-start.7 = (f32[15,32,128]{2,1,0:T(8,128)S(1)}, f32[15,32,128]{2,1,0:T(8,128)S(1)}, u32[]{:S(2)}, u32[]{:S(2)}) collective-permute-start(f32[15,32,128]{2,1,0:T(8,128)S(1)} %get-tuple-element.45), channel_id=1, source_target_pairs={{128,0},{129,1},{130,2},{131,3},{132,4},{133,5},{134,6},{135,7},{1... | collective-permute-start | bytes 737288 | tf_op jit(solution)/shard_map/ppermute | solution.py:284
  160.6 8.7 %collective-permute-start.8 = (f32[15,32,128]{2,1,0:T(8,128)S(1)}, f32[15,32,128]{2,1,0:T(8,128)S(1)}, u32[]{:S(2)}, u32[]{:S(2)}) collective-permute-start(f32[15,32,128]{2,1,0:T(8,128)S(1)} %get-tuple-element.46), channel_id=1, source_target_pairs={{0,4},{4,8},{8,12},{12,16},{16,20},{20,24},{24,28},{28,32},{32,36}... | collective-permute-start | bytes 737288 | tf_op jit(solution)/shard_map/ppermute | solution.py:283
  166.2 7.5 %collective-permute-start.9 = (f32[15,32,128]{2,1,0:T(8,128)S(1)}, f32[15,32,128]{2,1,0:T(8,128)S(1)}, u32[]{:S(2)}, u32[]{:S(2)}) collective-permute-start(f32[15,32,128]{2,1,0:T(8,128)S(1)} %get-tuple-element.48), channel_id=1, source_target_pairs={{4,0},{8,4},{12,8},{16,12},{20,16},{24,20},{28,24},{32,28},{36,32}... | collective-permute-start | bytes 737288 | tf_op jit(solution)/shard_map/ppermute | solution.py:284
  176.2 6.1 %collective-permute-start.10 = (f32[15,32,128]{2,1,0:T(8,128)S(1)}, f32[15,32,128]{2,1,0:T(8,128)S(1)}, u32[]{:S(2)}, u32[]{:S(2)}) collective-permute-start(f32[15,32,128]{2,1,0:T(8,128)S(1)} %get-tuple-element.49), channel_id=1, source_target_pairs={{0,128},{1,129},{2,130},{3,131},{4,132},{5,133},{6,134},{7,135},{8... | collective-permute-start | bytes 737288 | tf_op jit(solution)/shard_map/ppermute | solution.py:283
  179.1 7.4 %collective-permute-start.11 = (f32[15,32,128]{2,1,0:T(8,128)S(1)}, f32[15,32,128]{2,1,0:T(8,128)S(1)}, u32[]{:S(2)}, u32[]{:S(2)}) collective-permute-start(f32[15,32,128]{2,1,0:T(8,128)S(1)} %get-tuple-element.51), channel_id=1, source_target_pairs={{128,0},{129,1},{130,2},{131,3},{132,4},{133,5},{134,6},{135,7},{1... | collective-permute-start | bytes 737288 | tf_op jit(solution)/shard_map/ppermute | solution.py:284
  190.7 8.3 %collective-permute-start.12 = (f32[15,32,128]{2,1,0:T(8,128)S(1)}, f32[15,32,128]{2,1,0:T(8,128)S(1)}, u32[]{:S(2)}, u32[]{:S(2)}) collective-permute-start(f32[15,32,128]{2,1,0:T(8,128)S(1)} %get-tuple-element.53), channel_id=1, source_target_pairs={{0,4},{4,8},{8,12},{12,16},{16,20},{20,24},{24,28},{28,32},{32,36}... | collective-permute-start | bytes 737288 | tf_op jit(solution)/shard_map/ppermute | solution.py:283
  195.9 7.5 %collective-permute-start.13 = (f32[15,32,128]{2,1,0:T(8,128)S(1)}, f32[15,32,128]{2,1,0:T(8,128)S(1)}, u32[]{:S(2)}, u32[]{:S(2)}) collective-permute-start(f32[15,32,128]{2,1,0:T(8,128)S(1)} %get-tuple-element.55), channel_id=1, source_target_pairs={{4,0},{8,4},{12,8},{16,12},{20,16},{24,20},{28,24},{32,28},{36,32}... | collective-permute-start | bytes 737288 | tf_op jit(solution)/shard_map/ppermute | solution.py:284
  205.9 7.0 %collective-permute-start.14 = (f32[15,32,128]{2,1,0:T(8,128)S(1)}, f32[15,32,128]{2,1,0:T(8,128)S(1)}, u32[]{:S(2)}, u32[]{:S(2)}) collective-permute-start(f32[15,32,128]{2,1,0:T(8,128)S(1)} %get-tuple-element.56), channel_id=1, source_target_pairs={{0,128},{1,129},{2,130},{3,131},{4,132},{5,133},{6,134},{7,135},{8... | collective-permute-start | bytes 737288 | tf_op jit(solution)/shard_map/ppermute | solution.py:283
  209.7 7.2 %collective-permute-start.15 = (f32[15,32,128]{2,1,0:T(8,128)S(1)}, f32[15,32,128]{2,1,0:T(8,128)S(1)}, u32[]{:S(2)}, u32[]{:S(2)}) collective-permute-start(f32[15,32,128]{2,1,0:T(8,128)S(1)} %get-tuple-element.58), channel_id=1, source_target_pairs={{128,0},{129,1},{130,2},{131,3},{132,4},{133,5},{134,6},{135,7},{1... | collective-permute-start | bytes 737288 | tf_op jit(solution)/shard_map/ppermute | solution.py:284
where the time goes:
time: 274 us; the launch traced here: 273 us
  waiting for transfers between devices  96.2 us (35%)
  starting transfers between devices  84.2 us (31%)
  blocking collectives  52.5 us (19%)
  Pallas kernels  34.3 us (13%)
  local copies, waits for them, and re-layouts  3.29 us (1%)
    all_to_all x1, blocking collectives, turn(): lax.all_to_all(pieces, 'slab', split_axis=0, concat_axis=0, tiled=True)  52.5 us
    pallas_call x14, Pallas kernels, call(): pl.pallas_call(kernel, out_shape=outs, in_specs=specs, out_specs=tuple((p...  34.3 us
    ppermute x8, starting transfers between devices, exchange(): low = lax.ppermute(last, axes, pairs)  33.6 us
    all_to_all x2, starting transfers between devices, turn(): lax.all_to_all(pieces, 'slab', split_axis=0, concat_axis=0, tiled=True)  32.6 us
    ppermute x8, waiting for transfers between devices, exchange(): high = lax.ppermute(first, axes, [(b, a) for a, b in pairs])  31.8 us
    all_to_all x2, waiting for transfers between devices, turn(): lax.all_to_all(pieces, 'slab', split_axis=0, concat_axis=0, tiled=True)  29 us
    ppermute x8, waiting for transfers between devices, exchange(): low = lax.ppermute(last, axes, pairs)  28.2 us
    ppermute x8, starting transfers between devices, exchange(): high = lax.ppermute(first, axes, [(b, a) for a, b in pairs])  13 us
  transfers between devices with their start and end apart: 19, of which 18 were waited for; matrix products, arithmetic and copies ran while one was open for 1% of the time, Pallas kernels for 4%

commit v1 on v0

--- a/solution.py
+++ b/solution.py
@@ -77,7 +77,8 @@
     band_ref[...] = jnp.where(jnp.abs(j - z) <= 31, rolled, 0.0)
 
 
-def pack_rows(rows_ref, blend_ref, route_ref, line_ref, out_ref, split_ref, hot_ref):
+def pack_rows(rep_ref, rows_ref, blend_ref, route_ref, line_ref, *refs):
+    out_refs, (split_ref, hot_ref) = refs[:OWNERS], refs[OWNERS:]
     chunks = rows_ref.shape[0] // LANES
     blend = blend_ref[...]
     route = route_ref[...]
@@ -117,38 +118,40 @@
         ],
         axis=1,
     ).astype(BF16)
-    for owner in range(OWNERS):
+    for step, out_ref in enumerate(out_refs):
+        owner = (rep_ref[0] + step) % OWNERS
         slot = lax.broadcasted_iota(jnp.int32, (CAPACITY, LANES), 0) + owner * CAPACITY
         for c in range(chunks):
             hot = jnp.where(slot == key[c : c + 1, :], 1.0, 0.0)
             hot_ref[:, c * LANES : (c + 1) * LANES] = hot.astype(BF16)
         hot = hot_ref[...]
         both = jnp.dot(hot, split_ref[...], preferred_element_type=F32)
-        out_ref[owner, :CAPACITY, :] = both[:, :LANES] + both[:, LANES:]
+        out_ref[:CAPACITY, :] = both[:, :LANES] + both[:, LANES:]
         meta = lax.dot_general(
             notes, hot, (((1,), (1,)), ((), ())), preferred_element_type=F32
         )
         weight = meta[0:1] + meta[1:2] + meta[2:3]
         where = meta[3:4] * 32.0 + meta[4:5]
-        out_ref[owner, CAPACITY:, :] = jnp.concatenate(
+        out_ref[CAPACITY:, :] = jnp.concatenate(
             [weight[:, q * LANES : (q + 1) * LANES] for q in range(4)]
             + [where[:, q * LANES : (q + 1) * LANES] for q in range(4)],
             axis=0,
         )
 
 
-def observe(got_ref, out_ref, hot_ref):
+def observe(*refs):
+    got_refs, (out_ref, hot_ref) = refs[:OWNERS], refs[OWNERS:]
     total = jnp.zeros((LINES, 2 * LANES), F32)
     weights = jnp.zeros((LINES, 8), F32)
     at = lax.broadcasted_iota(jnp.int32, (LINES, LANES), 0)
-    for source in range(OWNERS):
-        meta = got_ref[source, CAPACITY:, :]
+    for got_ref in got_refs:
+        meta = got_ref[CAPACITY:, :]
         where = meta[4:8].astype(jnp.int32)
         for q in range(4):
             hot = jnp.where(at == where[q : q + 1, :], 1.0, 0.0)
             hot_ref[:, q * LANES : (q + 1) * LANES] = hot.astype(BF16)
         hot = hot_ref[...]
-        high, low = halves(got_ref[source, :CAPACITY, :])
+        high, low = halves(got_ref[:CAPACITY, :])
         total += jnp.dot(hot, jnp.concatenate([high, low], axis=1), preferred_element_type=F32)
         weight = jnp.concatenate([meta[q : q + 1] for q in range(4)], axis=1)
         parts = [p.astype(F32) for p in thirds(weight)]
@@ -311,21 +314,26 @@
     taps = psf_xy / jnp.sum(psf_xy)
     taps_z = jnp.pad((psf_z / jnp.sum(psf_z))[::-1], (0, LANES - psf_z.shape[0]))[None, :]
 
+    pieces, band = call(
+        tiles_of_start, [PIECES, (Z, LANES)], [], start.reshape(LINES, LANES), taps_z
+    )
+    arrived = turn(pieces)
     sent = call(
         pack_rows,
-        [(OWNERS, CAPACITY + META, LANES)],
+        [(CAPACITY + META, LANES)] * OWNERS,
         [((chunks * LANES, 2 * LANES), BF16), ((CAPACITY, chunks * LANES), BF16)],
+        lax.axis_index("rep").reshape(1),
         camera_rows,
         blend.reshape(chunks, LANES),
         route.reshape(chunks, LANES),
         line.reshape(chunks, LANES),
-    )[0]
-    got = lax.all_to_all(sent, "rep", split_axis=0, concat_axis=0, tiled=True)
-    pieces, band = call(
-        tiles_of_start, [PIECES, (Z, LANES)], [], start.reshape(LINES, LANES), taps_z
-    )
-    arrived = turn(pieces)
-    seen_pieces = call(observe, [PIECES], [((LINES, CAPACITY), BF16)], got)[0]
+        smem=1,
+    )
+    got = [
+        block if step == 0 else lax.ppermute(block, "rep", [(r, (r + step) % reps) for r in range(reps)])
+        for step, block in enumerate(sent)
+    ]
+    seen_pieces = call(observe, [PIECES], [((LINES, CAPACITY), BF16)], *got)[0]
     seen_arrived = turn(seen_pieces)
 
     estimate, first, last = call(

time: 274 us -> 257 us (0.938)
  waiting for transfers between devices: 96.2 us -> 73.6 us
  starting transfers between devices: 84.2 us -> 91 us
    all_to_all x2, waiting for transfers between devices: 29 us -> 6.44 us  [turn(): lax.all_to_all(pieces, 'slab', split_axis=0, concat_axis=0, tiled=True)]
    ppermute x0 -> x3, starting transfers between devices: none -> 10.5 us  [shards(): lax.ppermute(block, 'rep', [(r, (r + step) % reps) for r in range(reps)])]
    ppermute x0 -> x3, waiting for transfers between devices: none -> 7.44 us  [shards(): lax.ppermute(block, 'rep', [(r, (r + step) % reps) for r in range(reps)])]
    all_to_all x1 -> x0, waiting for transfers between devices: 7.18 us -> none  [shards(): got = lax.all_to_all(sent, 'rep', split_axis=0, concat_axis=0, tiled=True)]
    all_to_all x1 -> x0, starting transfers between devices: 4.97 us -> none  [shards(): got = lax.all_to_all(sent, 'rep', split_axis=0, concat_axis=0, tiled=True)]
  transfers between devices with their start and end apart: 19 -> 21, of which waited for: 18 -> 19; matrix products, arithmetic and copies ran while one was open for 1% -> 0% of each run, Pallas kernels for 4% -> 5%
where the time goes in v1:
time: 257 us; the launch traced here: 256 us
  starting transfers between devices  91 us (35%)
  waiting for transfers between devices  73.6 us (29%)
  blocking collectives  52.5 us (20%)
  Pallas kernels  33.2 us (13%)
    all_to_all x1, blocking collectives, turn(): lax.all_to_all(pieces, 'slab', split_axis=0, concat_axis=0, tiled=True)  52.5 us
    ppermute x8, starting transfers between devices, exchange(): low = lax.ppermute(last, axes, pairs)  35.2 us
    pallas_call x14, Pallas kernels, call(): pl.pallas_call(kernel, out_shape=outs, in_specs=specs, out_specs=tuple((p...  33.2 us
    all_to_all x2, starting transfers between devices, turn(): lax.all_to_all(pieces, 'slab', split_axis=0, concat_axis=0, tiled=True)  32.2 us
    ppermute x8, waiting for transfers between devices, exchange(): high = lax.ppermute(first, axes, [(b, a) for a, b in pairs])  31.6 us
    ppermute x8, waiting for transfers between devices, exchange(): low = lax.ppermute(last, axes, pairs)  28.1 us
    ppermute x8, starting transfers between devices, exchange(): high = lax.ppermute(first, axes, [(b, a) for a, b in pairs])  13 us
    ppermute x3, starting transfers between devices, shards(): lax.ppermute(block, 'rep', [(r, (r + step) % reps) for r in range(reps)])  10.5 us
  transfers between devices with their start and end apart: 21, of which 19 were waited for; matrix products, arithmetic and copies ran while one was open for 0% of the time, Pallas kernels for 5%

profile of v1, /device:TPU:1, one launch (start us, length us, event | category | flops | bytes accessed | tf_op | source)
XLA Modules:
  0.0 255.7 jit_solution(15086116886652133434)
XLA Ops:
  0.0 0.8 reverse.3
  0.8 0.6 reduce_sum.19
  1.4 0.6 broadcast_divide_fusion
  2.1 0.0 copy-start.1
  2.1 1.0 copy-done.1
  3.1 1.3 tiles_of_start.1
  4.4 20.7 %all-to-all-start.1 = ((f32[128,8,128]{2,1,0:T(8,128)}), f32[128,8,128]{2,1,0:T(8,128)S(1)}, u32[]{:S(2)}, u32[]{:S(2)}) async-start(f32[128,8,128]{2,1,0:T(8,128)} %get-tuple-element.40), calls=%async_computation.1 | async-start | bytes 1048576 | tf_op jit(solution)/shard_map/all_to_all | solution.py:312
  25.2 0.7 copy-done.2
  25.8 3.8 %pack_rows.1 = (f32[520,128]{1,0:T(8,128)S(1)}, f32[520,128]{1,0:T(8,128)S(1)}, f32[520,128]{1,0:T(8,128)S(1)}, f32[520,128]{1,0:T(8,128)S(1)}) custom-call(s32[1]{0:T(128)} %bitcast.rep_ref, f32[1280,128]{1,0:T(8,128)S(1)} %copy-done, f32[10,128]{1,0:T(8,128)S(1)} %bitcast.15, s32[10,128]{1,0:T(8,128)S(1)} %bitcast.16, s32[10,128]{1,0:T(8,128)S(1)} %bitcast.17), custom_call_target="tpu_custom_call" | custom-call | tf_op jit(solution)/shard_map/pack_rows/pallas_call | solution.py:30
  29.6 3.1 %collective-permute-start = (f32[520,128]{1,0:T(8,128)S(1)}, f32[520,128]{1,0:T(8,128)S(1)}, u32[]{:S(2)}, u32[]{:S(2)}) collective-permute-start(f32[520,128]{1,0:T(8,128)S(1)} %get-tuple-element.37), channel_id=1, source_target_pairs={{0,1},{1,2},{2,3},{3,0},{4,5},{5,6},{6,7},{7,4},{8,9},{9,10},{10,1... | collective-permute-start | bytes 798728 | tf_op jit(solution)/shard_map/ppermute | solution.py:333
  32.7 4.4 %collective-permute-start.1 = (f32[520,128]{1,0:T(8,128)S(1)}, f32[520,128]{1,0:T(8,128)S(1)}, u32[]{:S(2)}, u32[]{:S(2)}) collective-permute-start(f32[520,128]{1,0:T(8,128)S(1)} %get-tuple-element.38), channel_id=1, source_target_pairs={{0,2},{1,3},{2,0},{3,1},{4,6},{5,7},{6,4},{7,5},{8,10},{9,11},{10,... | collective-permute-start | bytes 798728 | tf_op jit(solution)/shard_map/ppermute | solution.py:333
  37.1 3.1 %collective-permute-start.2 = (f32[520,128]{1,0:T(8,128)S(1)}, f32[520,128]{1,0:T(8,128)S(1)}, u32[]{:S(2)}, u32[]{:S(2)}) collective-permute-start(f32[520,128]{1,0:T(8,128)S(1)} %get-tuple-element.39), channel_id=1, source_target_pairs={{0,3},{1,0},{2,1},{3,2},{4,7},{5,4},{6,5},{7,6},{8,11},{9,8},{10,9... | collective-permute-start | bytes 798728 | tf_op jit(solution)/shard_map/ppermute | solution.py:333
  40.2 6.2 %collective-permute-done.1.refs_2_ = f32[520,128]{1,0:T(8,128)S(1)} collective-permute-done((f32[520,128]{1,0:T(8,128)S(1)}, f32[520,128]{1,0:T(8,128)S(1)}, u32[]{:S(2)}, u32[]{:S(2)}) %collective-permute-start.1) | collective-permute-done | bytes 266272 | tf_op jit(solution)/shard_map/ppermute | solution.py:333
  46.4 1.2 collective-permute-done.2.refs_3_
  47.6 4.3 %observe.1 = f32[128,8,128]{2,1,0:T(8,128)} custom-call(f32[520,128]{1,0:T(8,128)S(1)} %get-tuple-element.36.refs_0_, f32[520,128]{1,0:T(8,128)S(1)} %collective-permute-done.refs_1_, f32[520,128]{1,0:T(8,128)S(1)} %collective-permute-done.1.refs_2_, f32[520,128]{1,0:T(8,128)S(1)} %collective-permute-done.2.refs_3_), custom_call_target="tpu_custom_call" | custom-call | tf_op jit(solution)/shard_map/observe/pallas_call | solution.py:30
  51.9 6.4 %all-to-all-done.1 = f32[128,8,128]{2,1,0:T(8,128)S(1)} async-done(((f32[128,8,128]{2,1,0:T(8,128)}), f32[128,8,128]{2,1,0:T(8,128)S(1)}, u32[]{:S(2)}, u32[]{:S(2)}) %all-to-all-start.1) | async-done | bytes 524320 | tf_op jit(solution)/shard_map/all_to_all | solution.py:312
  58.3 11.5 %all-to-all-start = ((f32[128,8,128]{2,1,0:T(8,128)}), f32[128,8,128]{2,1,0:T(8,128)S(1)}, u32[]{:S(2)}, u32[]{:S(2)}) async-start(f32[128,8,128]{2,1,0:T(8,128)} %observe.1), calls=%async_computation | async-start | bytes 1048576 | tf_op jit(solution)/shard_map/all_to_all | solution.py:312
  69.8 0.2 arrive.1
  70.0 0.0 copy-start.6
  70.0 3.5 %collective-permute-start.3 = (f32[15,32,128]{2,1,0:T(8,128)S(1)}, f32[15,32,128]{2,1,0:T(8,128)S(1)}, u32[]{:S(2)}, u32[]{:S(2)}) collective-permute-start(f32[15,32,128]{2,1,0:T(8,128)S(1)} %get-tuple-element.41), channel_id=1, source_target_pairs={{0,4},{4,8},{8,12},{12,16},{16,20},{20,24},{24,28},{28,32},{32,36}... | collective-permute-start | bytes 737288 | tf_op jit(solution)/shard_map/ppermute | solution.py:286
  73.6 1.9 collective-permute-start.4
  75.5 0.6 reduce_sum.18
  76.1 0.6 broadcast_divide_fusion.1.taps_ref
  76.8 17.5 %collective-permute-done.3.low_ref = f32[15,32,128]{2,1,0:T(8,128)S(1)} collective-permute-done((f32[15,32,128]{2,1,0:T(8,128)S(1)}, f32[15,32,128]{2,1,0:T(8,128)S(1)}, u32[]{:S(2)}, u32[]{:S(2)}) %collective-permute-start.3) | collective-permute-done | bytes 245792 | tf_op jit(solution)/shard_map/ppermute | solution.py:286
  94.3 2.6 %collective-permute-done.4.high_ref = f32[15,32,128]{2,1,0:T(8,128)S(1)} collective-permute-done((f32[15,32,128]{2,1,0:T(8,128)S(1)}, f32[15,32,128]{2,1,0:T(8,128)S(1)}, u32[]{:S(2)}, u32[]{:S(2)}) %collective-permute-start.4) | collective-permute-done | bytes 245792 | tf_op jit(solution)/shard_map/ppermute | solution.py:287
  96.9 2.4 along_x.4
  99.3 3.2 %collective-permute-start.5 = (f32[15,32,128]{2,1,0:T(8,128)S(1)}, f32[15,32,128]{2,1,0:T(8,128)S(1)}, u32[]{:S(2)}, u32[]{:S(2)}) collective-permute-start(f32[15,32,128]{2,1,0:T(8,128)S(1)} %get-tuple-element.44), channel_id=1, source_target_pairs={{0,128},{1,129},{2,130},{3,131},{4,132},{5,133},{6,134},{7,135},{8... | collective-permute-start | bytes 737288 | tf_op jit(solution)/shard_map/ppermute | solution.py:286
  102.5 1.5 collective-permute-start.6
  104.0 1.6 collective-permute-done.5.low_ref
  105.6 3.8 %collective-permute-done.6.high_ref = f32[15,32,128]{2,1,0:T(8,128)S(1)} collective-permute-done((f32[15,32,128]{2,1,0:T(8,128)S(1)}, f32[15,32,128]{2,1,0:T(8,128)S(1)}, u32[]{:S(2)}, u32[]{:S(2)}) %collective-permute-start.6) | collective-permute-done | bytes 245792 | tf_op jit(solution)/shard_map/ppermute | solution.py:287
  109.5 2.9 %blur.1.blurred_ref = f32[1024,128]{1,0:T(8,128)S(1)} custom-call(f32[31]{0:T(128)S(1)} %broadcast_divide_fusion.1.taps_ref, f32[15,32,128]{2,1,0:T(8,128)S(1)} %collective-permute-done.5.low_ref, f32[32,32,128]{2,1,0:T(8,128)S(1)} %get-tuple-element.45.mid_ref, f32[15,32,128]{2,1,0:T(8,128)S(1)} %collective-permute-done.6.high_ref, ...), custom_call_target="tpu_custom_call" | custom-call | tf_op jit(solution)/shard_map/blur/pallas_call | solution.py:30
  112.4 0.7 first_ratio.1
  113.1 6.0 %collective-permute-start.7 = (f32[15,32,128]{2,1,0:T(8,128)S(1)}, f32[15,32,128]{2,1,0:T(8,128)S(1)}, u32[]{:S(2)}, u32[]{:S(2)}) collective-permute-start(f32[15,32,128]{2,1,0:T(8,128)S(1)} %get-tuple-element.48), channel_id=1, source_target_pairs={{0,4},{4,8},{8,12},{12,16},{16,20},{20,24},{24,28},{28,32},{32,36}... | collective-permute-start | bytes 737288 | tf_op jit(solution)/shard_map/ppermute | solution.py:286
  119.1 1.9 collective-permute-start.8
  121.0 1.2 collective-permute-done.7.low_ref
  122.2 4.4 %collective-permute-done.8.high_ref = f32[15,32,128]{2,1,0:T(8,128)S(1)} collective-permute-done((f32[15,32,128]{2,1,0:T(8,128)S(1)}, f32[15,32,128]{2,1,0:T(8,128)S(1)}, u32[]{:S(2)}, u32[]{:S(2)}) %collective-permute-start.8) | collective-permute-done | bytes 245792 | tf_op jit(solution)/shard_map/ppermute | solution.py:287
  126.6 2.4 along_x.5
  129.0 3.3 %collective-permute-start.9 = (f32[15,32,128]{2,1,0:T(8,128)S(1)}, f32[15,32,128]{2,1,0:T(8,128)S(1)}, u32[]{:S(2)}, u32[]{:S(2)}) collective-permute-start(f32[15,32,128]{2,1,0:T(8,128)S(1)} %get-tuple-element.51), channel_id=1, source_target_pairs={{0,128},{1,129},{2,130},{3,131},{4,132},{5,133},{6,134},{7,135},{8... | collective-permute-start | bytes 737288 | tf_op jit(solution)/shard_map/ppermute | solution.py:286
  132.4 1.3 collective-permute-start.10
  133.7 1.8 collective-permute-done.9.low_ref
  135.5 3.8 %collective-permute-done.10.high_ref = f32[15,32,128]{2,1,0:T(8,128)S(1)} collective-permute-done((f32[15,32,128]{2,1,0:T(8,128)S(1)}, f32[15,32,128]{2,1,0:T(8,128)S(1)}, u32[]{:S(2)}, u32[]{:S(2)}) %collective-permute-start.10) | collective-permute-done | bytes 245792 | tf_op jit(solution)/shard_map/ppermute | solution.py:287
  139.3 2.4 update.1
  141.7 5.6 %collective-permute-start.11 = (f32[15,32,128]{2,1,0:T(8,128)S(1)}, f32[15,32,128]{2,1,0:T(8,128)S(1)}, u32[]{:S(2)}, u32[]{:S(2)}) collective-permute-start(f32[15,32,128]{2,1,0:T(8,128)S(1)} %get-tuple-element.54), channel_id=1, source_target_pairs={{0,4},{4,8},{8,12},{12,16},{16,20},{20,24},{24,28},{28,32},{32,36}... | collective-permute-start | bytes 737288 | tf_op jit(solution)/shard_map/ppermute | solution.py:286
  147.3 1.9 collective-permute-start.12
  149.2 1.2 collective-permute-done.11.low_ref
  150.4 4.4 %collective-permute-done.12.high_ref = f32[15,32,128]{2,1,0:T(8,128)S(1)} collective-permute-done((f32[15,32,128]{2,1,0:T(8,128)S(1)}, f32[15,32,128]{2,1,0:T(8,128)S(1)}, u32[]{:S(2)}, u32[]{:S(2)}) %collective-permute-start.12) | collective-permute-done | bytes 245792 | tf_op jit(solution)/shard_map/ppermute | solution.py:287
  154.8 2.4 along_x.6
  157.3 4.7 %collective-permute-start.13 = (f32[15,32,128]{2,1,0:T(8,128)S(1)}, f32[15,32,128]{2,1,0:T(8,128)S(1)}, u32[]{:S(2)}, u32[]{:S(2)}) collective-permute-start(f32[15,32,128]{2,1,0:T(8,128)S(1)} %get-tuple-element.57), channel_id=1, source_target_pairs={{0,128},{1,129},{2,130},{3,131},{4,132},{5,133},{6,134},{7,135},{8... | collective-permute-start | bytes 737288 | tf_op jit(solution)/shard_map/ppermute | solution.py:286
  162.0 1.3 collective-permute-start.14
  163.3 1.8 collective-permute-done.13.low_ref
  165.1 4.3 %collective-permute-done.14.high_ref = f32[15,32,128]{2,1,0:T(8,128)S(1)} collective-permute-done((f32[15,32,128]{2,1,0:T(8,128)S(1)}, f32[15,32,128]{2,1,0:T(8,128)S(1)}, u32[]{:S(2)}, u32[]{:S(2)}) %collective-permute-start.14) | collective-permute-done | bytes 245792 | tf_op jit(solution)/shard_map/ppermute | solution.py:287
  169.4 4.1 %blur_ratio.1 = (f32[32,32,128]{2,1,0:T(8,128)S(1)}, f32[15,32,128]{2,1,0:T(8,128)S(1)}, f32[15,32,128]{2,1,0:T(8,128)S(1)}) custom-call(f32[31]{0:T(128)S(1)} %broadcast_divide_fusion.1.taps_ref, f32[15,32,128]{2,1,0:T(8,128)S(1)} %collective-permute-done.13.low_ref, f32[32,32,128]{2,1,0:T(8,128)S(1)} %get-tuple-element.58.mid_ref, ...), custom_call_target="tpu_custom_call" | custom-call | tf_op jit(solution)/shard_map/blur_ratio/pallas_call | solution.py:30
  173.6 5.4 %collective-permute-start.15 = (f32[15,32,128]{2,1,0:T(8,128)S(1)}, f32[15,32,128]{2,1,0:T(8,128)S(1)}, u32[]{:S(2)}, u32[]{:S(2)}) collective-permute-start(f32[15,32,128]{2,1,0:T(8,128)S(1)} %get-tuple-element.61), channel_id=1, source_target_pairs={{0,4},{4,8},{8,12},{12,16},{16,20},{20,24},{24,28},{28,32},{32,36}... | collective-permute-start | bytes 737288 | tf_op jit(solution)/shard_map/ppermute | solution.py:286
  179.0 1.9 collective-permute-start.16
  180.9 1.2 collective-permute-done.15.low_ref
  182.1 4.4 %collective-permute-done.16.high_ref = f32[15,32,128]{2,1,0:T(8,128)S(1)} collective-permute-done((f32[15,32,128]{2,1,0:T(8,128)S(1)}, f32[15,32,128]{2,1,0:T(8,128)S(1)}, u32[]{:S(2)}, u32[]{:S(2)}) %collective-permute-start.16) | collective-permute-done | bytes 245792 | tf_op jit(solution)/shard_map/ppermute | solution.py:287
  186.5 2.4 along_x.7
  189.0 3.4 %collective-permute-start.17 = (f32[15,32,128]{2,1,0:T(8,128)S(1)}, f32[15,32,128]{2,1,0:T(8,128)S(1)}, u32[]{:S(2)}, u32[]{:S(2)}) collective-permute-start(f32[15,32,128]{2,1,0:T(8,128)S(1)} %get-tuple-element.64), channel_id=1, source_target_pairs={{0,128},{1,129},{2,130},{3,131},{4,132},{5,133},{6,134},{7,135},{8... | collective-permute-start | bytes 737288 | tf_op jit(solution)/shard_map/ppermute | solution.py:286
  192.4 1.3 collective-permute-start.18
  193.7 1.8 collective-permute-done.17.low_ref
  195.5 3.8 %collective-permute-done.18.high_ref = f32[15,32,128]{2,1,0:T(8,128)S(1)} collective-permute-done((f32[15,32,128]{2,1,0:T(8,128)S(1)}, f32[15,32,128]{2,1,0:T(8,128)S(1)}, u32[]{:S(2)}, u32[]{:S(2)}) %collective-permute-start.18) | collective-permute-done | bytes 245792 | tf_op jit(solution)/shard_map/ppermute | solution.py:287
  199.3 2.5 last_update.1
  201.9 52.5 %all_to_all.15.got_ref = f32[128,8,128]{2,1,0:T(8,128)S(1)} all-to-all(f32[128,8,128]{2,1,0:T(8,128)S(1)} %bitcast.11), channel_id=1, replica_groups=mesh['slab'=128,'rep'=4] {'slab'}, dimensions={0} | all-to-all | bytes 1048576 | tf_op jit(solution)/shard_map/all_to_all | solution.py:312
  254.4 1.3 plane_of.1
  (13 shorter events, 0.0 us)
Async XLA Ops:
  0.0 0.8 copy-start.5
  2.1 1.0 copy-start.1
  4.4 20.7 %copy-start = (f32[1280,128]{1,0:T(8,128)S(1)}, f32[1280,128]{1,0:T(8,128)}, u32[]{:S(2)}) copy-start(f32[1280,128]{1,0:T(8,128)} %rows_ref.1) | copy-start | bytes 1966084
  4.4 20.7 %copy-start.3 = (s32[1280]{0:T(1024)S(1)}, s32[1280]{0:T(1024)}, u32[]{:S(2)}) copy-start(s32[1280]{0:T(1024)} %param.9) | copy-start | bytes 15364
  4.4 20.7 %copy-start.4 = (s32[1280]{0:T(1024)S(1)}, s32[1280]{0:T(1024)}, u32[]{:S(2)}) copy-start(s32[1280]{0:T(1024)} %param.10) | copy-start | bytes 15364
  4.4 53.9 %all-to-all-start.1 = ((f32[128,8,128]{2,1,0:T(8,128)}), f32[128,8,128]{2,1,0:T(8,128)S(1)}, u32[]{:S(2)}, u32[]{:S(2)}) async-start(f32[128,8,128]{2,1,0:T(8,128)} %get-tuple-element.40), calls=%async_computation.1 | async-start | bytes 1048576 | tf_op jit(solution)/shard_map/all_to_all | solution.py:312
  25.1 0.7 copy-start.2
  29.6 10.6 %collective-permute-start = (f32[520,128]{1,0:T(8,128)S(1)}, f32[520,128]{1,0:T(8,128)S(1)}, u32[]{:S(2)}, u32[]{:S(2)}) collective-permute-start(f32[520,128]{1,0:T(8,128)S(1)} %get-tuple-element.37), channel_id=1, source_target_pairs={{0,1},{1,2},{2,3},{3,0},{4,5},{5,6},{6,7},{7,4},{8,9},{9,10},{10,1... | collective-permute-start | bytes 798728 | tf_op jit(solution)/shard_map/ppermute | solution.py:333
  32.7 13.7 %collective-permute-start.1 = (f32[520,128]{1,0:T(8,128)S(1)}, f32[520,128]{1,0:T(8,128)S(1)}, u32[]{:S(2)}, u32[]{:S(2)}) collective-permute-start(f32[520,128]{1,0:T(8,128)S(1)} %get-tuple-element.38), channel_id=1, source_target_pairs={{0,2},{1,3},{2,0},{3,1},{4,6},{5,7},{6,4},{7,5},{8,10},{9,11},{10,... | collective-permute-start | bytes 798728 | tf_op jit(solution)/shard_map/ppermute | solution.py:333
  37.1 10.5 %collective-permute-start.2 = (f32[520,128]{1,0:T(8,128)S(1)}, f32[520,128]{1,0:T(8,128)S(1)}, u32[]{:S(2)}, u32[]{:S(2)}) collective-permute-start(f32[520,128]{1,0:T(8,128)S(1)} %get-tuple-element.39), channel_id=1, source_target_pairs={{0,3},{1,0},{2,1},{3,2},{4,7},{5,4},{6,5},{7,6},{8,11},{9,8},{10,9... | collective-permute-start | bytes 798728 | tf_op jit(solution)/shard_map/ppermute | solution.py:333
  58.3 54.1 %all-to-all-start = ((f32[128,8,128]{2,1,0:T(8,128)}), f32[128,8,128]{2,1,0:T(8,128)S(1)}, u32[]{:S(2)}, u32[]{:S(2)}) async-start(f32[128,8,128]{2,1,0:T(8,128)} %observe.1), calls=%async_computation | async-start | bytes 1048576 | tf_op jit(solution)/shard_map/all_to_all | solution.py:312
  70.0 5.5 %copy-start.6 = (f32[31]{0:T(128)S(1)}, f32[31]{0:T(128)}, u32[]{:S(2)}) copy-start(f32[31]{0:T(128)} %param.12) | copy-start | bytes 376
  70.0 24.3 %collective-permute-start.3 = (f32[15,32,128]{2,1,0:T(8,128)S(1)}, f32[15,32,128]{2,1,0:T(8,128)S(1)}, u32[]{:S(2)}, u32[]{:S(2)}) collective-permute-start(f32[15,32,128]{2,1,0:T(8,128)S(1)} %get-tuple-element.41), channel_id=1, source_target_pairs={{0,4},{4,8},{8,12},{12,16},{16,20},{20,24},{24,28},{28,32},{32,36}... | collective-permute-start | bytes 737288 | tf_op jit(solution)/shard_map/ppermute | solution.py:286
  73.6 23.3 %collective-permute-start.4 = (f32[15,32,128]{2,1,0:T(8,128)S(1)}, f32[15,32,128]{2,1,0:T(8,128)S(1)}, u32[]{:S(2)}, u32[]{:S(2)}) collective-permute-start(f32[15,32,128]{2,1,0:T(8,128)S(1)} %get-tuple-element.43), channel_id=1, source_target_pairs={{4,0},{8,4},{12,8},{16,12},{20,16},{24,20},{28,24},{32,28},{36,32}... | collective-permute-start | bytes 737288 | tf_op jit(solution)/shard_map/ppermute | solution.py:287
  99.3 6.3 %collective-permute-start.5 = (f32[15,32,128]{2,1,0:T(8,128)S(1)}, f32[15,32,128]{2,1,0:T(8,128)S(1)}, u32[]{:S(2)}, u32[]{:S(2)}) collective-permute-start(f32[15,32,128]{2,1,0:T(8,128)S(1)} %get-tuple-element.44), channel_id=1, source_target_pairs={{0,128},{1,129},{2,130},{3,131},{4,132},{5,133},{6,134},{7,135},{8... | collective-permute-start | bytes 737288 | tf_op jit(solution)/shard_map/ppermute | solution.py:286
  102.5 6.9 %collective-permute-start.6 = (f32[15,32,128]{2,1,0:T(8,128)S(1)}, f32[15,32,128]{2,1,0:T(8,128)S(1)}, u32[]{:S(2)}, u32[]{:S(2)}) collective-permute-start(f32[15,32,128]{2,1,0:T(8,128)S(1)} %get-tuple-element.46), channel_id=1, source_target_pairs={{128,0},{129,1},{130,2},{131,3},{132,4},{133,5},{134,6},{135,7},{1... | collective-permute-start | bytes 737288 | tf_op jit(solution)/shard_map/ppermute | solution.py:287
  113.1 9.1 %collective-permute-start.7 = (f32[15,32,128]{2,1,0:T(8,128)S(1)}, f32[15,32,128]{2,1,0:T(8,128)S(1)}, u32[]{:S(2)}, u32[]{:S(2)}) collective-permute-start(f32[15,32,128]{2,1,0:T(8,128)S(1)} %get-tuple-element.48), channel_id=1, source_target_pairs={{0,4},{4,8},{8,12},{12,16},{16,20},{20,24},{24,28},{28,32},{32,36}... | collective-permute-start | bytes 737288 | tf_op jit(solution)/shard_map/ppermute | solution.py:286
  119.1 7.5 %collective-permute-start.8 = (f32[15,32,128]{2,1,0:T(8,128)S(1)}, f32[15,32,128]{2,1,0:T(8,128)S(1)}, u32[]{:S(2)}, u32[]{:S(2)}) collective-permute-start(f32[15,32,128]{2,1,0:T(8,128)S(1)} %get-tuple-element.50), channel_id=1, source_target_pairs={{4,0},{8,4},{12,8},{16,12},{20,16},{24,20},{28,24},{32,28},{36,32}... | collective-permute-start | bytes 737288 | tf_op jit(solution)/shard_map/ppermute | solution.py:287
  129.0 6.4 %collective-permute-start.9 = (f32[15,32,128]{2,1,0:T(8,128)S(1)}, f32[15,32,128]{2,1,0:T(8,128)S(1)}, u32[]{:S(2)}, u32[]{:S(2)}) collective-permute-start(f32[15,32,128]{2,1,0:T(8,128)S(1)} %get-tuple-element.51), channel_id=1, source_target_pairs={{0,128},{1,129},{2,130},{3,131},{4,132},{5,133},{6,134},{7,135},{8... | collective-permute-start | bytes 737288 | tf_op jit(solution)/shard_map/ppermute | solution.py:286
  132.4 6.9 %collective-permute-start.10 = (f32[15,32,128]{2,1,0:T(8,128)S(1)}, f32[15,32,128]{2,1,0:T(8,128)S(1)}, u32[]{:S(2)}, u32[]{:S(2)}) collective-permute-start(f32[15,32,128]{2,1,0:T(8,128)S(1)} %get-tuple-element.53), channel_id=1, source_target_pairs={{128,0},{129,1},{130,2},{131,3},{132,4},{133,5},{134,6},{135,7},{1... | collective-permute-start | bytes 737288 | tf_op jit(solution)/shard_map/ppermute | solution.py:287
  141.7 8.7 %collective-permute-start.11 = (f32[15,32,128]{2,1,0:T(8,128)S(1)}, f32[15,32,128]{2,1,0:T(8,128)S(1)}, u32[]{:S(2)}, u32[]{:S(2)}) collective-permute-start(f32[15,32,128]{2,1,0:T(8,128)S(1)} %get-tuple-element.54), channel_id=1, source_target_pairs={{0,4},{4,8},{8,12},{12,16},{16,20},{20,24},{24,28},{28,32},{32,36}... | collective-permute-start | bytes 737288 | tf_op jit(solution)/shard_map/ppermute | solution.py:286
  147.3 7.5 %collective-permute-start.12 = (f32[15,32,128]{2,1,0:T(8,128)S(1)}, f32[15,32,128]{2,1,0:T(8,128)S(1)}, u32[]{:S(2)}, u32[]{:S(2)}) collective-permute-start(f32[15,32,128]{2,1,0:T(8,128)S(1)} %get-tuple-element.56), channel_id=1, source_target_pairs={{4,0},{8,4},{12,8},{16,12},{20,16},{24,20},{28,24},{32,28},{36,32}... | collective-permute-start | bytes 737288 | tf_op jit(solution)/shard_map/ppermute | solution.py:287
  157.3 7.9 %collective-permute-start.13 = (f32[15,32,128]{2,1,0:T(8,128)S(1)}, f32[15,32,128]{2,1,0:T(8,128)S(1)}, u32[]{:S(2)}, u32[]{:S(2)}) collective-permute-start(f32[15,32,128]{2,1,0:T(8,128)S(1)} %get-tuple-element.57), channel_id=1, source_target_pairs={{0,128},{1,129},{2,130},{3,131},{4,132},{5,133},{6,134},{7,135},{8... | collective-permute-start | bytes 737288 | tf_op jit(solution)/shard_map/ppermute | solution.py:286
  162.0 7.4 %collective-permute-start.14 = (f32[15,32,128]{2,1,0:T(8,128)S(1)}, f32[15,32,128]{2,1,0:T(8,128)S(1)}, u32[]{:S(2)}, u32[]{:S(2)}) collective-permute-start(f32[15,32,128]{2,1,0:T(8,128)S(1)} %get-tuple-element.59), channel_id=1, source_target_pairs={{128,0},{129,1},{130,2},{131,3},{132,4},{133,5},{134,6},{135,7},{1... | collective-permute-start | bytes 737288 | tf_op jit(solution)/shard_map/ppermute | solution.py:287
  173.6 8.6 %collective-permute-start.15 = (f32[15,32,128]{2,1,0:T(8,128)S(1)}, f32[15,32,128]{2,1,0:T(8,128)S(1)}, u32[]{:S(2)}, u32[]{:S(2)}) collective-permute-start(f32[15,32,128]{2,1,0:T(8,128)S(1)} %get-tuple-element.61), channel_id=1, source_target_pairs={{0,4},{4,8},{8,12},{12,16},{16,20},{20,24},{24,28},{28,32},{32,36}... | collective-permute-start | bytes 737288 | tf_op jit(solution)/shard_map/ppermute | solution.py:286
  179.0 7.5 %collective-permute-start.16 = (f32[15,32,128]{2,1,0:T(8,128)S(1)}, f32[15,32,128]{2,1,0:T(8,128)S(1)}, u32[]{:S(2)}, u32[]{:S(2)}) collective-permute-start(f32[15,32,128]{2,1,0:T(8,128)S(1)} %get-tuple-element.63), channel_id=1, source_target_pairs={{4,0},{8,4},{12,8},{16,12},{20,16},{24,20},{28,24},{32,28},{36,32}... | collective-permute-start | bytes 737288 | tf_op jit(solution)/shard_map/ppermute | solution.py:287
  189.0 6.6 %collective-permute-start.17 = (f32[15,32,128]{2,1,0:T(8,128)S(1)}, f32[15,32,128]{2,1,0:T(8,128)S(1)}, u32[]{:S(2)}, u32[]{:S(2)}) collective-permute-start(f32[15,32,128]{2,1,0:T(8,128)S(1)} %get-tuple-element.64), channel_id=1, source_target_pairs={{0,128},{1,129},{2,130},{3,131},{4,132},{5,133},{6,134},{7,135},{8... | collective-permute-start | bytes 737288 | tf_op jit(solution)/shard_map/ppermute | solution.py:286
  192.4 6.9 %collective-permute-start.18 = (f32[15,32,128]{2,1,0:T(8,128)S(1)}, f32[15,32,128]{2,1,0:T(8,128)S(1)}, u32[]{:S(2)}, u32[]{:S(2)}) collective-permute-start(f32[15,32,128]{2,1,0:T(8,128)S(1)} %get-tuple-element.66), channel_id=1, source_target_pairs={{128,0},{129,1},{130,2},{131,3},{132,4},{133,5},{134,6},{135,7},{1... | collective-permute-start | bytes 737288 | tf_op jit(solution)/shard_map/ppermute | solution.py:287

commit v2 on v1

--- a/solution.py
+++ b/solution.py
@@ -68,13 +68,19 @@
         out_ref[32 * sub : 32 * sub + 32] = out
 
 
-def tiles_of_start(start_ref, taps_ref, out_ref, band_ref):
+def tiles_of_start(start_ref, out_ref):
     store_tiles(start_ref[...], out_ref)
-    rows = jnp.broadcast_to(taps_ref[...], (Z, LANES))
+
+
+def axial_band(psf_ref, out_ref, row_ref):
+    row_ref[...] = jnp.zeros((8, LANES), F32)
+    row_ref[0:1, : psf_ref.shape[1]] = psf_ref[...]
+    psf = row_ref[0:1, :]
+    rows = jnp.broadcast_to(psf / jnp.sum(psf, axis=1, keepdims=True), (Z, LANES))
     rolled = pltpu.roll(rows, LANES - 31, axis=1, stride=1, stride_axis=0)
-    j = lax.broadcasted_iota(jnp.int32, (Z, LANES), 0)
-    z = lax.broadcasted_iota(jnp.int32, (Z, LANES), 1)
-    band_ref[...] = jnp.where(jnp.abs(j - z) <= 31, rolled, 0.0)
+    a = lax.broadcasted_iota(jnp.int32, (Z, LANES), 0)
+    b = lax.broadcasted_iota(jnp.int32, (Z, LANES), 1)
+    out_ref[...] = jnp.where(jnp.abs(a - b) <= 31, rolled, 0.0)
 
 
 def pack_rows(rep_ref, rows_ref, blend_ref, route_ref, line_ref, *refs):
@@ -170,41 +176,85 @@
             out_ref[8 * j + i] = turned[SIDE * j : SIDE * j + SIDE, :]
 
 
-def arrive(got_ref, out_ref, low_ref, high_ref):
+def store_edges(side_ref, out_ref, cross_ref, pair_ref):
+    side = side_ref[0]
+    cross_ref[...] = out_ref[pl.ds(side * (SIDE - RIM), RIM)]
+    pair_ref[...] = out_ref[pl.ds((1 - side) * (SIDE - RIM), RIM)]
+
+
+def arrive(got_ref, out_ref, swapped_ref, first_ref, last_ref, flat_ref):
     columns_from(got_ref, out_ref)
-    low_ref[...] = out_ref[:RIM]
-    high_ref[...] = out_ref[SIDE - RIM :]
-
-
-def convolve(taps_ref, flip, low_ref, mid_ref, high_ref, wide_ref, flat_ref):
-    wide_ref[:RIM] = low_ref[...]
-    wide_ref[RIM : RIM + SIDE] = mid_ref[...]
-    wide_ref[RIM + SIDE :] = high_ref[...]
-    taps = [taps_ref[TAPS - 1 - k if flip else k] for k in range(TAPS)]
+    for x in range(SIDE):
+        flat_ref[SIDE * x : SIDE * x + SIDE, :] = out_ref[x]
+    for y in range(SIDE):
+        swapped_ref[y] = flat_ref[pl.ds(y, SIDE, stride=SIDE), :]
+    first_ref[...] = swapped_ref[:RIM]
+    last_ref[...] = swapped_ref[SIDE - RIM :]
+
+
+def taps_of(taps_ref, flip):
+    return [taps_ref[TAPS - 1 - k if flip else k] for k in range(TAPS)]
+
+
+def own_share(flip, taps_ref, mid_ref, out_ref, wide_ref):
+    taps = taps_of(taps_ref, flip)
+    wide_ref[:8] = jnp.zeros((8, SIDE, Z), F32)
+    wide_ref[8 : 8 + SIDE] = mid_ref[...]
+    wide_ref[8 + SIDE :] = jnp.zeros((8, SIDE, Z), F32)
 
     def block(index, carry):
-        lead = (index // 4) * 8
-        row = pl.multiple_of((index % 4) * 8, 8)
-        total = taps[0] * wide_ref[pl.ds(lead, 8), pl.ds(row, 8), :]
-        for k in range(1, TAPS):
-            total = total + taps[k] * wide_ref[pl.ds(lead + k, 8), pl.ds(row, 8), :]
-        for i in range(8):
-            flat_ref[pl.ds(pl.multiple_of((lead + i) * SIDE + row, 8), 8), :] = total[i]
+        row = pl.multiple_of(index * 8, 8)
+        for lead in range(0, SIDE, 8):
+            total = None
+            for k in range(max(0, RIM - 7 - lead), min(TAPS, SIDE + RIM - lead)):
+                term = taps[k] * wide_ref[lead + k - 7 : lead + k + 1, pl.ds(row, 8), :]
+                total = term if total is None else total + term
+            for i in range(8):
+                out_ref[pl.ds(pl.multiple_of((lead + i) * SIDE + row, 8), 8), :] = total[i]
         return carry
 
-    lax.fori_loop(0, 16, block, 0)
-
-
-def along_x(flip, taps_ref, low_ref, mid_ref, high_ref, out_ref, first_ref, last_ref, wide_ref, flat_ref):
-    convolve(taps_ref, flip, low_ref, mid_ref, high_ref, wide_ref, flat_ref)
+    lax.fori_loop(0, SIDE // 8, block, 0)
+
+
+def add_rims(taps_ref, flip, side, part_ref, near_ref, far_ref, edge_ref, flat_ref):
+    taps = taps_of(taps_ref, flip)
+    zeros = jnp.zeros((8, SIDE, Z), F32)
+    edge_ref[0, RIM : RIM + 8] = zeros
+    edge_ref[1, :8] = zeros
+    edge_ref[side, pl.ds(8 * side, RIM)] = near_ref[...]
+    edge_ref[1 - side, pl.ds(8 * (1 - side), RIM)] = far_ref[...]
+
+    def block(index, carry):
+        row = pl.multiple_of(index * 8, 8)
+        for lead in range(0, SIDE, 8):
+            if lead < SIDE // 2:
+                side, first, ks = 0, lead, range(0, RIM - lead)
+            else:
+                side, first, ks = 1, lead - 39, range(SIDE + RIM - 7 - lead, TAPS)
+            spots = [pl.ds(pl.multiple_of((lead + i) * SIDE + row, 8), 8) for i in range(8)]
+            total = None
+            for k in ks:
+                term = taps[k] * edge_ref[side, first + k : first + k + 8, pl.ds(row, 8), :]
+                total = term if total is None else total + term
+            for i in range(8):
+                flat_ref[spots[i], :] = part_ref[spots[i], :] + total[i]
+        return carry
+
+    lax.fori_loop(0, SIDE // 8, block, 0)
+
+
+def along_x(
+    flip, taps_ref, side_ref, part_ref, cross_ref, pair_ref, out_ref, first_ref, last_ref, edge_ref, flat_ref
+):
+    add_rims(taps_ref, flip, side_ref[0], part_ref, cross_ref, pair_ref, edge_ref, flat_ref)
     for y in range(SIDE):
         out_ref[y] = flat_ref[pl.ds(y, SIDE, stride=SIDE), :]
     first_ref[...] = out_ref[:RIM]
     last_ref[...] = out_ref[SIDE - RIM :]
 
 
-def along_y(taps_ref, flip, low_ref, mid_ref, high_ref, wide_ref, flat_ref, out_ref):
-    convolve(taps_ref, flip, low_ref, mid_ref, high_ref, wide_ref, flat_ref)
+def along_y(taps_ref, flip, part_ref, low_ref, high_ref, edge_ref, flat_ref, out_ref):
+    add_rims(taps_ref, flip, 0, part_ref, low_ref, high_ref, edge_ref, flat_ref)
     for x in range(SIDE):
         out_ref[SIDE * x : SIDE * x + SIDE, :] = flat_ref[pl.ds(x, SIDE, stride=SIDE), :]
 
@@ -213,51 +263,80 @@
     return lax.dot_general(
         value,
         band,
-        (((1,), (1 if back else 0,)), ((), ())),
+        (((1,), (0 if back else 1,)), ((), ())),
         precision=lax.Precision.HIGHEST,
         preferred_element_type=F32,
     )
 
 
-def blur(taps_ref, low_ref, mid_ref, high_ref, band_ref, out_ref, wide_ref, flat_ref, cols_ref):
-    along_y(taps_ref, False, low_ref, mid_ref, high_ref, wide_ref, flat_ref, cols_ref)
-    out_ref[...] = axial(cols_ref[...], band_ref[...], False)
-
-
-def back_axial(ratio, band_ref, out_ref, first_ref, last_ref):
-    back = axial(ratio, band_ref[...], True)
-    out_ref[...] = back.reshape(SIDE, SIDE, Z)
-    first_ref[...] = back[: RIM * SIDE].reshape(RIM, SIDE, Z)
-    last_ref[...] = back[(SIDE - RIM) * SIDE :].reshape(RIM, SIDE, Z)
-
-
-def first_ratio(got_ref, blurred_ref, band_ref, seen_ref, out_ref, first_ref, last_ref):
+def along_y_first(
+    taps_ref, side_ref, part_ref, low_ref, high_ref, out_ref, cross_ref, pair_ref, edge_ref, flat_ref, cols_ref
+):
+    along_y(taps_ref, False, part_ref, low_ref, high_ref, edge_ref, flat_ref, cols_ref)
+    out_ref[...] = cols_ref[...].reshape(SIDE, SIDE, Z)
+    store_edges(side_ref, out_ref, cross_ref, pair_ref)
+
+
+def blur_x_last(taps_ref, side_ref, part_ref, cross_ref, pair_ref, band_ref, out_ref, edge_ref, flat_ref):
+    add_rims(taps_ref, False, side_ref[0], part_ref, cross_ref, pair_ref, edge_ref, flat_ref)
+    out_ref[...] = axial(flat_ref[...], band_ref[...], False)
+
+
+def back_axial(side_ref, ratio, band_ref, out_ref, cross_ref, pair_ref):
+    out_ref[...] = axial(ratio, band_ref[...], True).reshape(SIDE, SIDE, Z)
+    store_edges(side_ref, out_ref, cross_ref, pair_ref)
+
+
+def first_ratio(side_ref, got_ref, blurred_ref, band_ref, seen_ref, out_ref, cross_ref, pair_ref):
     columns_from(got_ref, seen_ref)
     ratio = seen_ref[...].reshape(SIDE * SIDE, Z) / blurred_ref[...]
-    back_axial(ratio, band_ref, out_ref, first_ref, last_ref)
+    back_axial(side_ref, ratio, band_ref, out_ref, cross_ref, pair_ref)
 
 
 def blur_ratio(
-    taps_ref, low_ref, mid_ref, high_ref, band_ref, seen_ref, out_ref, first_ref, last_ref, wide_ref, flat_ref, cols_ref
+    taps_ref,
+    side_ref,
+    part_ref,
+    low_ref,
+    high_ref,
+    band_ref,
+    seen_ref,
+    out_ref,
+    cross_ref,
+    pair_ref,
+    edge_ref,
+    flat_ref,
+    cols_ref,
 ):
-    along_y(taps_ref, False, low_ref, mid_ref, high_ref, wide_ref, flat_ref, cols_ref)
+    along_y(taps_ref, False, part_ref, low_ref, high_ref, edge_ref, flat_ref, cols_ref)
     blurred = axial(cols_ref[...], band_ref[...], False)
-    back_axial(seen_ref[...].reshape(SIDE * SIDE, Z) / blurred, band_ref, out_ref, first_ref, last_ref)
+    ratio = seen_ref[...].reshape(SIDE * SIDE, Z) / blurred
+    back_axial(side_ref, ratio, band_ref, out_ref, cross_ref, pair_ref)
 
 
 def update(
-    taps_ref, low_ref, mid_ref, high_ref, estimate_ref, out_ref, first_ref, last_ref, wide_ref, flat_ref, cols_ref
+    taps_ref,
+    side_ref,
+    part_ref,
+    low_ref,
+    high_ref,
+    estimate_ref,
+    out_ref,
+    cross_ref,
+    pair_ref,
+    edge_ref,
+    flat_ref,
+    cols_ref,
 ):
-    along_y(taps_ref, True, low_ref, mid_ref, high_ref, wide_ref, flat_ref, cols_ref)
+    along_y(taps_ref, True, part_ref, low_ref, high_ref, edge_ref, flat_ref, cols_ref)
     out_ref[...] = estimate_ref[...] * cols_ref[...].reshape(SIDE, SIDE, Z)
-    first_ref[...] = out_ref[:RIM]
-    last_ref[...] = out_ref[SIDE - RIM :]
+    store_edges(side_ref, out_ref, cross_ref, pair_ref)
 
 
 def last_update(
-    taps_ref, low_ref, mid_ref, high_ref, estimate_ref, out_ref, wide_ref, flat_ref, cols_ref
+    taps_ref, part_ref, low_ref, high_ref, estimate_ref, out_ref, edge_ref, flat_ref, cols_ref
 ):
-    along_y(taps_ref, True, low_ref, mid_ref, high_ref, wide_ref, flat_ref, cols_ref)
+    along_y(taps_ref, True, part_ref, low_ref, high_ref, edge_ref, flat_ref, cols_ref)
     for i in range(8):
         block = jnp.concatenate(
             [
@@ -279,13 +358,8 @@
 EDGE = (RIM, SIDE, Z)
 PIECES = (Z, 8, LANES)
 FLAT = (SIDE * SIDE, Z)
-SCRATCH = [((SIDE + 2 * RIM, SIDE, Z), F32), (FLAT, F32), (FLAT, F32)]
-
-
-def exchange(first, last, pairs, axes):
-    low = lax.ppermute(last, axes, pairs)
-    high = lax.ppermute(first, axes, [(b, a) for a, b in pairs])
-    return low, high
+SCRATCH = [((2, RIM + 8, SIDE, Z), F32), (FLAT, F32), (FLAT, F32)]
+WIDE = [((SIDE + 16, SIDE, Z), F32)]
 
 
 def shards(camera_rows, blend, route, line, start, psf_xy, psf_z):
@@ -293,7 +367,12 @@
     x_tiles = LINES // SIDE
     y_tiles = slabs // x_tiles
     chunks = camera_rows.shape[0] // LANES
-    x_pairs = [(t, t + 1) for t in range(slabs) if t % x_tiles != x_tiles - 1]
+    pair_swaps = [(t, t ^ 1) for t in range(slabs)]
+    cross_swaps = []
+    for t in range(1, slabs, 2):
+        if t % x_tiles != x_tiles - 1:
+            cross_swaps += [(t, t + 1), (t + 1, t)]
+    side = (lax.axis_index("slab") % 2).reshape(1)
     y_pairs = []
     for t in range(slabs):
         for r in range(reps):
@@ -302,22 +381,20 @@
                 up = (y % y_tiles) * x_tiles + t % x_tiles
                 y_pairs.append((t * reps + r, up * reps + y // y_tiles))
 
-    def rims_x(first, last):
-        return exchange(first, last, x_pairs, "slab")
+    def rims_x(cross, pair):
+        return lax.ppermute(cross, "slab", cross_swaps), lax.ppermute(pair, "slab", pair_swaps)
 
     def rims_y(first, last):
-        return exchange(first, last, y_pairs, ("slab", "rep"))
+        axes = ("slab", "rep")
+        return lax.ppermute(last, axes, y_pairs), lax.ppermute(first, axes, [(b, a) for a, b in y_pairs])
 
     def turn(pieces):
         return lax.all_to_all(pieces, "slab", split_axis=0, concat_axis=0, tiled=True)
 
     taps = psf_xy / jnp.sum(psf_xy)
-    taps_z = jnp.pad((psf_z / jnp.sum(psf_z))[::-1], (0, LANES - psf_z.shape[0]))[None, :]
-
-    pieces, band = call(
-        tiles_of_start, [PIECES, (Z, LANES)], [], start.reshape(LINES, LANES), taps_z
-    )
-    arrived = turn(pieces)
+
+    arrived = turn(call(tiles_of_start, [PIECES], [], start.reshape(LINES, LANES))[0])
+    band = call(axial_band, [(Z, LANES)], [((8, LANES), F32)], psf_z[None, :])[0]
     sent = call(
         pack_rows,
         [(CAPACITY + META, LANES)] * OWNERS,
@@ -334,35 +411,40 @@
         for step, block in enumerate(sent)
     ]
     seen_pieces = call(observe, [PIECES], [((LINES, CAPACITY), BF16)], *got)[0]
+    arrived, seen_pieces = lax.optimization_barrier((arrived, seen_pieces))
+    estimate, swapped, first, last = call(
+        arrive, [TILE, TILE, EDGE, EDGE], SCRATCH[1:2], arrived.reshape(Z * 8, LANES)
+    )
     seen_arrived = turn(seen_pieces)
-
-    estimate, first, last = call(
-        arrive, [TILE, EDGE, EDGE], [], arrived.reshape(Z * 8, LANES)
-    )
-
-    def lateral_x(flip, value, first, last):
-        low, high = rims_x(first, last)
+    own = functools.partial(call, functools.partial(own_share, False), [FLAT], WIDE, taps, smem=1)
+    own_back = functools.partial(call, functools.partial(own_share, True), [FLAT], WIDE, taps, smem=1)
+
+    def lateral(flip, part, rims):
         value, first, last = call(
-            functools.partial(along_x, flip), [TILE, EDGE, EDGE], SCRATCH[:2], taps, low, value, high, smem=1
+            functools.partial(along_x, flip), [TILE, EDGE, EDGE], SCRATCH[:2], taps, side, part, *rims, smem=2
         )
-        low, high = rims_y(first, last)
-        return low, value, high
-
-    wide = lateral_x(False, estimate, first, last)
-    blurred = call(blur, [FLAT], SCRATCH, taps, *wide, band, smem=1)[0]
-    seen, back, first, last = call(
-        first_ratio, [TILE, TILE, EDGE, EDGE], [], seen_arrived.reshape(Z * 8, LANES), blurred, band
-    )
-    wide = lateral_x(True, back, first, last)
-    estimate, first, last = call(
-        update, [TILE, EDGE, EDGE], SCRATCH, taps, *wide, estimate, smem=1
-    )
-    wide = lateral_x(False, estimate, first, last)
-    back, first, last = call(
-        blur_ratio, [TILE, EDGE, EDGE], SCRATCH, taps, *wide, band, seen, smem=1
-    )
-    wide = lateral_x(True, back, first, last)
-    pieces = call(last_update, [(Z * 8, LANES)], SCRATCH, taps, *wide, estimate, smem=1)[0]
+        rims = rims_y(first, last)
+        return (own_back if flip else own)(value)[0], *rims
+
+    value, *edges = call(
+        along_y_first, [TILE, EDGE, EDGE], SCRATCH, taps, side, own(swapped)[0], *rims_y(first, last), smem=2
+    )
+    blurred = call(
+        blur_x_last, [FLAT], SCRATCH[:2], taps, side, own(value)[0], *rims_x(*edges), band, smem=2
+    )[0]
+    seen, back, *edges = call(
+        first_ratio, [TILE, TILE, EDGE, EDGE], [], side, seen_arrived.reshape(Z * 8, LANES), blurred, band, smem=1
+    )
+    parts = lateral(True, own_back(back)[0], rims_x(*edges))
+    estimate, *edges = call(
+        update, [TILE, EDGE, EDGE], SCRATCH, taps, side, *parts, estimate, smem=2
+    )
+    parts = lateral(False, own(estimate)[0], rims_x(*edges))
+    back, *edges = call(
+        blur_ratio, [TILE, EDGE, EDGE], SCRATCH, taps, side, *parts, band, seen, smem=2
+    )
+    parts = lateral(True, own_back(back)[0], rims_x(*edges))
+    pieces = call(last_update, [(Z * 8, LANES)], SCRATCH, taps, *parts, estimate, smem=1)[0]
     done = turn(pieces.reshape(PIECES))
     plane = call(plane_of, [(LINES // SIDE, SIDE, LANES)], [], done)[0]
     return plane.reshape(1, LINES, LANES)

time: 257 us -> 224 us (0.87)
  waiting for transfers between devices: 73.6 us -> 49.2 us
  blocking collectives: 52.5 us -> 46 us
  starting transfers between devices: 91 us -> 85.3 us
  Pallas kernels: 33.2 us -> 38.3 us
    ppermute x16, waiting for transfers between devices: 59.7 us -> 30.8 us  [the longest x4 17.8 us: rims_y(): lax.ppermute(first, axes, [(b, a) for a, b in y_pairs])]
    all_to_all x1, blocking collectives: 52.5 us -> 46 us  [turn(): lax.all_to_all(pieces, 'slab', split_axis=0, concat_axis=0, tiled=True)]
    ppermute x16, starting transfers between devices: 48.2 us -> 42.6 us  [the longest x4 15.8 us: rims_x(): lax.ppermute(cross, 'slab', cross_swaps)]
    pallas_call x14 -> x23, Pallas kernels: 33.2 us -> 38.3 us  [call(): pl.pallas_call(kernel, out_shape=outs, in_specs=specs, out_specs=tuple((p...]
    all_to_all x2, waiting for transfers between devices: 6.44 us -> 11 us  [turn(): lax.all_to_all(pieces, 'slab', split_axis=0, concat_axis=0, tiled=True)]
  transfers between devices with their start and end apart: 21 -> 21, of which waited for: 19 -> 16; matrix products, arithmetic and copies ran while one was open for 0% -> 1% of each run, Pallas kernels for 5% -> 11%
where the time goes in v2:
time: 224 us; the launch traced here: 223 us
  starting transfers between devices  85.3 us (38%)
  waiting for transfers between devices  49.2 us (22%)
  blocking collectives  46 us (21%)
  Pallas kernels  38.3 us (17%)
  local copies, waits for them, and re-layouts  2.36 us (1%)
    all_to_all x1, blocking collectives, turn(): lax.all_to_all(pieces, 'slab', split_axis=0, concat_axis=0, tiled=True)  46 us
    pallas_call x23, Pallas kernels, call(): pl.pallas_call(kernel, out_shape=outs, in_specs=specs, out_specs=tuple((p...  38.3 us
    all_to_all x2, starting transfers between devices, turn(): lax.all_to_all(pieces, 'slab', split_axis=0, concat_axis=0, tiled=True)  32.2 us
    ppermute x4, waiting for transfers between devices, rims_y(): lax.ppermute(first, axes, [(b, a) for a, b in y_pairs])  17.8 us
    ppermute x4, starting transfers between devices, rims_x(): lax.ppermute(cross, 'slab', cross_swaps)  15.8 us
    ppermute x4, starting transfers between devices, rims_y(): lax.ppermute(last, axes, y_pairs)  13.7 us
    all_to_all x2, waiting for transfers between devices, turn(): lax.all_to_all(pieces, 'slab', split_axis=0, concat_axis=0, tiled=True)  11 us
    ppermute x3, starting transfers between devices, shards(): lax.ppermute(block, 'rep', [(r, (r + step) % reps) for r in range(reps)])  10.5 us
  transfers between devices with their start and end apart: 21, of which 16 were waited for; matrix products, arithmetic and copies ran while one was open for 1% of the time, Pallas kernels for 11%

profile of v2, /device:TPU:1, one launch (start us, length us, event | category | flops | bytes accessed | tf_op | source)
XLA Modules:
  0.0 222.8 jit_solution(6772600716280130775)
XLA Ops:
  0.0 1.0 copy-done.1
  1.0 1.3 tiles_of_start.1
  2.3 20.7 %all-to-all-start = ((f32[128,8,128]{2,1,0:T(8,128)}), f32[128,8,128]{2,1,0:T(8,128)S(1)}, u32[]{:S(2)}, u32[]{:S(2)}) async-start(f32[128,8,128]{2,1,0:T(8,128)} %tiles_of_start.1), calls=%async_computation | async-start | bytes 1048576 | tf_op jit(solution)/shard_map/all_to_all | solution.py:392
  23.1 0.7 copy-done.2
  23.7 3.8 %pack_rows.1 = (f32[520,128]{1,0:T(8,128)S(1)}, f32[520,128]{1,0:T(8,128)S(1)}, f32[520,128]{1,0:T(8,128)S(1)}, f32[520,128]{1,0:T(8,128)S(1)}) custom-call(s32[1]{0:T(128)} %bitcast.2.rep_ref, f32[1280,128]{1,0:T(8,128)S(1)} %copy-done, f32[10,128]{1,0:T(8,128)S(1)} %bitcast.15, s32[10,128]{1,0:T(8,128)S(1)} %bitcast.16, s32[10,128]{1,0:T(8,128)S(1)} %bitcast.17), custom_call_target="tpu_custom_call" | custom-call | tf_op jit(solution)/shard_map/pack_rows/pallas_call | solution.py:30
  27.5 3.1 %collective-permute-start = (f32[520,128]{1,0:T(8,128)S(1)}, f32[520,128]{1,0:T(8,128)S(1)}, u32[]{:S(2)}, u32[]{:S(2)}) collective-permute-start(f32[520,128]{1,0:T(8,128)S(1)} %get-tuple-element.38), channel_id=1, source_target_pairs={{0,1},{1,2},{2,3},{3,0},{4,5},{5,6},{6,7},{7,4},{8,9},{9,10},{10,1... | collective-permute-start | bytes 798728 | tf_op jit(solution)/shard_map/ppermute | solution.py:410
  30.6 4.4 %collective-permute-start.1 = (f32[520,128]{1,0:T(8,128)S(1)}, f32[520,128]{1,0:T(8,128)S(1)}, u32[]{:S(2)}, u32[]{:S(2)}) collective-permute-start(f32[520,128]{1,0:T(8,128)S(1)} %get-tuple-element.39), channel_id=1, source_target_pairs={{0,2},{1,3},{2,0},{3,1},{4,6},{5,7},{6,4},{7,5},{8,10},{9,11},{10,... | collective-permute-start | bytes 798728 | tf_op jit(solution)/shard_map/ppermute | solution.py:410
  35.0 3.1 %collective-permute-start.2 = (f32[520,128]{1,0:T(8,128)S(1)}, f32[520,128]{1,0:T(8,128)S(1)}, u32[]{:S(2)}, u32[]{:S(2)}) collective-permute-start(f32[520,128]{1,0:T(8,128)S(1)} %get-tuple-element.40), channel_id=1, source_target_pairs={{0,3},{1,0},{2,1},{3,2},{4,7},{5,4},{6,5},{7,6},{8,11},{9,8},{10,9... | collective-permute-start | bytes 798728 | tf_op jit(solution)/shard_map/ppermute | solution.py:410
  38.1 6.2 %collective-permute-done.1.refs_2_ = f32[520,128]{1,0:T(8,128)S(1)} collective-permute-done((f32[520,128]{1,0:T(8,128)S(1)}, f32[520,128]{1,0:T(8,128)S(1)}, u32[]{:S(2)}, u32[]{:S(2)}) %collective-permute-start.1) | collective-permute-done | bytes 266272 | tf_op jit(solution)/shard_map/ppermute | solution.py:410
  44.3 1.2 collective-permute-done.2.refs_3_
  45.5 4.3 %observe.1 = f32[128,8,128]{2,1,0:T(8,128)} custom-call(f32[520,128]{1,0:T(8,128)S(1)} %get-tuple-element.37.refs_0_, f32[520,128]{1,0:T(8,128)S(1)} %collective-permute-done.refs_1_, f32[520,128]{1,0:T(8,128)S(1)} %collective-permute-done.1.refs_2_, f32[520,128]{1,0:T(8,128)S(1)} %collective-permute-done.2.refs_3_), custom_call_target="tpu_custom_call" | custom-call | tf_op jit(solution)/shard_map/observe/pallas_call | solution.py:30
  49.8 6.4 %all-to-all-done = f32[128,8,128]{2,1,0:T(8,128)S(1)} async-done(((f32[128,8,128]{2,1,0:T(8,128)}), f32[128,8,128]{2,1,0:T(8,128)S(1)}, u32[]{:S(2)}, u32[]{:S(2)}) %all-to-all-start) | async-done | bytes 524320 | tf_op jit(solution)/shard_map/all_to_all | solution.py:392
  56.2 11.5 %all-to-all-start.1 = ((f32[128,8,128]{2,1,0:T(8,128)}), f32[128,8,128]{2,1,0:T(8,128)S(1)}, u32[]{:S(2)}, u32[]{:S(2)}) async-start(f32[128,8,128]{2,1,0:T(8,128)} %observe.1), calls=%async_computation.1 | async-start | bytes 1048576 | tf_op jit(solution)/shard_map/all_to_all | solution.py:392
  67.7 0.5 arrive.1
  68.2 3.4 %collective-permute-start.3 = (f32[15,32,128]{2,1,0:T(8,128)S(1)}, f32[15,32,128]{2,1,0:T(8,128)S(1)}, u32[]{:S(2)}, u32[]{:S(2)}) collective-permute-start(f32[15,32,128]{2,1,0:T(8,128)S(1)} %get-tuple-element.44), channel_id=1, source_target_pairs={{0,128},{1,129},{2,130},{3,131},{4,132},{5,133},{6,134},{7,135},{8... | collective-permute-start | bytes 737288 | tf_op jit(solution)/shard_map/ppermute | solution.py:389
  71.6 1.3 collective-permute-start.4
  73.0 0.6 copy-done.6
  73.6 0.7 reduce_sum.9
  74.3 0.7 broadcast_divide_fusion.taps_ref
  75.0 1.7 own_share.8.part_ref
  76.6 1.4 collective-permute-done.3.low_ref
  78.0 3.7 %collective-permute-done.4.high_ref = f32[15,32,128]{2,1,0:T(8,128)S(1)} collective-permute-done((f32[15,32,128]{2,1,0:T(8,128)S(1)}, f32[15,32,128]{2,1,0:T(8,128)S(1)}, u32[]{:S(2)}, u32[]{:S(2)}) %collective-permute-start.4) | collective-permute-done | bytes 245792 | tf_op jit(solution)/shard_map/ppermute | solution.py:389
  81.8 1.4 along_y_first.1
  83.1 4.7 %collective-permute-start.5 = (f32[15,32,128]{2,1,0:T(8,128)S(1)}, f32[15,32,128]{2,1,0:T(8,128)S(1)}, u32[]{:S(2)}, u32[]{:S(2)}) collective-permute-start(f32[15,32,128]{2,1,0:T(8,128)S(1)} %get-tuple-element.47), channel_id=1, source_target_pairs={{4,8},{8,4},{12,16},{16,12},{20,24},{24,20},{28,32},{32,28},{36,40... | collective-permute-start | bytes 737288 | tf_op jit(solution)/shard_map/ppermute | solution.py:385
  87.9 2.1 collective-permute-start.6
  90.2 1.7 own_share.9.part_ref
  91.8 3.0 %collective-permute-done.5.cross_ref = f32[15,32,128]{2,1,0:T(8,128)S(1)} collective-permute-done((f32[15,32,128]{2,1,0:T(8,128)S(1)}, f32[15,32,128]{2,1,0:T(8,128)S(1)}, u32[]{:S(2)}, u32[]{:S(2)}) %collective-permute-start.5) | collective-permute-done | bytes 245792 | tf_op jit(solution)/shard_map/ppermute | solution.py:385
  94.8 1.6 blur_x_last.1.blurred_ref
  96.4 4.5 %all-to-all-done.1 = f32[128,8,128]{2,1,0:T(8,128)S(1)} async-done(((f32[128,8,128]{2,1,0:T(8,128)}), f32[128,8,128]{2,1,0:T(8,128)S(1)}, u32[]{:S(2)}, u32[]{:S(2)}) %all-to-all-start.1) | async-done | bytes 524320 | tf_op jit(solution)/shard_map/all_to_all | solution.py:392
  100.9 0.7 first_ratio.1
  101.7 4.8 %collective-permute-start.7 = (f32[15,32,128]{2,1,0:T(8,128)S(1)}, f32[15,32,128]{2,1,0:T(8,128)S(1)}, u32[]{:S(2)}, u32[]{:S(2)}) collective-permute-start(f32[15,32,128]{2,1,0:T(8,128)S(1)} %get-tuple-element.50), channel_id=1, source_target_pairs={{4,8},{8,4},{12,16},{16,12},{20,24},{24,20},{28,32},{32,28},{36,40... | collective-permute-start | bytes 737288 | tf_op jit(solution)/shard_map/ppermute | solution.py:385
  106.5 1.9 collective-permute-start.8
  108.4 1.7 own_share.10.part_ref
  110.1 0.3 collective-permute-done.7.cross_ref
  110.4 1.4 along_x.3
  111.7 1.9 collective-permute-start.9
  113.6 1.3 collective-permute-start.10
  114.9 1.7 own_share.11.part_ref
  116.6 2.1 collective-permute-done.9.low_ref
  118.7 3.8 %collective-permute-done.10.high_ref = f32[15,32,128]{2,1,0:T(8,128)S(1)} collective-permute-done((f32[15,32,128]{2,1,0:T(8,128)S(1)}, f32[15,32,128]{2,1,0:T(8,128)S(1)}, u32[]{:S(2)}, u32[]{:S(2)}) %collective-permute-start.10) | collective-permute-done | bytes 245792 | tf_op jit(solution)/shard_map/ppermute | solution.py:389
  122.5 1.4 update.1
  123.9 3.7 %collective-permute-start.11 = (f32[15,32,128]{2,1,0:T(8,128)S(1)}, f32[15,32,128]{2,1,0:T(8,128)S(1)}, u32[]{:S(2)}, u32[]{:S(2)}) collective-permute-start(f32[15,32,128]{2,1,0:T(8,128)S(1)} %get-tuple-element.57), channel_id=1, source_target_pairs={{4,8},{8,4},{12,16},{16,12},{20,24},{24,20},{28,32},{32,28},{36,40... | collective-permute-start | bytes 737288 | tf_op jit(solution)/shard_map/ppermute | solution.py:385
  127.6 1.9 collective-permute-start.12
  129.6 1.7 own_share.12.part_ref
  131.5 1.4 along_x.4
  132.9 3.0 %collective-permute-start.13 = (f32[15,32,128]{2,1,0:T(8,128)S(1)}, f32[15,32,128]{2,1,0:T(8,128)S(1)}, u32[]{:S(2)}, u32[]{:S(2)}) collective-permute-start(f32[15,32,128]{2,1,0:T(8,128)S(1)} %get-tuple-element.60), channel_id=1, source_target_pairs={{0,128},{1,129},{2,130},{3,131},{4,132},{5,133},{6,134},{7,135},{8... | collective-permute-start | bytes 737288 | tf_op jit(solution)/shard_map/ppermute | solution.py:389
  135.9 1.3 collective-permute-start.14
  137.2 1.7 own_share.13.part_ref
  138.8 2.1 collective-permute-done.13.low_ref
  141.0 6.0 %collective-permute-done.14.high_ref = f32[15,32,128]{2,1,0:T(8,128)S(1)} collective-permute-done((f32[15,32,128]{2,1,0:T(8,128)S(1)}, f32[15,32,128]{2,1,0:T(8,128)S(1)}, u32[]{:S(2)}, u32[]{:S(2)}) %collective-permute-start.14) | collective-permute-done | bytes 245792 | tf_op jit(solution)/shard_map/ppermute | solution.py:389
  147.0 3.1 %blur_ratio.1 = (f32[32,32,128]{2,1,0:T(8,128)S(1)}, f32[15,32,128]{2,1,0:T(8,128)S(1)}, f32[15,32,128]{2,1,0:T(8,128)S(1)}) custom-call(f32[31]{0:T(128)S(1)} %broadcast_divide_fusion.taps_ref, s32[1]{0:T(128)} %bitcast.side_ref, f32[1024,128]{1,0:T(8,128)S(1)} %own_share.13.part_ref, f32[15,32,128]{2,1,0:T(8,128)S(1)} %collective-permute-done.13.low_ref, ...), custom_call_target="tpu_custom_call" | custom-call | tf_op jit(solution)/shard_map/blur_ratio/pallas_call | solution.py:30
  150.1 2.6 %collective-permute-start.15 = (f32[15,32,128]{2,1,0:T(8,128)S(1)}, f32[15,32,128]{2,1,0:T(8,128)S(1)}, u32[]{:S(2)}, u32[]{:S(2)}) collective-permute-start(f32[15,32,128]{2,1,0:T(8,128)S(1)} %get-tuple-element.64), channel_id=1, source_target_pairs={{4,8},{8,4},{12,16},{16,12},{20,24},{24,20},{28,32},{32,28},{36,40... | collective-permute-start | bytes 737288 | tf_op jit(solution)/shard_map/ppermute | solution.py:385
  152.7 1.9 collective-permute-start.16
  154.6 1.7 own_share.14.part_ref
  156.3 1.3 collective-permute-done.15.cross_ref
  157.6 1.4 along_x.5
  158.9 5.4 %collective-permute-start.17 = (f32[15,32,128]{2,1,0:T(8,128)S(1)}, f32[15,32,128]{2,1,0:T(8,128)S(1)}, u32[]{:S(2)}, u32[]{:S(2)}) collective-permute-start(f32[15,32,128]{2,1,0:T(8,128)S(1)} %get-tuple-element.67), channel_id=1, source_target_pairs={{0,128},{1,129},{2,130},{3,131},{4,132},{5,133},{6,134},{7,135},{8... | collective-permute-start | bytes 737288 | tf_op jit(solution)/shard_map/ppermute | solution.py:389
  164.3 1.3 collective-permute-start.18
  165.6 1.7 own_share.15.part_ref
  167.3 2.5 %collective-permute-done.17.low_ref = f32[15,32,128]{2,1,0:T(8,128)S(1)} collective-permute-done((f32[15,32,128]{2,1,0:T(8,128)S(1)}, f32[15,32,128]{2,1,0:T(8,128)S(1)}, u32[]{:S(2)}, u32[]{:S(2)}) %collective-permute-start.17) | collective-permute-done | bytes 245792 | tf_op jit(solution)/shard_map/ppermute | solution.py:389
  169.9 4.3 %collective-permute-done.18.high_ref = f32[15,32,128]{2,1,0:T(8,128)S(1)} collective-permute-done((f32[15,32,128]{2,1,0:T(8,128)S(1)}, f32[15,32,128]{2,1,0:T(8,128)S(1)}, u32[]{:S(2)}, u32[]{:S(2)}) %collective-permute-start.18) | collective-permute-done | bytes 245792 | tf_op jit(solution)/shard_map/ppermute | solution.py:389
  174.1 1.4 last_update.1
  175.6 46.0 %all_to_all.15.got_ref = f32[128,8,128]{2,1,0:T(8,128)S(1)} all-to-all(f32[128,8,128]{2,1,0:T(8,128)S(1)} %bitcast.11), channel_id=1, replica_groups=mesh['slab'=128,'rep'=4] {'slab'}, dimensions={0} | all-to-all | bytes 1048576 | tf_op jit(solution)/shard_map/all_to_all | solution.py:392
  221.6 1.3 plane_of.1
  (18 shorter events, 0.5 us)
Async XLA Ops:
  0.0 1.0 copy-start.1
  2.3 20.7 %copy-start = (f32[1280,128]{1,0:T(8,128)S(1)}, f32[1280,128]{1,0:T(8,128)}, u32[]{:S(2)}) copy-start(f32[1280,128]{1,0:T(8,128)} %rows_ref.1) | copy-start | bytes 1966084
  2.3 20.7 %copy-start.3 = (s32[1280]{0:T(1024)S(1)}, s32[1280]{0:T(1024)}, u32[]{:S(2)}) copy-start(s32[1280]{0:T(1024)} %param.9) | copy-start | bytes 15364
  2.3 20.7 %copy-start.4 = (s32[1280]{0:T(1024)S(1)}, s32[1280]{0:T(1024)}, u32[]{:S(2)}) copy-start(s32[1280]{0:T(1024)} %param.10) | copy-start | bytes 15364
  2.3 53.9 %all-to-all-start = ((f32[128,8,128]{2,1,0:T(8,128)}), f32[128,8,128]{2,1,0:T(8,128)S(1)}, u32[]{:S(2)}, u32[]{:S(2)}) async-start(f32[128,8,128]{2,1,0:T(8,128)} %tiles_of_start.1), calls=%async_computation | async-start | bytes 1048576 | tf_op jit(solution)/shard_map/all_to_all | solution.py:392
  23.0 0.7 copy-start.2
  27.5 10.6 %collective-permute-start = (f32[520,128]{1,0:T(8,128)S(1)}, f32[520,128]{1,0:T(8,128)S(1)}, u32[]{:S(2)}, u32[]{:S(2)}) collective-permute-start(f32[520,128]{1,0:T(8,128)S(1)} %get-tuple-element.38), channel_id=1, source_target_pairs={{0,1},{1,2},{2,3},{3,0},{4,5},{5,6},{6,7},{7,4},{8,9},{9,10},{10,1... | collective-permute-start | bytes 798728 | tf_op jit(solution)/shard_map/ppermute | solution.py:410
  30.6 13.7 %collective-permute-start.1 = (f32[520,128]{1,0:T(8,128)S(1)}, f32[520,128]{1,0:T(8,128)S(1)}, u32[]{:S(2)}, u32[]{:S(2)}) collective-permute-start(f32[520,128]{1,0:T(8,128)S(1)} %get-tuple-element.39), channel_id=1, source_target_pairs={{0,2},{1,3},{2,0},{3,1},{4,6},{5,7},{6,4},{7,5},{8,10},{9,11},{10,... | collective-permute-start | bytes 798728 | tf_op jit(solution)/shard_map/ppermute | solution.py:410
  35.0 10.5 %collective-permute-start.2 = (f32[520,128]{1,0:T(8,128)S(1)}, f32[520,128]{1,0:T(8,128)S(1)}, u32[]{:S(2)}, u32[]{:S(2)}) collective-permute-start(f32[520,128]{1,0:T(8,128)S(1)} %get-tuple-element.40), channel_id=1, source_target_pairs={{0,3},{1,0},{2,1},{3,2},{4,7},{5,4},{6,5},{7,6},{8,11},{9,8},{10,9... | collective-permute-start | bytes 798728 | tf_op jit(solution)/shard_map/ppermute | solution.py:410
  56.2 44.7 %all-to-all-start.1 = ((f32[128,8,128]{2,1,0:T(8,128)}), f32[128,8,128]{2,1,0:T(8,128)S(1)}, u32[]{:S(2)}, u32[]{:S(2)}) async-start(f32[128,8,128]{2,1,0:T(8,128)} %observe.1), calls=%async_computation.1 | async-start | bytes 1048576 | tf_op jit(solution)/shard_map/all_to_all | solution.py:392
  68.2 9.8 %collective-permute-start.3 = (f32[15,32,128]{2,1,0:T(8,128)S(1)}, f32[15,32,128]{2,1,0:T(8,128)S(1)}, u32[]{:S(2)}, u32[]{:S(2)}) collective-permute-start(f32[15,32,128]{2,1,0:T(8,128)S(1)} %get-tuple-element.44), channel_id=1, source_target_pairs={{0,128},{1,129},{2,130},{3,131},{4,132},{5,133},{6,134},{7,135},{8... | collective-permute-start | bytes 737288 | tf_op jit(solution)/shard_map/ppermute | solution.py:389
  71.6 10.1 %collective-permute-start.4 = (f32[15,32,128]{2,1,0:T(8,128)S(1)}, f32[15,32,128]{2,1,0:T(8,128)S(1)}, u32[]{:S(2)}, u32[]{:S(2)}) collective-permute-start(f32[15,32,128]{2,1,0:T(8,128)S(1)} %get-tuple-element.45), channel_id=1, source_target_pairs={{128,0},{129,1},{130,2},{131,3},{132,4},{133,5},{134,6},{135,7},{1... | collective-permute-start | bytes 737288 | tf_op jit(solution)/shard_map/ppermute | solution.py:389
  72.9 0.7 copy-start.6
  83.1 11.7 %collective-permute-start.5 = (f32[15,32,128]{2,1,0:T(8,128)S(1)}, f32[15,32,128]{2,1,0:T(8,128)S(1)}, u32[]{:S(2)}, u32[]{:S(2)}) collective-permute-start(f32[15,32,128]{2,1,0:T(8,128)S(1)} %get-tuple-element.47), channel_id=1, source_target_pairs={{4,8},{8,4},{12,16},{16,12},{20,24},{24,20},{28,32},{32,28},{36,40... | collective-permute-start | bytes 737288 | tf_op jit(solution)/shard_map/ppermute | solution.py:385
  87.9 2.1 copy-start.5
  87.9 6.9 %collective-permute-start.6 = (f32[15,32,128]{2,1,0:T(8,128)S(1)}, f32[15,32,128]{2,1,0:T(8,128)S(1)}, u32[]{:S(2)}, u32[]{:S(2)}) collective-permute-start(f32[15,32,128]{2,1,0:T(8,128)S(1)} %get-tuple-element.48), channel_id=1, source_target_pairs={{0,4},{4,0},{8,12},{12,8},{16,20},{20,16},{24,28},{28,24},{32,36},... | collective-permute-start | bytes 737288 | tf_op jit(solution)/shard_map/ppermute | solution.py:385
  101.7 8.7 %collective-permute-start.7 = (f32[15,32,128]{2,1,0:T(8,128)S(1)}, f32[15,32,128]{2,1,0:T(8,128)S(1)}, u32[]{:S(2)}, u32[]{:S(2)}) collective-permute-start(f32[15,32,128]{2,1,0:T(8,128)S(1)} %get-tuple-element.50), channel_id=1, source_target_pairs={{4,8},{8,4},{12,16},{16,12},{20,24},{24,20},{28,32},{32,28},{36,40... | collective-permute-start | bytes 737288 | tf_op jit(solution)/shard_map/ppermute | solution.py:385
  106.5 3.9 %collective-permute-start.8 = (f32[15,32,128]{2,1,0:T(8,128)S(1)}, f32[15,32,128]{2,1,0:T(8,128)S(1)}, u32[]{:S(2)}, u32[]{:S(2)}) collective-permute-start(f32[15,32,128]{2,1,0:T(8,128)S(1)} %get-tuple-element.51), channel_id=1, source_target_pairs={{0,4},{4,0},{8,12},{12,8},{16,20},{20,16},{24,28},{28,24},{32,36},... | collective-permute-start | bytes 737288 | tf_op jit(solution)/shard_map/ppermute | solution.py:385
  111.7 7.0 %collective-permute-start.9 = (f32[15,32,128]{2,1,0:T(8,128)S(1)}, f32[15,32,128]{2,1,0:T(8,128)S(1)}, u32[]{:S(2)}, u32[]{:S(2)}) collective-permute-start(f32[15,32,128]{2,1,0:T(8,128)S(1)} %get-tuple-element.53), channel_id=1, source_target_pairs={{0,128},{1,129},{2,130},{3,131},{4,132},{5,133},{6,134},{7,135},{8... | collective-permute-start | bytes 737288 | tf_op jit(solution)/shard_map/ppermute | solution.py:389
  113.6 8.9 %collective-permute-start.10 = (f32[15,32,128]{2,1,0:T(8,128)S(1)}, f32[15,32,128]{2,1,0:T(8,128)S(1)}, u32[]{:S(2)}, u32[]{:S(2)}) collective-permute-start(f32[15,32,128]{2,1,0:T(8,128)S(1)} %get-tuple-element.54), channel_id=1, source_target_pairs={{128,0},{129,1},{130,2},{131,3},{132,4},{133,5},{134,6},{135,7},{1... | collective-permute-start | bytes 737288 | tf_op jit(solution)/shard_map/ppermute | solution.py:389
  123.9 7.6 %collective-permute-start.11 = (f32[15,32,128]{2,1,0:T(8,128)S(1)}, f32[15,32,128]{2,1,0:T(8,128)S(1)}, u32[]{:S(2)}, u32[]{:S(2)}) collective-permute-start(f32[15,32,128]{2,1,0:T(8,128)S(1)} %get-tuple-element.57), channel_id=1, source_target_pairs={{4,8},{8,4},{12,16},{16,12},{20,24},{24,20},{28,32},{32,28},{36,40... | collective-permute-start | bytes 737288 | tf_op jit(solution)/shard_map/ppermute | solution.py:385
  127.6 3.9 %collective-permute-start.12 = (f32[15,32,128]{2,1,0:T(8,128)S(1)}, f32[15,32,128]{2,1,0:T(8,128)S(1)}, u32[]{:S(2)}, u32[]{:S(2)}) collective-permute-start(f32[15,32,128]{2,1,0:T(8,128)S(1)} %get-tuple-element.58), channel_id=1, source_target_pairs={{0,4},{4,0},{8,12},{12,8},{16,20},{20,16},{24,28},{28,24},{32,36},... | collective-permute-start | bytes 737288 | tf_op jit(solution)/shard_map/ppermute | solution.py:385
  132.9 8.1 %collective-permute-start.13 = (f32[15,32,128]{2,1,0:T(8,128)S(1)}, f32[15,32,128]{2,1,0:T(8,128)S(1)}, u32[]{:S(2)}, u32[]{:S(2)}) collective-permute-start(f32[15,32,128]{2,1,0:T(8,128)S(1)} %get-tuple-element.60), channel_id=1, source_target_pairs={{0,128},{1,129},{2,130},{3,131},{4,132},{5,133},{6,134},{7,135},{8... | collective-permute-start | bytes 737288 | tf_op jit(solution)/shard_map/ppermute | solution.py:389
  135.9 11.1 %collective-permute-start.14 = (f32[15,32,128]{2,1,0:T(8,128)S(1)}, f32[15,32,128]{2,1,0:T(8,128)S(1)}, u32[]{:S(2)}, u32[]{:S(2)}) collective-permute-start(f32[15,32,128]{2,1,0:T(8,128)S(1)} %get-tuple-element.61), channel_id=1, source_target_pairs={{128,0},{129,1},{130,2},{131,3},{132,4},{133,5},{134,6},{135,7},{1... | collective-permute-start | bytes 737288 | tf_op jit(solution)/shard_map/ppermute | solution.py:389
  150.1 7.5 %collective-permute-start.15 = (f32[15,32,128]{2,1,0:T(8,128)S(1)}, f32[15,32,128]{2,1,0:T(8,128)S(1)}, u32[]{:S(2)}, u32[]{:S(2)}) collective-permute-start(f32[15,32,128]{2,1,0:T(8,128)S(1)} %get-tuple-element.64), channel_id=1, source_target_pairs={{4,8},{8,4},{12,16},{16,12},{20,24},{24,20},{28,32},{32,28},{36,40... | collective-permute-start | bytes 737288 | tf_op jit(solution)/shard_map/ppermute | solution.py:385
  152.7 4.9 %collective-permute-start.16 = (f32[15,32,128]{2,1,0:T(8,128)S(1)}, f32[15,32,128]{2,1,0:T(8,128)S(1)}, u32[]{:S(2)}, u32[]{:S(2)}) collective-permute-start(f32[15,32,128]{2,1,0:T(8,128)S(1)} %get-tuple-element.65), channel_id=1, source_target_pairs={{0,4},{4,0},{8,12},{12,8},{16,20},{20,16},{24,28},{28,24},{32,36},... | collective-permute-start | bytes 737288 | tf_op jit(solution)/shard_map/ppermute | solution.py:385
  158.9 10.9 %collective-permute-start.17 = (f32[15,32,128]{2,1,0:T(8,128)S(1)}, f32[15,32,128]{2,1,0:T(8,128)S(1)}, u32[]{:S(2)}, u32[]{:S(2)}) collective-permute-start(f32[15,32,128]{2,1,0:T(8,128)S(1)} %get-tuple-element.67), channel_id=1, source_target_pairs={{0,128},{1,129},{2,130},{3,131},{4,132},{5,133},{6,134},{7,135},{8... | collective-permute-start | bytes 737288 | tf_op jit(solution)/shard_map/ppermute | solution.py:389
  164.3 9.8 %collective-permute-start.18 = (f32[15,32,128]{2,1,0:T(8,128)S(1)}, f32[15,32,128]{2,1,0:T(8,128)S(1)}, u32[]{:S(2)}, u32[]{:S(2)}) collective-permute-start(f32[15,32,128]{2,1,0:T(8,128)S(1)} %get-tuple-element.68), channel_id=1, source_target_pairs={{128,0},{129,1},{130,2},{131,3},{132,4},{133,5},{134,6},{135,7},{1... | collective-permute-start | bytes 737288 | tf_op jit(solution)/shard_map/ppermute | solution.py:389

commit v3 on v2

v3 whole, which is shorter than its diff:
```python
import functools

import jax
import jax.numpy as jnp
from jax import lax
from jax.experimental import pallas as pl
from jax.experimental.pallas import tpu as pltpu
from jax.sharding import PartitionSpec as P

F32 = jnp.float32
BF16 = jnp.bfloat16
LANES = 128
SIDE = 32
TAPS = 31
RIM = TAPS // 2
OWNERS = 4
CAPACITY = 512
META = 8
LINES = 1024
Z = 128
VMEM_LIMIT = 40 * 1024 * 1024


def call(kernel, out_shapes, scratch, *args, smem=0):
    specs = [
        pl.BlockSpec(memory_space=pltpu.SMEM if i < smem else pltpu.VMEM)
        for i in range(len(args))
    ]
    outs = tuple(jax.ShapeDtypeStruct(s, F32) for s in out_shapes)
    return pl.pallas_call(
        kernel,
        out_shape=outs,
        in_specs=specs,
        out_specs=tuple(pl.BlockSpec(memory_space=pltpu.VMEM) for _ in outs),
        scratch_shapes=[pltpu.VMEM(s, d) for s, d in scratch],
        compiler_params=pltpu.CompilerParams(vmem_limit_bytes=VMEM_LIMIT),
        name=kernel.func.__name__ if isinstance(kernel, functools.partial) else kernel.__name__,
    )(*args)


def halves(value):
    high = value.astype(BF16)
    return high, (value - high.astype(F32)).astype(BF16)


def thirds(value):
    high, rest = halves(value)
    low = (value - high.astype(F32) - rest.astype(F32)).astype(BF16)
    return high, rest, low


def swap_lanes(pairs, first, moves):
    mixed = [jnp.where(first, b, a) for a, b in pairs]
    up = [pltpu.roll(m, moves[0], axis=1) for m in mixed]
    down = up if moves[0] == moves[1] else [pltpu.roll(m, moves[1], axis=1) for m in mixed]
    return [
        (jnp.where(first, a, u), jnp.where(first, d, b)) for (a, b), u, d in zip(pairs, up, down, strict=True)
    ]


def lane_blocks(pieces):
    lane = lax.broadcasted_iota(jnp.int32, (8, LANES), 1)
    outer = swap_lanes([pair for a, b, c, d in pieces for pair in ((a, c), (b, d))], lane < 64, (64, 64))
    rows = [(ac[0], bd[0], ac[1], bd[1]) for ac, bd in zip(outer[::2], outer[1::2], strict=True)]
    inner = swap_lanes([pair for a, b, c, d in rows for pair in ((a, b), (c, d))], lane % 64 < 32, (32, 96))
    return [ab + cd for ab, cd in zip(inner[::2], inner[1::2], strict=True)]


def store_tiles(plane_ref, out_ref):
    for first in range(0, 32, 8):
        parts = range(first, first + 8)
        rows = [
            tuple(plane_ref[SIDE * p + 8 * j : SIDE * p + 8 * j + 8, :] for j in range(4)) for p in parts
        ]
        for part, piece in zip(parts, lane_blocks(rows), strict=True):
            for sub in range(4):
                out_ref[32 * sub + part] = piece[sub]


def plane_of(got_ref, out_ref):
    for first in range(0, 32, 8):
        parts = range(first, first + 8)
        pieces = [tuple(got_ref[32 * sub + p] for sub in range(4)) for p in parts]
        for part, rows in zip(parts, lane_blocks(pieces), strict=True):
            for j in range(4):
                out_ref[SIDE * part + 8 * j : SIDE * part + 8 * j + 8, :] = rows[j]


def axial_band(psf_ref, out_ref, row_ref):
    row_ref[...] = jnp.zeros((8, LANES), F32)
    row_ref[0:1, : psf_ref.shape[1]] = psf_ref[...]
    psf = row_ref[0:1, :]
    rows = jnp.broadcast_to(psf / jnp.sum(psf, axis=1, keepdims=True), (Z, LANES))
    rolled = pltpu.roll(rows, LANES - 31, axis=1, stride=1, stride_axis=0)
    a = lax.broadcasted_iota(jnp.int32, (Z, LANES), 0)
    b = lax.broadcasted_iota(jnp.int32, (Z, LANES), 1)
    out_ref[...] = jnp.where(jnp.abs(a - b) <= 31, rolled, 0.0)


def pack_rows(rep_ref, rows_ref, blend_ref, route_ref, line_ref, *refs):
    out_refs, (split_ref, hot_ref) = refs[:OWNERS], refs[OWNERS:]
    chunks = rows_ref.shape[0] // LANES
    blend = blend_ref[...]
    route = route_ref[...]
    line = line_ref[...]
    i = lax.broadcasted_iota(jnp.int32, (LANES, LANES), 0)
    j = lax.broadcasted_iota(jnp.int32, (LANES, LANES), 1)
    upto = (i <= j).astype(BF16)
    ones = jnp.ones((LANES, LANES), BF16)
    ci = lax.broadcasted_iota(jnp.int32, (16, 16), 0)
    cj = lax.broadcasted_iota(jnp.int32, (16, 16), 1)
    before = (cj < ci).astype(BF16)
    key = route * CAPACITY
    for owner in range(OWNERS):
        mine = (route == owner).astype(F32)
        mine16 = jnp.concatenate([mine, jnp.zeros((16 - chunks, LANES), F32)], axis=0).astype(BF16)
        upto_here = jnp.dot(mine16, upto, preferred_element_type=F32)
        totals = jnp.dot(mine16, ones, preferred_element_type=F32).astype(BF16)
        offset = jnp.dot(before, totals, preferred_element_type=F32)
        rank = (upto_here + offset)[:chunks] - 1.0
        key = key + jnp.where(route == owner, rank, 0.0).astype(jnp.int32)
    square = jnp.concatenate([blend, jnp.zeros((LANES - chunks, LANES), F32)], axis=0)
    columns = square.T
    for c in range(chunks):
        weighted = rows_ref[c * LANES : (c + 1) * LANES, :] * columns[:, c : c + 1]
        high, low = halves(weighted)
        split_ref[c * LANES : (c + 1) * LANES, :LANES] = high
        split_ref[c * LANES : (c + 1) * LANES, LANES:] = low
    first, second, third = thirds(blend)
    upper = line // 32
    parts = [first, second, third, upper.astype(BF16), (line - upper * 32).astype(BF16)]
    notes = jnp.concatenate(
        [
            jnp.concatenate(
                [p.astype(F32)[c : c + 1] for p in parts] + [jnp.zeros((3, LANES), F32)], axis=0
            )
            for c in range(chunks)
        ],
        axis=1,
    ).astype(BF16)
    for step, out_ref in enumerate(out_refs):
        owner = (rep_ref[0] + step) % OWNERS
        slot = lax.broadcasted_iota(jnp.int32, (CAPACITY, LANES), 0) + owner * CAPACITY
        for c in range(chunks):
            hot = jnp.where(slot == key[c : c + 1, :], 1.0, 0.0)
            hot_ref[:, c * LANES : (c + 1) * LANES] = hot.astype(BF16)
        hot = hot_ref[...]
        both = jnp.dot(hot, split_ref[...], preferred_element_type=F32)
        out_ref[:CAPACITY, :] = both[:, :LANES] + both[:, LANES:]
        meta = lax.dot_general(
            notes, hot, (((1,), (1,)), ((), ())), preferred_element_type=F32
        )
        weight = meta[0:1] + meta[1:2] + meta[2:3]
        where = meta[3:4] * 32.0 + meta[4:5]
        out_ref[CAPACITY:, :] = jnp.concatenate(
            [weight[:, q * LANES : (q + 1) * LANES] for q in range(4)]
            + [where[:, q * LANES : (q + 1) * LANES] for q in range(4)],
            axis=0,
        )


def observe(*refs):
    got_refs, (out_ref, hot_ref, plane_ref) = refs[:OWNERS], refs[OWNERS:]
    total = jnp.zeros((LINES, 2 * LANES), F32)
    weights = jnp.zeros((LINES, 8), F32)
    at = lax.broadcasted_iota(jnp.int32, (LINES, LANES), 0)
    for got_ref in got_refs:
        meta = got_ref[CAPACITY:, :]
        where = meta[4:8].astype(jnp.int32)
        for q in range(4):
            hot = jnp.where(at == where[q : q + 1, :], 1.0, 0.0)
            hot_ref[:, q * LANES : (q + 1) * LANES] = hot.astype(BF16)
        hot = hot_ref[...]
        high, low = halves(got_ref[:CAPACITY, :])
        total += jnp.dot(hot, jnp.concatenate([high, low], axis=1), preferred_element_type=F32)
        weight = jnp.concatenate([meta[q : q + 1] for q in range(4)], axis=1)
        parts = [p.astype(F32) for p in thirds(weight)]
        stacked = jnp.concatenate(parts + [jnp.zeros((5, CAPACITY), F32)], axis=0).astype(BF16)
        weights += lax.dot_general(
            hot, stacked, (((1,), (1,)), ((), ())), preferred_element_type=F32
        )
    weight_sum = weights[:, 0:1] + weights[:, 1:2] + weights[:, 2:3]
    plane_ref[...] = (total[:, :LANES] + total[:, LANES:]) / weight_sum
    store_tiles(plane_ref, out_ref)


def columns_from(got_ref, out_ref):
    for i in range(8):
        turned = got_ref[pl.ds(i, Z, stride=8), :].T
        for j in range(4):
            out_ref[SIDE * (8 * j + i) : SIDE * (8 * j + i) + SIDE, :] = turned[SIDE * j : SIDE * j + SIDE, :]


def store_ends(out_ref, first_ref, last_ref):
    first_ref[...] = out_ref[: RIM * SIDE, :]
    last_ref[...] = out_ref[(SIDE - RIM) * SIDE :, :]


def store_edges(side_ref, out_ref, cross_ref, pair_ref):
    skip = (SIDE - RIM) * SIDE
    cross_ref[...] = out_ref[pl.ds(pl.multiple_of(side_ref[0] * skip, 8), RIM * SIDE), :]
    pair_ref[...] = out_ref[pl.ds(pl.multiple_of((1 - side_ref[0]) * skip, 8), RIM * SIDE), :]


def arrive(got_ref, out_ref, swapped_ref, first_ref, last_ref):
    columns_from(got_ref, out_ref)
    for y in range(SIDE):
        swapped_ref[SIDE * y : SIDE * y + SIDE, :] = out_ref[pl.ds(y, SIDE, stride=SIDE), :]
    store_ends(swapped_ref, first_ref, last_ref)


def taps_of(taps_ref, flip):
    return [taps_ref[TAPS - 1 - k if flip else k] for k in range(TAPS)]


def own_share(flip, taps_ref, mid_ref, out_ref):
    taps = taps_of(taps_ref, flip)

    def block(index, carry):
        row = index * 8
        for lead in range(0, SIDE, 8):
            totals = [None] * 8
            for cell in range(max(0, lead - RIM), min(SIDE, lead + 8 + RIM)):
                value = mid_ref[pl.ds(pl.multiple_of(cell * SIDE + row, 8), 8), :]
                for i in range(8):
                    k = cell - lead - i + RIM
                    if 0 <= k < TAPS:
                        term = taps[k] * value
                        totals[i] = term if totals[i] is None else totals[i] + term
            for i in range(8):
                out_ref[pl.ds(pl.multiple_of((lead + i) * SIDE + row, 8), 8), :] = totals[i]
        return carry

    lax.fori_loop(0, SIDE // 8, block, 0)


def add_rims(taps_ref, flip, side, part_ref, near_ref, far_ref, store):
    taps = taps_of(taps_ref, flip)
    for row in range(0, SIDE, 8):
        near = [near_ref[SIDE * i + row : SIDE * i + row + 8, :] for i in range(RIM)]
        far = [far_ref[SIDE * i + row : SIDE * i + row + 8, :] for i in range(RIM)]
        if side is None:
            low, high = near, far
        else:
            low = [jnp.where(side == 0, a, b) for a, b in zip(near, far, strict=True)]
            high = [jnp.where(side == 0, b, a) for a, b in zip(near, far, strict=True)]
        for lead in range(SIDE):
            total = part_ref[SIDE * lead + row : SIDE * lead + row + 8, :]
            for i in range(RIM):
                if i >= lead:
                    total = total + taps[i - lead] * low[i]
                if i <= lead - SIDE + RIM:
                    total = total + taps[SIDE + RIM + i - lead] * high[i]
            store(lead, row, total)


def swapped(lead, row):
    return pl.ds(SIDE * row + lead, 8, stride=SIDE)


def along_x(flip, taps_ref, side_ref, part_ref, cross_ref, pair_ref, out_ref, first_ref, last_ref):
    def store(lead, row, value):
        out_ref[swapped(lead, row), :] = value

    add_rims(taps_ref, flip, side_ref[0], part_ref, cross_ref, pair_ref, store)
    store_ends(out_ref, first_ref, last_ref)


def along_y_first(taps_ref, side_ref, part_ref, low_ref, high_ref, out_ref, cross_ref, pair_ref):
    def store(lead, row, value):
        out_ref[swapped(lead, row), :] = value

    add_rims(taps_ref, False, None, part_ref, low_ref, high_ref, store)
    store_edges(side_ref, out_ref, cross_ref, pair_ref)


def axial(value, band, back):
    dims = (((1,), (0 if back else 1,)), ((), ()))
    high, low = halves(value)
    band_high, band_low = halves(band)
    double = jnp.concatenate([band_high, band_high], axis=0 if back else 1)
    both = jnp.concatenate([high, low], axis=1)
    return lax.dot_general(both, double, dims, preferred_element_type=F32) + lax.dot_general(
        high, band_low, dims, preferred_element_type=F32
    )


def blur_x_last(taps_ref, side_ref, part_ref, cross_ref, pair_ref, band_ref, out_ref, cols_ref):
    def store(lead, row, value):
        cols_ref[SIDE * lead + row : SIDE * lead + row + 8, :] = value

    add_rims(taps_ref, False, side_ref[0], part_ref, cross_ref, pair_ref, store)
    out_ref[...] = axial(cols_ref[...], band_ref[...], False)


def first_ratio(side_ref, got_ref, blurred_ref, band_ref, seen_ref, out_ref, cross_ref, pair_ref):
    columns_from(got_ref, seen_ref)
    out_ref[...] = axial(seen_ref[...] / blurred_ref[...], band_ref[...], True)
    store_edges(side_ref, out_ref, cross_ref, pair_ref)


def blur_ratio(
    taps_ref, side_ref, part_ref, low_ref, high_ref, band_ref, seen_ref, out_ref, cross_ref, pair_ref, cols_ref
):
    def store(lead, row, value):
        cols_ref[swapped(lead, row), :] = value

    add_rims(taps_ref, False, None, part_ref, low_ref, high_ref, store)
    band = band_ref[...]
    for start in range(0, SIDE * SIDE, 256):
        spot = slice(start, start + 256)
        ratio = seen_ref[spot, :] / axial(cols_ref[spot, :], band, False)
        out_ref[spot, :] = axial(ratio, band, True)
    store_edges(side_ref, out_ref, cross_ref, pair_ref)


def update(taps_ref, side_ref, part_ref, low_ref, high_ref, estimate_ref, out_ref, cross_ref, pair_ref):
    def store(lead, row, value):
        spot = swapped(lead, row)
        out_ref[spot, :] = estimate_ref[spot, :] * value

    add_rims(taps_ref, True, None, part_ref, low_ref, high_ref, store)
    store_edges(side_ref, out_ref, cross_ref, pair_ref)


def last_update(taps_ref, part_ref, low_ref, high_ref, estimate_ref, out_ref, cols_ref):
    def store(lead, row, value):
        cols_ref[swapped(lead, row), :] = value

    add_rims(taps_ref, True, None, part_ref, low_ref, high_ref, store)
    for i in range(8):
        spots = [slice(SIDE * (8 * j + i), SIDE * (8 * j + i) + SIDE) for j in range(4)]
        block = jnp.concatenate([estimate_ref[spot, :] * cols_ref[spot, :] for spot in spots], axis=0)
        out_ref[pl.ds(i, Z, stride=8), :] = block.T


FLAT = (SIDE * SIDE, Z)
EDGE = (RIM * SIDE, Z)
PIECES = (Z, 8, LANES)


def shards(camera_rows, blend, route, line, start, psf_xy, psf_z):
    slabs, reps = lax.axis_size("slab"), lax.axis_size("rep")
    x_tiles = LINES // SIDE
    y_tiles = slabs // x_tiles
    chunks = camera_rows.shape[0] // LANES
    pair_swaps = [(t, t ^ 1) for t in range(slabs)]
    cross_swaps = []
    for t in range(1, slabs, 2):
        if t % x_tiles != x_tiles - 1:
            cross_swaps += [(t, t + 1), (t + 1, t)]
    side = (lax.axis_index("slab") % 2).reshape(1)
    y_pairs = []
    for t in range(slabs):
        for r in range(reps):
            y = r * y_tiles + t // x_tiles + 1
            if y < y_tiles * reps:
                up = (y % y_tiles) * x_tiles + t % x_tiles
                y_pairs.append((t * reps + r, up * reps + y // y_tiles))

    def rims_x(cross, pair):
        return lax.ppermute(cross, "slab", cross_swaps), lax.ppermute(pair, "slab", pair_swaps)

    def rims_y(first, last):
        axes = ("slab", "rep")
        return lax.ppermute(last, axes, y_pairs), lax.ppermute(first, axes, [(b, a) for a, b in y_pairs])

    def turn(pieces):
        return lax.all_to_all(pieces, "slab", split_axis=0, concat_axis=0, tiled=True)

    taps = psf_xy / jnp.sum(psf_xy)

    arrived = turn(call(store_tiles, [PIECES], [], start.reshape(LINES, LANES))[0])
    band = call(axial_band, [(Z, LANES)], [((8, LANES), F32)], psf_z[None, :])[0]
    sent = call(
        pack_rows,
        [(CAPACITY + META, LANES)] * OWNERS,
        [((chunks * LANES, 2 * LANES), BF16), ((CAPACITY, chunks * LANES), BF16)],
        lax.axis_index("rep").reshape(1),
        camera_rows,
        blend.reshape(chunks, LANES),
        route.reshape(chunks, LANES),
        line.reshape(chunks, LANES),
        smem=1,
    )
    got = [
        block if step == 0 else lax.ppermute(block, "rep", [(r, (r + step) % reps) for r in range(reps)])
        for step, block in enumerate(sent)
    ]
    seen_pieces = call(observe, [PIECES], [((LINES, CAPACITY), BF16), ((LINES, LANES), F32)], *got)[0]
    arrived, seen_pieces = lax.optimization_barrier((arrived, seen_pieces))
    estimate, flipped, first, last = call(
        arrive, [FLAT, FLAT, EDGE, EDGE], [], arrived.reshape(Z * 8, LANES)
    )
    seen_arrived = turn(seen_pieces)
    own = functools.partial(call, functools.partial(own_share, False), [FLAT], [], taps, smem=1)
    own_back = functools.partial(call, functools.partial(own_share, True), [FLAT], [], taps, smem=1)

    def lateral(flip, part, rims):
        value, first, last = call(
            functools.partial(along_x, flip), [FLAT, EDGE, EDGE], [], taps, side, part, *rims, smem=2
        )
        rims = rims_y(first, last)
        return (own_back if flip else own)(value)[0], *rims

    value, *edges = call(
        along_y_first, [FLAT, EDGE, EDGE], [], taps, side, own(flipped)[0], *rims_y(first, last), smem=2
    )
    cols = [(FLAT, F32)]
    blurred = call(
        blur_x_last, [FLAT], cols, taps, side, own(value)[0], *rims_x(*edges), band, smem=2
    )[0]
    seen, back, *edges = call(
        first_ratio, [FLAT, FLAT, EDGE, EDGE], [], side, seen_arrived.reshape(Z * 8, LANES), blurred, band, smem=1
    )
    parts = lateral(True, own_back(back)[0], rims_x(*edges))
    estimate, *edges = call(update, [FLAT, EDGE, EDGE], [], taps, side, *parts, estimate, smem=2)
    parts = lateral(False, own(estimate)[0], rims_x(*edges))
    back, *edges = call(
        blur_ratio, [FLAT, EDGE, EDGE], cols, taps, side, *parts, band, seen, smem=2
    )
    parts = lateral(True, own_back(back)[0], rims_x(*edges))
    pieces = call(last_update, [(Z * 8, LANES)], cols, taps, *parts, estimate, smem=1)[0]
    done = turn(pieces.reshape(PIECES))
    plane = call(plane_of, [(LINES, LANES)], [], done)[0]
    return plane.reshape(1, LINES, LANES)


def solution(mesh):
    in_specs = (
        P(("slab", "rep"), None),
        P(("slab", "rep")),
        P(("slab", "rep")),
        P(("slab", "rep")),
        P("slab", None, "rep"),
        P(),
        P(),
    )
    out_specs = P("slab", None, "rep")
    return jax.shard_map(shards, mesh=mesh, in_specs=in_specs, out_specs=out_specs, check_vma=False)
```

time: 224 us -> 220 us (0.982)
  Pallas kernels: 38.3 us -> 32.7 us
    pallas_call x23, Pallas kernels: 38.3 us -> 32.7 us  [call(): pl.pallas_call(kernel, out_shape=outs, in_specs=specs, out_specs=tuple((p...]
  transfers between devices with their start and end apart: 21 -> 21, of which waited for: 16 -> 16; matrix products, arithmetic and copies ran while one was open for 1% -> 1% of each run, Pallas kernels for 11% -> 10%
where the time goes in v3:
time: 220 us
  starting transfers between devices  85.5 us (39%)
  waiting for transfers between devices  50.9 us (23%)
  blocking collectives  46.3 us (21%)
  Pallas kernels  32.7 us (15%)
  local copies, waits for them, and re-layouts  2.36 us (1%)
    all_to_all x1, blocking collectives, turn(): lax.all_to_all(pieces, 'slab', split_axis=0, concat_axis=0, tiled=True)  46.3 us
    pallas_call x23, Pallas kernels, call(): pl.pallas_call(kernel, out_shape=outs, in_specs=specs, out_specs=tuple((p...  32.7 us
    all_to_all x2, starting transfers between devices, turn(): lax.all_to_all(pieces, 'slab', split_axis=0, concat_axis=0, tiled=True)  32.1 us
    ppermute x4, waiting for transfers between devices, rims_y(): lax.ppermute(first, axes, [(b, a) for a, b in y_pairs])  16.8 us
    ppermute x4, starting transfers between devices, rims_x(): lax.ppermute(cross, 'slab', cross_swaps)  15.9 us
    ppermute x4, starting transfers between devices, rims_y(): lax.ppermute(last, axes, y_pairs)  14 us
    all_to_all x2, waiting for transfers between devices, turn(): lax.all_to_all(pieces, 'slab', split_axis=0, concat_axis=0, tiled=True)  11.6 us
    ppermute x3, starting transfers between devices, shards(): lax.ppermute(block, 'rep', [(r, (r + step) % reps) for r in range(reps)])  10.5 us
  transfers between devices with their start and end apart: 21, of which 16 were waited for; matrix products, arithmetic and copies ran while one was open for 1% of the time, Pallas kernels for 10%

profile of v3, /device:TPU:1, one launch (start us, length us, event | category | flops | bytes accessed | tf_op | source)
XLA Modules:
  0.0 219.6 jit_solution(15614408245269128423)
XLA Ops:
  0.0 1.0 copy-done.1
  1.0 1.2 store_tiles.1
  2.2 20.7 %all-to-all-start = ((f32[128,8,128]{2,1,0:T(8,128)}), f32[128,8,128]{2,1,0:T(8,128)S(1)}, u32[]{:S(2)}, u32[]{:S(2)}) async-start(f32[128,8,128]{2,1,0:T(8,128)} %store_tiles.1), calls=%async_computation | async-start | bytes 1048576 | tf_op jit(solution)/shard_map/all_to_all | solution.py:369
  23.0 0.7 copy-done.2
  23.6 3.8 %pack_rows.1 = (f32[520,128]{1,0:T(8,128)S(1)}, f32[520,128]{1,0:T(8,128)S(1)}, f32[520,128]{1,0:T(8,128)S(1)}, f32[520,128]{1,0:T(8,128)S(1)}) custom-call(s32[1]{0:T(128)} %bitcast.2.rep_ref, f32[1280,128]{1,0:T(8,128)S(1)} %copy-done, f32[10,128]{1,0:T(8,128)S(1)} %bitcast.15, s32[10,128]{1,0:T(8,128)S(1)} %bitcast.16, s32[10,128]{1,0:T(8,128)S(1)} %bitcast.17), custom_call_target="tpu_custom_call" | custom-call | tf_op jit(solution)/shard_map/pack_rows/pallas_call | solution.py:30
  27.4 3.1 %collective-permute-start = (f32[520,128]{1,0:T(8,128)S(1)}, f32[520,128]{1,0:T(8,128)S(1)}, u32[]{:S(2)}, u32[]{:S(2)}) collective-permute-start(f32[520,128]{1,0:T(8,128)S(1)} %get-tuple-element.38), channel_id=1, source_target_pairs={{0,1},{1,2},{2,3},{3,0},{4,5},{5,6},{6,7},{7,4},{8,9},{9,10},{10,1... | collective-permute-start | bytes 798728 | tf_op jit(solution)/shard_map/ppermute | solution.py:387
  30.6 4.4 %collective-permute-start.1 = (f32[520,128]{1,0:T(8,128)S(1)}, f32[520,128]{1,0:T(8,128)S(1)}, u32[]{:S(2)}, u32[]{:S(2)}) collective-permute-start(f32[520,128]{1,0:T(8,128)S(1)} %get-tuple-element.39), channel_id=1, source_target_pairs={{0,2},{1,3},{2,0},{3,1},{4,6},{5,7},{6,4},{7,5},{8,10},{9,11},{10,... | collective-permute-start | bytes 798728 | tf_op jit(solution)/shard_map/ppermute | solution.py:387
  34.9 3.1 %collective-permute-start.2 = (f32[520,128]{1,0:T(8,128)S(1)}, f32[520,128]{1,0:T(8,128)S(1)}, u32[]{:S(2)}, u32[]{:S(2)}) collective-permute-start(f32[520,128]{1,0:T(8,128)S(1)} %get-tuple-element.40), channel_id=1, source_target_pairs={{0,3},{1,0},{2,1},{3,2},{4,7},{5,4},{6,5},{7,6},{8,11},{9,8},{10,9... | collective-permute-start | bytes 798728 | tf_op jit(solution)/shard_map/ppermute | solution.py:387
  38.0 6.2 %collective-permute-done.1.refs_2_ = f32[520,128]{1,0:T(8,128)S(1)} collective-permute-done((f32[520,128]{1,0:T(8,128)S(1)}, f32[520,128]{1,0:T(8,128)S(1)}, u32[]{:S(2)}, u32[]{:S(2)}) %collective-permute-start.1) | collective-permute-done | bytes 266272 | tf_op jit(solution)/shard_map/ppermute | solution.py:387
  44.2 1.2 collective-permute-done.2.refs_3_
  45.5 4.1 %observe.1 = f32[128,8,128]{2,1,0:T(8,128)} custom-call(f32[520,128]{1,0:T(8,128)S(1)} %get-tuple-element.37.refs_0_, f32[520,128]{1,0:T(8,128)S(1)} %collective-permute-done.refs_1_, f32[520,128]{1,0:T(8,128)S(1)} %collective-permute-done.1.refs_2_, f32[520,128]{1,0:T(8,128)S(1)} %collective-permute-done.2.refs_3_), custom_call_target="tpu_custom_call" | custom-call | tf_op jit(solution)/shard_map/observe/pallas_call | solution.py:30
  49.6 6.6 %all-to-all-done = f32[128,8,128]{2,1,0:T(8,128)S(1)} async-done(((f32[128,8,128]{2,1,0:T(8,128)}), f32[128,8,128]{2,1,0:T(8,128)S(1)}, u32[]{:S(2)}, u32[]{:S(2)}) %all-to-all-start) | async-done | bytes 524320 | tf_op jit(solution)/shard_map/all_to_all | solution.py:369
  56.2 11.4 %all-to-all-start.1 = ((f32[128,8,128]{2,1,0:T(8,128)}), f32[128,8,128]{2,1,0:T(8,128)S(1)}, u32[]{:S(2)}, u32[]{:S(2)}) async-start(f32[128,8,128]{2,1,0:T(8,128)} %observe.1), calls=%async_computation.1 | async-start | bytes 1048576 | tf_op jit(solution)/shard_map/all_to_all | solution.py:369
  67.5 0.5 arrive.1
  68.1 3.4 %collective-permute-start.3 = (f32[480,128]{1,0:T(8,128)S(1)}, f32[480,128]{1,0:T(8,128)S(1)}, u32[]{:S(2)}, u32[]{:S(2)}) collective-permute-start(f32[480,128]{1,0:T(8,128)S(1)} %get-tuple-element.44), channel_id=1, source_target_pairs={{0,128},{1,129},{2,130},{3,131},{4,132},{5,133},{6,134},{7,135},{8... | collective-permute-start | bytes 737288 | tf_op jit(solution)/shard_map/ppermute | solution.py:366
  71.5 1.3 collective-permute-start.4
  72.8 0.6 copy-done.6
  73.4 0.7 reduce_sum.9
  74.1 0.7 broadcast_divide_fusion.taps_ref
  74.8 1.5 own_share.8.part_ref
  76.3 1.6 collective-permute-done.3.low_ref
  77.9 3.7 %collective-permute-done.4.high_ref = f32[480,128]{1,0:T(8,128)S(1)} collective-permute-done((f32[480,128]{1,0:T(8,128)S(1)}, f32[480,128]{1,0:T(8,128)S(1)}, u32[]{:S(2)}, u32[]{:S(2)}) %collective-permute-start.4) | collective-permute-done | bytes 245792 | tf_op jit(solution)/shard_map/ppermute | solution.py:366
  81.6 1.0 along_y_first.1
  82.6 4.7 %collective-permute-start.5 = (f32[480,128]{1,0:T(8,128)S(1)}, f32[480,128]{1,0:T(8,128)S(1)}, u32[]{:S(2)}, u32[]{:S(2)}) collective-permute-start(f32[480,128]{1,0:T(8,128)S(1)} %get-tuple-element.47), channel_id=1, source_target_pairs={{4,8},{8,4},{12,16},{16,12},{20,24},{24,20},{28,32},{32,28},{36,40... | collective-permute-start | bytes 737288 | tf_op jit(solution)/shard_map/ppermute | solution.py:362
  87.4 2.1 collective-permute-start.6
  89.7 1.5 own_share.9.part_ref
  91.1 3.5 %collective-permute-done.5.cross_ref = f32[480,128]{1,0:T(8,128)S(1)} collective-permute-done((f32[480,128]{1,0:T(8,128)S(1)}, f32[480,128]{1,0:T(8,128)S(1)}, u32[]{:S(2)}, u32[]{:S(2)}) %collective-permute-start.5) | collective-permute-done | bytes 245792 | tf_op jit(solution)/shard_map/ppermute | solution.py:362
  94.6 1.1 blur_x_last.1.blurred_ref
  95.7 5.0 %all-to-all-done.1 = f32[128,8,128]{2,1,0:T(8,128)S(1)} async-done(((f32[128,8,128]{2,1,0:T(8,128)}), f32[128,8,128]{2,1,0:T(8,128)S(1)}, u32[]{:S(2)}, u32[]{:S(2)}) %all-to-all-start.1) | async-done | bytes 524320 | tf_op jit(solution)/shard_map/all_to_all | solution.py:369
  100.7 0.5 first_ratio.1
  101.3 4.8 %collective-permute-start.7 = (f32[480,128]{1,0:T(8,128)S(1)}, f32[480,128]{1,0:T(8,128)S(1)}, u32[]{:S(2)}, u32[]{:S(2)}) collective-permute-start(f32[480,128]{1,0:T(8,128)S(1)} %get-tuple-element.50), channel_id=1, source_target_pairs={{4,8},{8,4},{12,16},{16,12},{20,24},{24,20},{28,32},{32,28},{36,40... | collective-permute-start | bytes 737288 | tf_op jit(solution)/shard_map/ppermute | solution.py:362
  106.1 1.9 collective-permute-start.8
  108.0 1.5 own_share.10.part_ref
  110.0 1.0 along_x.3
  111.0 1.9 collective-permute-start.9
  112.9 1.3 collective-permute-start.10
  114.2 1.5 own_share.11.part_ref
  115.7 2.5 %collective-permute-done.9.low_ref = f32[480,128]{1,0:T(8,128)S(1)} collective-permute-done((f32[480,128]{1,0:T(8,128)S(1)}, f32[480,128]{1,0:T(8,128)S(1)}, u32[]{:S(2)}, u32[]{:S(2)}) %collective-permute-start.9) | collective-permute-done | bytes 245792 | tf_op jit(solution)/shard_map/ppermute | solution.py:366
  118.2 3.8 %collective-permute-done.10.high_ref = f32[480,128]{1,0:T(8,128)S(1)} collective-permute-done((f32[480,128]{1,0:T(8,128)S(1)}, f32[480,128]{1,0:T(8,128)S(1)}, u32[]{:S(2)}, u32[]{:S(2)}) %collective-permute-start.10) | collective-permute-done | bytes 245792 | tf_op jit(solution)/shard_map/ppermute | solution.py:366
  122.0 1.3 update.1
  123.3 3.5 %collective-permute-start.11 = (f32[480,128]{1,0:T(8,128)S(1)}, f32[480,128]{1,0:T(8,128)S(1)}, u32[]{:S(2)}, u32[]{:S(2)}) collective-permute-start(f32[480,128]{1,0:T(8,128)S(1)} %get-tuple-element.57), channel_id=1, source_target_pairs={{4,8},{8,4},{12,16},{16,12},{20,24},{24,20},{28,32},{32,28},{36,40... | collective-permute-start | bytes 737288 | tf_op jit(solution)/shard_map/ppermute | solution.py:362
  126.8 1.9 collective-permute-start.12
  128.7 1.5 own_share.12.part_ref
  130.2 0.6 collective-permute-done.11.cross_ref
  130.8 1.0 along_x.4
  131.8 3.0 %collective-permute-start.13 = (f32[480,128]{1,0:T(8,128)S(1)}, f32[480,128]{1,0:T(8,128)S(1)}, u32[]{:S(2)}, u32[]{:S(2)}) collective-permute-start(f32[480,128]{1,0:T(8,128)S(1)} %get-tuple-element.60), channel_id=1, source_target_pairs={{0,128},{1,129},{2,130},{3,131},{4,132},{5,133},{6,134},{7,135},{8... | collective-permute-start | bytes 737288 | tf_op jit(solution)/shard_map/ppermute | solution.py:366
  134.9 1.3 collective-permute-start.14
  136.2 1.5 own_share.13.part_ref
  137.6 2.7 %collective-permute-done.13.low_ref = f32[480,128]{1,0:T(8,128)S(1)} collective-permute-done((f32[480,128]{1,0:T(8,128)S(1)}, f32[480,128]{1,0:T(8,128)S(1)}, u32[]{:S(2)}, u32[]{:S(2)}) %collective-permute-start.13) | collective-permute-done | bytes 245792 | tf_op jit(solution)/shard_map/ppermute | solution.py:366
  140.3 5.2 %collective-permute-done.14.high_ref = f32[480,128]{1,0:T(8,128)S(1)} collective-permute-done((f32[480,128]{1,0:T(8,128)S(1)}, f32[480,128]{1,0:T(8,128)S(1)}, u32[]{:S(2)}, u32[]{:S(2)}) %collective-permute-start.14) | collective-permute-done | bytes 245792 | tf_op jit(solution)/shard_map/ppermute | solution.py:366
  145.5 1.6 blur_ratio.1
  147.2 2.9 %collective-permute-start.15 = (f32[480,128]{1,0:T(8,128)S(1)}, f32[480,128]{1,0:T(8,128)S(1)}, u32[]{:S(2)}, u32[]{:S(2)}) collective-permute-start(f32[480,128]{1,0:T(8,128)S(1)} %get-tuple-element.64), channel_id=1, source_target_pairs={{4,8},{8,4},{12,16},{16,12},{20,24},{24,20},{28,32},{32,28},{36,40... | collective-permute-start | bytes 737288 | tf_op jit(solution)/shard_map/ppermute | solution.py:362
  150.1 1.9 collective-permute-start.16
  152.0 1.5 own_share.14.part_ref
  153.5 1.2 collective-permute-done.15.cross_ref
  154.7 1.0 along_x.5
  155.7 5.7 %collective-permute-start.17 = (f32[480,128]{1,0:T(8,128)S(1)}, f32[480,128]{1,0:T(8,128)S(1)}, u32[]{:S(2)}, u32[]{:S(2)}) collective-permute-start(f32[480,128]{1,0:T(8,128)S(1)} %get-tuple-element.67), channel_id=1, source_target_pairs={{0,128},{1,129},{2,130},{3,131},{4,132},{5,133},{6,134},{7,135},{8... | collective-permute-start | bytes 737288 | tf_op jit(solution)/shard_map/ppermute | solution.py:366
  161.4 1.3 collective-permute-start.18
  162.7 1.5 own_share.15.part_ref
  164.2 2.6 %collective-permute-done.17.low_ref = f32[480,128]{1,0:T(8,128)S(1)} collective-permute-done((f32[480,128]{1,0:T(8,128)S(1)}, f32[480,128]{1,0:T(8,128)S(1)}, u32[]{:S(2)}, u32[]{:S(2)}) %collective-permute-start.17) | collective-permute-done | bytes 245792 | tf_op jit(solution)/shard_map/ppermute | solution.py:366
  166.7 4.1 %collective-permute-done.18.high_ref = f32[480,128]{1,0:T(8,128)S(1)} collective-permute-done((f32[480,128]{1,0:T(8,128)S(1)}, f32[480,128]{1,0:T(8,128)S(1)}, u32[]{:S(2)}, u32[]{:S(2)}) %collective-permute-start.18) | collective-permute-done | bytes 245792 | tf_op jit(solution)/shard_map/ppermute | solution.py:366
  170.9 1.2 last_update.1
  172.1 46.3 %all_to_all.15.got_ref = f32[128,8,128]{2,1,0:T(8,128)S(1)} all-to-all(f32[128,8,128]{2,1,0:T(8,128)S(1)} %bitcast.11), channel_id=1, replica_groups=mesh['slab'=128,'rep'=4] {'slab'}, dimensions={0} | all-to-all | bytes 1048576 | tf_op jit(solution)/shard_map/all_to_all | solution.py:369
  218.4 1.2 plane_of.1
  (18 shorter events, 0.7 us)
Async XLA Ops:
  0.0 1.0 copy-start.1
  2.2 20.7 %copy-start = (f32[1280,128]{1,0:T(8,128)S(1)}, f32[1280,128]{1,0:T(8,128)}, u32[]{:S(2)}) copy-start(f32[1280,128]{1,0:T(8,128)} %rows_ref.1) | copy-start | bytes 1966084
  2.2 20.7 %copy-start.3 = (s32[1280]{0:T(1024)S(1)}, s32[1280]{0:T(1024)}, u32[]{:S(2)}) copy-start(s32[1280]{0:T(1024)} %param.9) | copy-start | bytes 15364
  2.2 20.7 %copy-start.4 = (s32[1280]{0:T(1024)S(1)}, s32[1280]{0:T(1024)}, u32[]{:S(2)}) copy-start(s32[1280]{0:T(1024)} %param.10) | copy-start | bytes 15364
  2.2 53.9 %all-to-all-start = ((f32[128,8,128]{2,1,0:T(8,128)}), f32[128,8,128]{2,1,0:T(8,128)S(1)}, u32[]{:S(2)}, u32[]{:S(2)}) async-start(f32[128,8,128]{2,1,0:T(8,128)} %store_tiles.1), calls=%async_computation | async-start | bytes 1048576 | tf_op jit(solution)/shard_map/all_to_all | solution.py:369
  22.9 0.7 copy-start.2
  27.4 10.6 %collective-permute-start = (f32[520,128]{1,0:T(8,128)S(1)}, f32[520,128]{1,0:T(8,128)S(1)}, u32[]{:S(2)}, u32[]{:S(2)}) collective-permute-start(f32[520,128]{1,0:T(8,128)S(1)} %get-tuple-element.38), channel_id=1, source_target_pairs={{0,1},{1,2},{2,3},{3,0},{4,5},{5,6},{6,7},{7,4},{8,9},{9,10},{10,1... | collective-permute-start | bytes 798728 | tf_op jit(solution)/shard_map/ppermute | solution.py:387
  30.6 13.7 %collective-permute-start.1 = (f32[520,128]{1,0:T(8,128)S(1)}, f32[520,128]{1,0:T(8,128)S(1)}, u32[]{:S(2)}, u32[]{:S(2)}) collective-permute-start(f32[520,128]{1,0:T(8,128)S(1)} %get-tuple-element.39), channel_id=1, source_target_pairs={{0,2},{1,3},{2,0},{3,1},{4,6},{5,7},{6,4},{7,5},{8,10},{9,11},{10,... | collective-permute-start | bytes 798728 | tf_op jit(solution)/shard_map/ppermute | solution.py:387
  34.9 10.5 %collective-permute-start.2 = (f32[520,128]{1,0:T(8,128)S(1)}, f32[520,128]{1,0:T(8,128)S(1)}, u32[]{:S(2)}, u32[]{:S(2)}) collective-permute-start(f32[520,128]{1,0:T(8,128)S(1)} %get-tuple-element.40), channel_id=1, source_target_pairs={{0,3},{1,0},{2,1},{3,2},{4,7},{5,4},{6,5},{7,6},{8,11},{9,8},{10,9... | collective-permute-start | bytes 798728 | tf_op jit(solution)/shard_map/ppermute | solution.py:387
  56.2 44.6 %all-to-all-start.1 = ((f32[128,8,128]{2,1,0:T(8,128)}), f32[128,8,128]{2,1,0:T(8,128)S(1)}, u32[]{:S(2)}, u32[]{:S(2)}) async-start(f32[128,8,128]{2,1,0:T(8,128)} %observe.1), calls=%async_computation.1 | async-start | bytes 1048576 | tf_op jit(solution)/shard_map/all_to_all | solution.py:369
  68.1 9.8 %collective-permute-start.3 = (f32[480,128]{1,0:T(8,128)S(1)}, f32[480,128]{1,0:T(8,128)S(1)}, u32[]{:S(2)}, u32[]{:S(2)}) collective-permute-start(f32[480,128]{1,0:T(8,128)S(1)} %get-tuple-element.44), channel_id=1, source_target_pairs={{0,128},{1,129},{2,130},{3,131},{4,132},{5,133},{6,134},{7,135},{8... | collective-permute-start | bytes 737288 | tf_op jit(solution)/shard_map/ppermute | solution.py:366
  71.5 10.1 %collective-permute-start.4 = (f32[480,128]{1,0:T(8,128)S(1)}, f32[480,128]{1,0:T(8,128)S(1)}, u32[]{:S(2)}, u32[]{:S(2)}) collective-permute-start(f32[480,128]{1,0:T(8,128)S(1)} %get-tuple-element.45), channel_id=1, source_target_pairs={{128,0},{129,1},{130,2},{131,3},{132,4},{133,5},{134,6},{135,7},{1... | collective-permute-start | bytes 737288 | tf_op jit(solution)/shard_map/ppermute | solution.py:366
  72.8 0.7 copy-start.6
  82.6 12.0 %collective-permute-start.5 = (f32[480,128]{1,0:T(8,128)S(1)}, f32[480,128]{1,0:T(8,128)S(1)}, u32[]{:S(2)}, u32[]{:S(2)}) collective-permute-start(f32[480,128]{1,0:T(8,128)S(1)} %get-tuple-element.47), channel_id=1, source_target_pairs={{4,8},{8,4},{12,16},{16,12},{20,24},{24,20},{28,32},{32,28},{36,40... | collective-permute-start | bytes 737288 | tf_op jit(solution)/shard_map/ppermute | solution.py:362
  87.3 2.1 copy-start.5
  87.4 7.2 %collective-permute-start.6 = (f32[480,128]{1,0:T(8,128)S(1)}, f32[480,128]{1,0:T(8,128)S(1)}, u32[]{:S(2)}, u32[]{:S(2)}) collective-permute-start(f32[480,128]{1,0:T(8,128)S(1)} %get-tuple-element.48), channel_id=1, source_target_pairs={{0,4},{4,0},{8,12},{12,8},{16,20},{20,16},{24,28},{28,24},{32,36},... | collective-permute-start | bytes 737288 | tf_op jit(solution)/shard_map/ppermute | solution.py:362
  101.3 8.7 %collective-permute-start.7 = (f32[480,128]{1,0:T(8,128)S(1)}, f32[480,128]{1,0:T(8,128)S(1)}, u32[]{:S(2)}, u32[]{:S(2)}) collective-permute-start(f32[480,128]{1,0:T(8,128)S(1)} %get-tuple-element.50), channel_id=1, source_target_pairs={{4,8},{8,4},{12,16},{16,12},{20,24},{24,20},{28,32},{32,28},{36,40... | collective-permute-start | bytes 737288 | tf_op jit(solution)/shard_map/ppermute | solution.py:362
  106.1 3.9 %collective-permute-start.8 = (f32[480,128]{1,0:T(8,128)S(1)}, f32[480,128]{1,0:T(8,128)S(1)}, u32[]{:S(2)}, u32[]{:S(2)}) collective-permute-start(f32[480,128]{1,0:T(8,128)S(1)} %get-tuple-element.51), channel_id=1, source_target_pairs={{0,4},{4,0},{8,12},{12,8},{16,20},{20,16},{24,28},{28,24},{32,36},... | collective-permute-start | bytes 737288 | tf_op jit(solution)/shard_map/ppermute | solution.py:362
  111.0 7.2 %collective-permute-start.9 = (f32[480,128]{1,0:T(8,128)S(1)}, f32[480,128]{1,0:T(8,128)S(1)}, u32[]{:S(2)}, u32[]{:S(2)}) collective-permute-start(f32[480,128]{1,0:T(8,128)S(1)} %get-tuple-element.53), channel_id=1, source_target_pairs={{0,128},{1,129},{2,130},{3,131},{4,132},{5,133},{6,134},{7,135},{8... | collective-permute-start | bytes 737288 | tf_op jit(solution)/shard_map/ppermute | solution.py:366
  112.9 9.1 %collective-permute-start.10 = (f32[480,128]{1,0:T(8,128)S(1)}, f32[480,128]{1,0:T(8,128)S(1)}, u32[]{:S(2)}, u32[]{:S(2)}) collective-permute-start(f32[480,128]{1,0:T(8,128)S(1)} %get-tuple-element.54), channel_id=1, source_target_pairs={{128,0},{129,1},{130,2},{131,3},{132,4},{133,5},{134,6},{135,7},{1... | collective-permute-start | bytes 737288 | tf_op jit(solution)/shard_map/ppermute | solution.py:366
  123.3 7.5 %collective-permute-start.11 = (f32[480,128]{1,0:T(8,128)S(1)}, f32[480,128]{1,0:T(8,128)S(1)}, u32[]{:S(2)}, u32[]{:S(2)}) collective-permute-start(f32[480,128]{1,0:T(8,128)S(1)} %get-tuple-element.57), channel_id=1, source_target_pairs={{4,8},{8,4},{12,16},{16,12},{20,24},{24,20},{28,32},{32,28},{36,40... | collective-permute-start | bytes 737288 | tf_op jit(solution)/shard_map/ppermute | solution.py:362
  126.8 4.0 %collective-permute-start.12 = (f32[480,128]{1,0:T(8,128)S(1)}, f32[480,128]{1,0:T(8,128)S(1)}, u32[]{:S(2)}, u32[]{:S(2)}) collective-permute-start(f32[480,128]{1,0:T(8,128)S(1)} %get-tuple-element.58), channel_id=1, source_target_pairs={{0,4},{4,0},{8,12},{12,8},{16,20},{20,16},{24,28},{28,24},{32,36},... | collective-permute-start | bytes 737288 | tf_op jit(solution)/shard_map/ppermute | solution.py:362
  131.8 8.5 %collective-permute-start.13 = (f32[480,128]{1,0:T(8,128)S(1)}, f32[480,128]{1,0:T(8,128)S(1)}, u32[]{:S(2)}, u32[]{:S(2)}) collective-permute-start(f32[480,128]{1,0:T(8,128)S(1)} %get-tuple-element.60), channel_id=1, source_target_pairs={{0,128},{1,129},{2,130},{3,131},{4,132},{5,133},{6,134},{7,135},{8... | collective-permute-start | bytes 737288 | tf_op jit(solution)/shard_map/ppermute | solution.py:366
  134.9 10.7 %collective-permute-start.14 = (f32[480,128]{1,0:T(8,128)S(1)}, f32[480,128]{1,0:T(8,128)S(1)}, u32[]{:S(2)}, u32[]{:S(2)}) collective-permute-start(f32[480,128]{1,0:T(8,128)S(1)} %get-tuple-element.61), channel_id=1, source_target_pairs={{128,0},{129,1},{130,2},{131,3},{132,4},{133,5},{134,6},{135,7},{1... | collective-permute-start | bytes 737288 | tf_op jit(solution)/shard_map/ppermute | solution.py:366
  147.2 7.5 %collective-permute-start.15 = (f32[480,128]{1,0:T(8,128)S(1)}, f32[480,128]{1,0:T(8,128)S(1)}, u32[]{:S(2)}, u32[]{:S(2)}) collective-permute-start(f32[480,128]{1,0:T(8,128)S(1)} %get-tuple-element.64), channel_id=1, source_target_pairs={{4,8},{8,4},{12,16},{16,12},{20,24},{24,20},{28,32},{32,28},{36,40... | collective-permute-start | bytes 737288 | tf_op jit(solution)/shard_map/ppermute | solution.py:362
  150.1 4.6 %collective-permute-start.16 = (f32[480,128]{1,0:T(8,128)S(1)}, f32[480,128]{1,0:T(8,128)S(1)}, u32[]{:S(2)}, u32[]{:S(2)}) collective-permute-start(f32[480,128]{1,0:T(8,128)S(1)} %get-tuple-element.65), channel_id=1, source_target_pairs={{0,4},{4,0},{8,12},{12,8},{16,20},{20,16},{24,28},{28,24},{32,36},... | collective-permute-start | bytes 737288 | tf_op jit(solution)/shard_map/ppermute | solution.py:362
  155.7 11.0 %collective-permute-start.17 = (f32[480,128]{1,0:T(8,128)S(1)}, f32[480,128]{1,0:T(8,128)S(1)}, u32[]{:S(2)}, u32[]{:S(2)}) collective-permute-start(f32[480,128]{1,0:T(8,128)S(1)} %get-tuple-element.67), channel_id=1, source_target_pairs={{0,128},{1,129},{2,130},{3,131},{4,132},{5,133},{6,134},{7,135},{8... | collective-permute-start | bytes 737288 | tf_op jit(solution)/shard_map/ppermute | solution.py:366
  161.4 9.4 %collective-permute-start.18 = (f32[480,128]{1,0:T(8,128)S(1)}, f32[480,128]{1,0:T(8,128)S(1)}, u32[]{:S(2)}, u32[]{:S(2)}) collective-permute-start(f32[480,128]{1,0:T(8,128)S(1)} %get-tuple-element.68), channel_id=1, source_target_pairs={{128,0},{129,1},{130,2},{131,3},{132,4},{133,5},{134,6},{135,7},{1... | collective-permute-start | bytes 737288 | tf_op jit(solution)/shard_map/ppermute | solution.py:366

commit v4 on v3

--- a/solution.py
+++ b/solution.py
@@ -13,6 +13,8 @@
 SIDE = 32
 TAPS = 31
 RIM = TAPS // 2
+WIDE = 64
+MARGIN = 16
 OWNERS = 4
 CAPACITY = 512
 META = 8
@@ -191,61 +193,63 @@
             out_ref[SIDE * (8 * j + i) : SIDE * (8 * j + i) + SIDE, :] = turned[SIDE * j : SIDE * j + SIDE, :]
 
 
-def store_ends(out_ref, first_ref, last_ref):
-    first_ref[...] = out_ref[: RIM * SIDE, :]
-    last_ref[...] = out_ref[(SIDE - RIM) * SIDE :, :]
-
-
-def store_edges(side_ref, out_ref, cross_ref, pair_ref):
-    skip = (SIDE - RIM) * SIDE
-    cross_ref[...] = out_ref[pl.ds(pl.multiple_of(side_ref[0] * skip, 8), RIM * SIDE), :]
-    pair_ref[...] = out_ref[pl.ds(pl.multiple_of((1 - side_ref[0]) * skip, 8), RIM * SIDE), :]
-
-
-def arrive(got_ref, out_ref, swapped_ref, first_ref, last_ref):
+def store_edges(side_ref, out_ref, own_ref, other_ref, rows=SIDE, rim=RIM):
+    skip = (SIDE - rim) * rows
+    own_ref[...] = out_ref[pl.ds(pl.multiple_of(side_ref[0] * skip, 8), rim * rows), :]
+    other_ref[...] = out_ref[pl.ds(pl.multiple_of((1 - side_ref[0]) * skip, 8), rim * rows), :]
+
+
+def swap_leading(in_ref, out_ref):
+    for i in range(SIDE):
+        out_ref[SIDE * i : SIDE * i + SIDE, :] = in_ref[pl.ds(i, SIDE, stride=SIDE), :]
+
+
+def arrive(side_ref, got_ref, out_ref, swapped_ref, own_ref, other_ref):
     columns_from(got_ref, out_ref)
-    for y in range(SIDE):
-        swapped_ref[SIDE * y : SIDE * y + SIDE, :] = out_ref[pl.ds(y, SIDE, stride=SIDE), :]
-    store_ends(swapped_ref, first_ref, last_ref)
+    swap_leading(out_ref, swapped_ref)
+    store_edges(side_ref, swapped_ref, own_ref, other_ref)
 
 
 def taps_of(taps_ref, flip):
     return [taps_ref[TAPS - 1 - k if flip else k] for k in range(TAPS)]
 
 
-def own_share(flip, taps_ref, mid_ref, out_ref):
-    taps = taps_of(taps_ref, flip)
-
+def correlate(taps, in_ref, cells, leads, rows, shift, store):
     def block(index, carry):
         row = index * 8
-        for lead in range(0, SIDE, 8):
+        for first in range(0, leads, 8):
             totals = [None] * 8
-            for cell in range(max(0, lead - RIM), min(SIDE, lead + 8 + RIM)):
-                value = mid_ref[pl.ds(pl.multiple_of(cell * SIDE + row, 8), 8), :]
+            for cell in range(max(0, first - shift), min(cells, first + 7 + TAPS - shift)):
+                value = in_ref[pl.ds(pl.multiple_of(cell * rows + row, 8), 8), :]
                 for i in range(8):
-                    k = cell - lead - i + RIM
+                    k = cell - first - i + shift
                     if 0 <= k < TAPS:
                         term = taps[k] * value
                         totals[i] = term if totals[i] is None else totals[i] + term
             for i in range(8):
-                out_ref[pl.ds(pl.multiple_of((lead + i) * SIDE + row, 8), 8), :] = totals[i]
+                store(first + i, row, jnp.zeros((8, Z), F32) if totals[i] is None else totals[i])
         return carry
 
-    lax.fori_loop(0, SIDE // 8, block, 0)
-
-
-def add_rims(taps_ref, flip, side, part_ref, near_ref, far_ref, store):
+    lax.fori_loop(0, rows // 8, block, 0)
+
+
+def own_share(flip, leads, rows, shift, taps_ref, mid_ref, out_ref):
+    def store(lead, row, value):
+        out_ref[pl.ds(pl.multiple_of(lead * rows + row, 8), 8), :] = value
+
+    correlate(taps_of(taps_ref, flip), mid_ref, SIDE, leads, rows, shift, store)
+
+
+def add_rims(taps_ref, flip, side_ref, part_ref, near_ref, far_ref, store, rows=SIDE):
     taps = taps_of(taps_ref, flip)
-    for row in range(0, SIDE, 8):
-        near = [near_ref[SIDE * i + row : SIDE * i + row + 8, :] for i in range(RIM)]
-        far = [far_ref[SIDE * i + row : SIDE * i + row + 8, :] for i in range(RIM)]
-        if side is None:
-            low, high = near, far
-        else:
-            low = [jnp.where(side == 0, a, b) for a, b in zip(near, far, strict=True)]
-            high = [jnp.where(side == 0, b, a) for a, b in zip(near, far, strict=True)]
+    side = side_ref[0]
+    for row in range(0, rows, 8):
+        near = [near_ref[rows * i + row : rows * i + row + 8, :] for i in range(RIM)]
+        far = [far_ref[rows * i + row : rows * i + row + 8, :] for i in range(RIM)]
+        low = [jnp.where(side == 0, a, b) for a, b in zip(near, far, strict=True)]
+        high = [jnp.where(side == 0, b, a) for a, b in zip(near, far, strict=True)]
         for lead in range(SIDE):
-            total = part_ref[SIDE * lead + row : SIDE * lead + row + 8, :]
+            total = part_ref[rows * lead + row : rows * lead + row + 8, :]
             for i in range(RIM):
                 if i >= lead:
                     total = total + taps[i - lead] * low[i]
@@ -258,20 +262,99 @@
     return pl.ds(SIDE * row + lead, 8, stride=SIDE)
 
 
-def along_x(flip, taps_ref, side_ref, part_ref, cross_ref, pair_ref, out_ref, first_ref, last_ref):
+def along_x(taps_ref, side_ref, part_ref, cross_ref, pair_ref, out_ref, own_ref, other_ref):
     def store(lead, row, value):
         out_ref[swapped(lead, row), :] = value
 
-    add_rims(taps_ref, flip, side_ref[0], part_ref, cross_ref, pair_ref, store)
-    store_ends(out_ref, first_ref, last_ref)
-
-
-def along_y_first(taps_ref, side_ref, part_ref, low_ref, high_ref, out_ref, cross_ref, pair_ref):
+    add_rims(taps_ref, True, side_ref, part_ref, cross_ref, pair_ref, store)
+    store_edges(side_ref, out_ref, own_ref, other_ref)
+
+
+def along_y_first(taps_ref, side_ref, part_ref, near_ref, far_ref, out_ref, cross_ref, pair_ref):
     def store(lead, row, value):
         out_ref[swapped(lead, row), :] = value
 
-    add_rims(taps_ref, False, None, part_ref, low_ref, high_ref, store)
+    add_rims(taps_ref, False, side_ref, part_ref, near_ref, far_ref, store)
     store_edges(side_ref, out_ref, cross_ref, pair_ref)
+
+
+def extend(side_ref, tile_ref, near_ref, far_ref, out_ref):
+    zeros = jnp.zeros((8, Z), F32)
+    for x in range(SIDE):
+        out_ref[WIDE * x : WIDE * x + 8, :] = zeros
+        out_ref[WIDE * x + WIDE - 8 : WIDE * x + WIDE, :] = zeros
+        out_ref[WIDE * x + MARGIN : WIDE * x + MARGIN + SIDE, :] = tile_ref[SIDE * x : SIDE * x + SIDE, :]
+    for r in range(RIM):
+        for x in range(0, SIDE, 8):
+            near = near_ref[SIDE * r + x : SIDE * r + x + 8, :]
+            far = far_ref[SIDE * r + x : SIDE * r + x + 8, :]
+            below = pl.ds(WIDE * x + r + 1, 8, stride=WIDE)
+            above = pl.ds(WIDE * x + MARGIN + SIDE + r, 8, stride=WIDE)
+            out_ref[below, :] = jnp.where(side_ref[0] == 0, near, far)
+            out_ref[above, :] = jnp.where(side_ref[0] == 0, far, near)
+
+
+def rim_share(taps, upper, rim_ref, row):
+    cells = [rim_ref[SIDE * i + row : SIDE * i + row + 8, :] for i in range(2 * RIM)]
+    for n in range(2 * RIM):
+        used = range(n + 1) if upper else range(n, 2 * RIM)
+        total = None
+        for i in used:
+            term = taps[2 * RIM + i - n if upper else i - n] * cells[i]
+            total = term if total is None else total + term
+        yield n, total
+
+
+def near_share(taps_ref, side_ref, near_ref, out_ref):
+    taps = taps_of(taps_ref, True)
+    for side in range(2):
+
+        @pl.when(side_ref[0] == side)
+        def _():
+            for row in range(0, SIDE, 8):
+                for n, total in rim_share(taps, side == 1, near_ref, row):
+                    out_ref[SIDE * n + row : SIDE * n + row + 8, :] = total
+
+
+def wide_rows(taps_ref, side_ref, part_ref, near_ref, far_ref, out_ref, cross_ref, pair_ref):
+    taps = taps_of(taps_ref, True)
+    for side in range(2):
+
+        @pl.when(side_ref[0] == side)
+        def _():
+            for row in range(0, SIDE, 8):
+
+                def store(e, total):
+                    out_ref[pl.ds(WIDE * row + e, 8, stride=WIDE), :] = (
+                        part_ref[SIDE * e + row : SIDE * e + row + 8, :] + total
+                    )
+
+                for n, total in rim_share(taps, side == 0, far_ref, row):
+                    share = near_ref[SIDE * n + row : SIDE * n + row + 8, :]
+                    store(1 + n, share if side == 0 else total)
+                    store(SIDE + 1 + n, total if side == 0 else share)
+                for e in (0, SIDE - 1, SIDE, WIDE - 1):
+                    store(e, 0.0)
+
+    store_edges(side_ref, out_ref, cross_ref, pair_ref, WIDE)
+
+
+def update_wide(
+    taps_ref, side_ref, part_ref, cross_ref, pair_ref, start_ref, new_ref, out_ref, own_ref, other_ref, turned_ref
+):
+    def store(x, e, value):
+        spot = slice(WIDE * x + e, WIDE * x + e + 8)
+        new = start_ref[spot, :] * value
+        new_ref[spot, :] = new
+        turned_ref[pl.ds(SIDE * e + x, 8, stride=SIDE), :] = new
+
+    add_rims(taps_ref, True, side_ref, part_ref, cross_ref, pair_ref, store, WIDE)
+
+    def store_y(y, x, value):
+        out_ref[swapped(y, x), :] = value
+
+    correlate(taps_of(taps_ref, False), turned_ref, WIDE, SIDE, SIDE, RIM - MARGIN, store_y)
+    store_edges(side_ref, out_ref, own_ref, other_ref)
 
 
 def axial(value, band, back):
@@ -285,57 +368,59 @@
     )
 
 
-def blur_x_last(taps_ref, side_ref, part_ref, cross_ref, pair_ref, band_ref, out_ref, cols_ref):
+def along_x_last(taps_ref, side_ref, part_ref, cross_ref, pair_ref, cols_ref):
     def store(lead, row, value):
         cols_ref[SIDE * lead + row : SIDE * lead + row + 8, :] = value
 
-    add_rims(taps_ref, False, side_ref[0], part_ref, cross_ref, pair_ref, store)
+    add_rims(taps_ref, False, side_ref, part_ref, cross_ref, pair_ref, store)
+
+
+def blur(taps_ref, side_ref, part_ref, cross_ref, pair_ref, band_ref, out_ref, cols_ref):
+    along_x_last(taps_ref, side_ref, part_ref, cross_ref, pair_ref, cols_ref)
     out_ref[...] = axial(cols_ref[...], band_ref[...], False)
 
 
-def first_ratio(side_ref, got_ref, blurred_ref, band_ref, seen_ref, out_ref, cross_ref, pair_ref):
+def first_ratio(side_ref, got_ref, blurred_ref, band_ref, seen_ref, out_ref, own_ref, other_ref, cols_ref):
     columns_from(got_ref, seen_ref)
-    out_ref[...] = axial(seen_ref[...] / blurred_ref[...], band_ref[...], True)
-    store_edges(side_ref, out_ref, cross_ref, pair_ref)
+    cols_ref[...] = axial(seen_ref[...] / blurred_ref[...], band_ref[...], True)
+    swap_leading(cols_ref, out_ref)
+    store_edges(side_ref, out_ref, own_ref, other_ref, rim=2 * RIM)
 
 
 def blur_ratio(
-    taps_ref, side_ref, part_ref, low_ref, high_ref, band_ref, seen_ref, out_ref, cross_ref, pair_ref, cols_ref
+    taps_ref, side_ref, part_ref, cross_ref, pair_ref, band_ref, seen_ref, out_ref, own_ref, other_ref, cols_ref
 ):
-    def store(lead, row, value):
-        cols_ref[swapped(lead, row), :] = value
-
-    add_rims(taps_ref, False, None, part_ref, low_ref, high_ref, store)
+    along_x_last(taps_ref, side_ref, part_ref, cross_ref, pair_ref, cols_ref)
     band = band_ref[...]
     for start in range(0, SIDE * SIDE, 256):
         spot = slice(start, start + 256)
         ratio = seen_ref[spot, :] / axial(cols_ref[spot, :], band, False)
         out_ref[spot, :] = axial(ratio, band, True)
-    store_edges(side_ref, out_ref, cross_ref, pair_ref)
-
-
-def update(taps_ref, side_ref, part_ref, low_ref, high_ref, estimate_ref, out_ref, cross_ref, pair_ref):
-    def store(lead, row, value):
-        spot = swapped(lead, row)
-        out_ref[spot, :] = estimate_ref[spot, :] * value
-
-    add_rims(taps_ref, True, None, part_ref, low_ref, high_ref, store)
-    store_edges(side_ref, out_ref, cross_ref, pair_ref)
-
-
-def last_update(taps_ref, part_ref, low_ref, high_ref, estimate_ref, out_ref, cols_ref):
+    store_edges(side_ref, out_ref, own_ref, other_ref)
+
+
+def last_update(taps_ref, side_ref, part_ref, near_ref, far_ref, estimate_ref, out_ref, cols_ref):
     def store(lead, row, value):
         cols_ref[swapped(lead, row), :] = value
 
-    add_rims(taps_ref, True, None, part_ref, low_ref, high_ref, store)
+    add_rims(taps_ref, True, side_ref, part_ref, near_ref, far_ref, store)
     for i in range(8):
-        spots = [slice(SIDE * (8 * j + i), SIDE * (8 * j + i) + SIDE) for j in range(4)]
-        block = jnp.concatenate([estimate_ref[spot, :] * cols_ref[spot, :] for spot in spots], axis=0)
+        block = jnp.concatenate(
+            [
+                estimate_ref[WIDE * x + MARGIN : WIDE * x + MARGIN + SIDE, :]
+                * cols_ref[SIDE * x : SIDE * x + SIDE, :]
+                for x in range(i, SIDE, 8)
+            ],
+            axis=0,
+        )
         out_ref[pl.ds(i, Z, stride=8), :] = block.T
 
 
 FLAT = (SIDE * SIDE, Z)
 EDGE = (RIM * SIDE, Z)
+WIDE_FLAT = (SIDE * WIDE, Z)
+WIDE_EDGE = (RIM * WIDE, Z)
+WIDE_RIM = (2 * RIM * SIDE, Z)
 PIECES = (Z, 8, LANES)
 
 
@@ -361,9 +446,15 @@
     def rims_x(cross, pair):
         return lax.ppermute(cross, "slab", cross_swaps), lax.ppermute(pair, "slab", pair_swaps)
 
-    def rims_y(first, last):
+    y_one, y_two = [], []
+    for low, high in y_pairs:
+        upward, downward = (y_one, y_two) if (low // reps) % 2 == 0 else (y_two, y_one)
+        upward.append((low, high))
+        downward.append((high, low))
+
+    def rims_y(own, other):
         axes = ("slab", "rep")
-        return lax.ppermute(last, axes, y_pairs), lax.ppermute(first, axes, [(b, a) for a, b in y_pairs])
+        return lax.ppermute(other, axes, y_one), lax.ppermute(own, axes, y_two)
 
     def turn(pieces):
         return lax.all_to_all(pieces, "slab", split_axis=0, concat_axis=0, tiled=True)
@@ -389,38 +480,62 @@
     ]
     seen_pieces = call(observe, [PIECES], [((LINES, CAPACITY), BF16), ((LINES, LANES), F32)], *got)[0]
     arrived, seen_pieces = lax.optimization_barrier((arrived, seen_pieces))
-    estimate, flipped, first, last = call(
-        arrive, [FLAT, FLAT, EDGE, EDGE], [], arrived.reshape(Z * 8, LANES)
+    estimate, flipped, *edges = call(
+        arrive, [FLAT, FLAT, EDGE, EDGE], [], side, arrived.reshape(Z * 8, LANES), smem=1
     )
     seen_arrived = turn(seen_pieces)
-    own = functools.partial(call, functools.partial(own_share, False), [FLAT], [], taps, smem=1)
-    own_back = functools.partial(call, functools.partial(own_share, True), [FLAT], [], taps, smem=1)
-
-    def lateral(flip, part, rims):
-        value, first, last = call(
-            functools.partial(along_x, flip), [FLAT, EDGE, EDGE], [], taps, side, part, *rims, smem=2
-        )
-        rims = rims_y(first, last)
-        return (own_back if flip else own)(value)[0], *rims
-
+
+    def own(flip, value, rows=SIDE):
+        kernel = functools.partial(own_share, flip, SIDE, rows, RIM)
+        return call(kernel, [(SIDE * rows, Z)], [], taps, value, smem=1)[0]
+
+    cols = [(FLAT, F32)]
+    start_rims = rims_y(*edges)
     value, *edges = call(
-        along_y_first, [FLAT, EDGE, EDGE], [], taps, side, own(flipped)[0], *rims_y(first, last), smem=2
-    )
-    cols = [(FLAT, F32)]
-    blurred = call(
-        blur_x_last, [FLAT], cols, taps, side, own(value)[0], *rims_x(*edges), band, smem=2
+        along_y_first, [FLAT, EDGE, EDGE], [], taps, side, own(False, flipped), *start_rims, smem=2
+    )
+    blurred = call(blur, [FLAT], cols, taps, side, own(False, value), *rims_x(*edges), band, smem=2)[0]
+    seen, back, *edges = call(
+        first_ratio,
+        [FLAT, FLAT, WIDE_RIM, WIDE_RIM],
+        cols,
+        side,
+        seen_arrived.reshape(Z * 8, LANES),
+        blurred,
+        band,
+        smem=1,
+    )
+    near, far = rims_y(*edges)
+    part = call(
+        functools.partial(own_share, True, WIDE, SIDE, RIM + MARGIN), [WIDE_FLAT], [], taps, back, smem=1
     )[0]
-    seen, back, *edges = call(
-        first_ratio, [FLAT, FLAT, EDGE, EDGE], [], side, seen_arrived.reshape(Z * 8, LANES), blurred, band, smem=1
-    )
-    parts = lateral(True, own_back(back)[0], rims_x(*edges))
-    estimate, *edges = call(update, [FLAT, EDGE, EDGE], [], taps, side, *parts, estimate, smem=2)
-    parts = lateral(False, own(estimate)[0], rims_x(*edges))
+    near = call(near_share, [WIDE_RIM], [], taps, side, near, smem=2)[0]
+    value, *edges = call(
+        wide_rows, [WIDE_FLAT, WIDE_EDGE, WIDE_EDGE], [], taps, side, part, near, far, smem=2
+    )
+    rims = rims_x(*edges)
+    wide = call(extend, [WIDE_FLAT], [], side, estimate, *start_rims, smem=1)[0]
+    wide, value, *edges = call(
+        update_wide,
+        [WIDE_FLAT, FLAT, EDGE, EDGE],
+        [(WIDE_FLAT, F32)],
+        taps,
+        side,
+        own(True, value, WIDE),
+        *rims,
+        wide,
+        smem=2,
+    )
+    rims = rims_x(*edges)
     back, *edges = call(
-        blur_ratio, [FLAT, EDGE, EDGE], cols, taps, side, *parts, band, seen, smem=2
-    )
-    parts = lateral(True, own_back(back)[0], rims_x(*edges))
-    pieces = call(last_update, [(Z * 8, LANES)], cols, taps, *parts, estimate, smem=1)[0]
+        blur_ratio, [FLAT, EDGE, EDGE], cols, taps, side, own(False, value), *rims, band, seen, smem=2
+    )
+    rims = rims_x(*edges)
+    value, *edges = call(along_x, [FLAT, EDGE, EDGE], [], taps, side, own(True, back), *rims, smem=2)
+    rims = rims_y(*edges)
+    pieces = call(
+        last_update, [(Z * 8, LANES)], cols, taps, side, own(True, value), *rims, wide, smem=2
+    )[0]
     done = turn(pieces.reshape(PIECES))
     plane = call(plane_of, [(LINES, LANES)], [], done)[0]
     return plane.reshape(1, LINES, LANES)

time: 220 us -> 215 us (0.977)
  waiting for transfers between devices: 50.9 us -> 42.5 us
  blocking collectives: 46.3 us -> 52.4 us
  starting transfers between devices: 85.5 us -> 80.8 us
  Pallas kernels: 32.7 us -> 35.5 us
    ppermute x8 -> x6, waiting for transfers between devices: 26.2 us -> 13.7 us  [rims_y(): return (lax.ppermute(other, axes, y_one), lax.ppermute(own, axes, y_two))]
    all_to_all x1, blocking collectives: 46.3 us -> 52.4 us  [turn(): lax.all_to_all(pieces, 'slab', split_axis=0, concat_axis=0, tiled=True)]
    ppermute x4, waiting for transfers between devices: 5.7 us -> 9.76 us  [rims_x(): lax.ppermute(cross, 'slab', cross_swaps)]
    pallas_call x23, Pallas kernels: 32.7 us -> 35.5 us  [call(): pl.pallas_call(kernel, out_shape=outs, in_specs=specs, out_specs=tuple((p...]
    ppermute x8 -> x6, starting transfers between devices: 19.1 us -> 16.4 us  [rims_y(): return (lax.ppermute(other, axes, y_one), lax.ppermute(own, axes, y_two))]
  transfers between devices with their start and end apart: 21 -> 19, of which waited for: 16 -> 13; matrix products, arithmetic and copies ran while one was open for 1% -> 1% of each run, Pallas kernels for 10% -> 11%
where the time goes in v4:
time: 215 us
  starting transfers between devices  80.8 us (38%)
  blocking collectives  52.4 us (24%)
  waiting for transfers between devices  42.5 us (20%)
  Pallas kernels  35.5 us (17%)
    all_to_all x1, blocking collectives, turn(): lax.all_to_all(pieces, 'slab', split_axis=0, concat_axis=0, tiled=True)  52.4 us
    pallas_call x23, Pallas kernels, call(): pl.pallas_call(kernel, out_shape=outs, in_specs=specs, out_specs=tuple((p...  35.5 us
    all_to_all x2, starting transfers between devices, turn(): lax.all_to_all(pieces, 'slab', split_axis=0, concat_axis=0, tiled=True)  32.1 us
    ppermute x6, starting transfers between devices, rims_y(): return (lax.ppermute(other, axes, y_one), lax.ppermute(own, axes, y_two))  16.4 us
    ppermute x4, starting transfers between devices, rims_x(): lax.ppermute(cross, 'slab', cross_swaps)  14 us
    ppermute x6, waiting for transfers between devices, rims_y(): return (lax.ppermute(other, axes, y_one), lax.ppermute(own, axes, y_two))  13.7 us
    all_to_all x2, waiting for transfers between devices, turn(): lax.all_to_all(pieces, 'slab', split_axis=0, concat_axis=0, tiled=True)  11.6 us
    ppermute x3, starting transfers between devices, shards(): lax.ppermute(block, 'rep', [(r, (r + step) % reps) for r in range(reps)])  10.5 us
  transfers between devices with their start and end apart: 19, of which 13 were waited for; matrix products, arithmetic and copies ran while one was open for 1% of the time, Pallas kernels for 11%

profile of v4, /device:TPU:1, one launch (start us, length us, event | category | flops | bytes accessed | tf_op | source)
XLA Modules:
  0.0 214.6 jit_solution(2296870233594410474)
XLA Ops:
  0.0 1.0 copy-done.1
  1.0 1.2 store_tiles.1
  2.2 20.7 %all-to-all-start = ((f32[128,8,128]{2,1,0:T(8,128)}), f32[128,8,128]{2,1,0:T(8,128)S(1)}, u32[]{:S(2)}, u32[]{:S(2)}) async-start(f32[128,8,128]{2,1,0:T(8,128)} %store_tiles.1), calls=%async_computation | async-start | bytes 1048576 | tf_op jit(solution)/shard_map/all_to_all | solution.py:460
  22.9 0.0 copy-start.2
  23.0 0.7 copy-done.2
  23.6 3.8 %pack_rows.1 = (f32[520,128]{1,0:T(8,128)S(1)}, f32[520,128]{1,0:T(8,128)S(1)}, f32[520,128]{1,0:T(8,128)S(1)}, f32[520,128]{1,0:T(8,128)S(1)}) custom-call(s32[1]{0:T(128)} %bitcast.2.rep_ref, f32[1280,128]{1,0:T(8,128)S(1)} %copy-done, f32[10,128]{1,0:T(8,128)S(1)} %bitcast.15, s32[10,128]{1,0:T(8,128)S(1)} %bitcast.16, s32[10,128]{1,0:T(8,128)S(1)} %bitcast.17), custom_call_target="tpu_custom_call" | custom-call | tf_op jit(solution)/shard_map/pack_rows/pallas_call | solution.py:32
  27.4 3.1 %collective-permute-start = (f32[520,128]{1,0:T(8,128)S(1)}, f32[520,128]{1,0:T(8,128)S(1)}, u32[]{:S(2)}, u32[]{:S(2)}) collective-permute-start(f32[520,128]{1,0:T(8,128)S(1)} %get-tuple-element.36), channel_id=1, source_target_pairs={{0,1},{1,2},{2,3},{3,0},{4,5},{5,6},{6,7},{7,4},{8,9},{9,10},{10,1... | collective-permute-start | bytes 798728 | tf_op jit(solution)/shard_map/ppermute | solution.py:478
  30.6 4.4 %collective-permute-start.1 = (f32[520,128]{1,0:T(8,128)S(1)}, f32[520,128]{1,0:T(8,128)S(1)}, u32[]{:S(2)}, u32[]{:S(2)}) collective-permute-start(f32[520,128]{1,0:T(8,128)S(1)} %get-tuple-element.37), channel_id=1, source_target_pairs={{0,2},{1,3},{2,0},{3,1},{4,6},{5,7},{6,4},{7,5},{8,10},{9,11},{10,... | collective-permute-start | bytes 798728 | tf_op jit(solution)/shard_map/ppermute | solution.py:478
  34.9 3.1 %collective-permute-start.2 = (f32[520,128]{1,0:T(8,128)S(1)}, f32[520,128]{1,0:T(8,128)S(1)}, u32[]{:S(2)}, u32[]{:S(2)}) collective-permute-start(f32[520,128]{1,0:T(8,128)S(1)} %get-tuple-element.38), channel_id=1, source_target_pairs={{0,3},{1,0},{2,1},{3,2},{4,7},{5,4},{6,5},{7,6},{8,11},{9,8},{10,9... | collective-permute-start | bytes 798728 | tf_op jit(solution)/shard_map/ppermute | solution.py:478
  38.0 6.2 %collective-permute-done.1.refs_2_ = f32[520,128]{1,0:T(8,128)S(1)} collective-permute-done((f32[520,128]{1,0:T(8,128)S(1)}, f32[520,128]{1,0:T(8,128)S(1)}, u32[]{:S(2)}, u32[]{:S(2)}) %collective-permute-start.1) | collective-permute-done | bytes 266272 | tf_op jit(solution)/shard_map/ppermute | solution.py:478
  44.2 1.2 collective-permute-done.2.refs_3_
  45.5 4.1 %observe.1 = f32[128,8,128]{2,1,0:T(8,128)} custom-call(f32[520,128]{1,0:T(8,128)S(1)} %get-tuple-element.35.refs_0_, f32[520,128]{1,0:T(8,128)S(1)} %collective-permute-done.refs_1_, f32[520,128]{1,0:T(8,128)S(1)} %collective-permute-done.1.refs_2_, f32[520,128]{1,0:T(8,128)S(1)} %collective-permute-done.2.refs_3_), custom_call_target="tpu_custom_call" | custom-call | tf_op jit(solution)/shard_map/observe/pallas_call | solution.py:32
  49.6 6.6 %all-to-all-done = f32[128,8,128]{2,1,0:T(8,128)S(1)} async-done(((f32[128,8,128]{2,1,0:T(8,128)}), f32[128,8,128]{2,1,0:T(8,128)S(1)}, u32[]{:S(2)}, u32[]{:S(2)}) %all-to-all-start) | async-done | bytes 524320 | tf_op jit(solution)/shard_map/all_to_all | solution.py:460
  56.1 11.4 %all-to-all-start.1 = ((f32[128,8,128]{2,1,0:T(8,128)}), f32[128,8,128]{2,1,0:T(8,128)S(1)}, u32[]{:S(2)}, u32[]{:S(2)}) async-start(f32[128,8,128]{2,1,0:T(8,128)} %observe.1), calls=%async_computation.1 | async-start | bytes 1048576 | tf_op jit(solution)/shard_map/all_to_all | solution.py:460
  67.5 0.6 arrive.1
  68.1 0.0 copy-start.6
  68.1 1.3 collective-permute-start.3
  69.4 4.0 %collective-permute-start.4 = (f32[480,128]{1,0:T(8,128)S(1)}, f32[480,128]{1,0:T(8,128)S(1)}, u32[]{:S(2)}, u32[]{:S(2)}) collective-permute-start(f32[480,128]{1,0:T(8,128)S(1)} %get-tuple-element.43), channel_id=1, source_target_pairs={{128,0},{129,1},{130,2},{131,3},{4,132},{5,133},{6,134},{7,135},{1... | collective-permute-start | bytes 737288 | tf_op jit(solution)/shard_map/ppermute | solution.py:457
  73.5 0.6 reduce_sum.9
  74.1 0.6 broadcast_divide_fusion.taps_ref
  74.7 1.5 own_share.7.part_ref
  76.2 0.0 collective-permute-done.3.near_ref
  76.2 3.5 %collective-permute-done.4.far_ref = f32[480,128]{1,0:T(8,128)S(1)} collective-permute-done((f32[480,128]{1,0:T(8,128)S(1)}, f32[480,128]{1,0:T(8,128)S(1)}, u32[]{:S(2)}, u32[]{:S(2)}) %collective-permute-start.4) | collective-permute-done | bytes 245792 | tf_op jit(solution)/shard_map/ppermute | solution.py:457
  79.6 1.0 along_y_first.1
  80.7 4.5 %collective-permute-start.5 = (f32[480,128]{1,0:T(8,128)S(1)}, f32[480,128]{1,0:T(8,128)S(1)}, u32[]{:S(2)}, u32[]{:S(2)}) collective-permute-start(f32[480,128]{1,0:T(8,128)S(1)} %get-tuple-element.45), channel_id=1, source_target_pairs={{4,8},{8,4},{12,16},{16,12},{20,24},{24,20},{28,32},{32,28},{36,40... | collective-permute-start | bytes 737288 | tf_op jit(solution)/shard_map/ppermute | solution.py:447
  85.2 0.0 copy-start.5
  85.2 2.1 collective-permute-start.6
  87.3 0.2 axial_band.1.band_ref
  87.5 1.5 own_share.8.part_ref
  89.0 5.6 %collective-permute-done.5.cross_ref = f32[480,128]{1,0:T(8,128)S(1)} collective-permute-done((f32[480,128]{1,0:T(8,128)S(1)}, f32[480,128]{1,0:T(8,128)S(1)}, u32[]{:S(2)}, u32[]{:S(2)}) %collective-permute-start.5) | collective-permute-done | bytes 245792 | tf_op jit(solution)/shard_map/ppermute | solution.py:447
  94.6 1.1 blur.1.blurred_ref
  95.7 5.0 %all-to-all-done.1 = f32[128,8,128]{2,1,0:T(8,128)S(1)} async-done(((f32[128,8,128]{2,1,0:T(8,128)}), f32[128,8,128]{2,1,0:T(8,128)S(1)}, u32[]{:S(2)}, u32[]{:S(2)}) %all-to-all-start.1) | async-done | bytes 524320 | tf_op jit(solution)/shard_map/all_to_all | solution.py:460
  100.7 0.8 first_ratio.1
  101.6 1.3 collective-permute-start.7
  102.9 4.0 %collective-permute-start.8 = (f32[960,128]{1,0:T(8,128)S(1)}, f32[960,128]{1,0:T(8,128)S(1)}, u32[]{:S(2)}, u32[]{:S(2)}) collective-permute-start(f32[960,128]{1,0:T(8,128)S(1)} %get-tuple-element.49), channel_id=1, source_target_pairs={{128,0},{129,1},{130,2},{131,3},{4,132},{5,133},{6,134},{7,135},{1... | collective-permute-start | bytes 1474568 | tf_op jit(solution)/shard_map/ppermute | solution.py:457
  106.9 1.8 own_share.9.part_ref
  108.7 2.9 %collective-permute-done.7.near_ref = f32[960,128]{1,0:T(8,128)S(1)} collective-permute-done((f32[960,128]{1,0:T(8,128)S(1)}, f32[960,128]{1,0:T(8,128)S(1)}, u32[]{:S(2)}, u32[]{:S(2)}) %collective-permute-start.7) | collective-permute-done | bytes 491552 | tf_op jit(solution)/shard_map/ppermute | solution.py:457
  111.5 1.1 near_share.1.near_ref
  112.6 4.7 %collective-permute-done.8.far_ref = f32[960,128]{1,0:T(8,128)S(1)} collective-permute-done((f32[960,128]{1,0:T(8,128)S(1)}, f32[960,128]{1,0:T(8,128)S(1)}, u32[]{:S(2)}, u32[]{:S(2)}) %collective-permute-start.8) | collective-permute-done | bytes 491552 | tf_op jit(solution)/shard_map/ppermute | solution.py:457
  117.4 1.8 wide_rows.1
  119.1 3.2 %collective-permute-start.9 = (f32[960,128]{1,0:T(8,128)S(1)}, f32[960,128]{1,0:T(8,128)S(1)}, u32[]{:S(2)}, u32[]{:S(2)}) collective-permute-start(f32[960,128]{1,0:T(8,128)S(1)} %get-tuple-element.51), channel_id=1, source_target_pairs={{4,8},{8,4},{12,16},{16,12},{20,24},{24,20},{28,32},{32,28},{36,40... | collective-permute-start | bytes 1474568 | tf_op jit(solution)/shard_map/ppermute | solution.py:447
  122.3 1.9 collective-permute-start.10
  124.2 0.4 extend.1.start_ref
  124.6 2.4 %own_share.10.part_ref = f32[2048,128]{1,0:T(8,128)S(1)} custom-call(f32[31]{0:T(128)S(1)} %broadcast_divide_fusion.taps_ref, f32[2048,128]{1,0:T(8,128)S(1)} %get-tuple-element.50.mid_ref), custom_call_target="tpu_custom_call" | custom-call | tf_op jit(solution)/shard_map/own_share/pallas_call | solution.py:32
  127.0 2.3 %collective-permute-done.9.cross_ref = f32[960,128]{1,0:T(8,128)S(1)} collective-permute-done((f32[960,128]{1,0:T(8,128)S(1)}, f32[960,128]{1,0:T(8,128)S(1)}, u32[]{:S(2)}, u32[]{:S(2)}) %collective-permute-start.9) | collective-permute-done | bytes 491552 | tf_op jit(solution)/shard_map/ppermute | solution.py:447
  129.3 2.9 %update_wide.1 = (f32[2048,128]{1,0:T(8,128)S(1)}, f32[1024,128]{1,0:T(8,128)S(1)}, f32[480,128]{1,0:T(8,128)S(1)}, f32[480,128]{1,0:T(8,128)S(1)}) custom-call(f32[31]{0:T(128)S(1)} %broadcast_divide_fusion.taps_ref, s32[1]{0:T(128)} %bitcast.side_ref, f32[2048,128]{1,0:T(8,128)S(1)} %own_share.10.part_ref, ...), custom_call_target="tpu_custom_call" | custom-call | tf_op jit(solution)/shard_map/update_wide/pallas_call | solution.py:32
  132.2 3.2 %collective-permute-start.11 = (f32[480,128]{1,0:T(8,128)S(1)}, f32[480,128]{1,0:T(8,128)S(1)}, u32[]{:S(2)}, u32[]{:S(2)}) collective-permute-start(f32[480,128]{1,0:T(8,128)S(1)} %get-tuple-element.55), channel_id=1, source_target_pairs={{4,8},{8,4},{12,16},{16,12},{20,24},{24,20},{28,32},{32,28},{36,40... | collective-permute-start | bytes 737288 | tf_op jit(solution)/shard_map/ppermute | solution.py:447
  135.4 1.9 collective-permute-start.12
  137.3 1.5 own_share.11.part_ref
  138.8 0.9 collective-permute-done.11.cross_ref
  139.7 1.5 blur_ratio.1
  141.2 3.2 %collective-permute-start.13 = (f32[480,128]{1,0:T(8,128)S(1)}, f32[480,128]{1,0:T(8,128)S(1)}, u32[]{:S(2)}, u32[]{:S(2)}) collective-permute-start(f32[480,128]{1,0:T(8,128)S(1)} %get-tuple-element.59), channel_id=1, source_target_pairs={{4,8},{8,4},{12,16},{16,12},{20,24},{24,20},{28,32},{32,28},{36,40... | collective-permute-start | bytes 737288 | tf_op jit(solution)/shard_map/ppermute | solution.py:447
  144.4 1.9 collective-permute-start.14
  146.3 1.5 own_share.12.part_ref
  147.8 0.9 collective-permute-done.13.cross_ref
  148.8 1.0 along_x.1
  149.8 1.3 collective-permute-start.15
  151.1 4.5 %collective-permute-start.16 = (f32[480,128]{1,0:T(8,128)S(1)}, f32[480,128]{1,0:T(8,128)S(1)}, u32[]{:S(2)}, u32[]{:S(2)}) collective-permute-start(f32[480,128]{1,0:T(8,128)S(1)} %get-tuple-element.63), channel_id=1, source_target_pairs={{128,0},{129,1},{130,2},{131,3},{4,132},{5,133},{6,134},{7,135},{1... | collective-permute-start | bytes 737288 | tf_op jit(solution)/shard_map/ppermute | solution.py:457
  155.6 1.5 own_share.13.part_ref
  157.1 0.2 collective-permute-done.15.near_ref
  157.2 2.5 %collective-permute-done.16.far_ref = f32[480,128]{1,0:T(8,128)S(1)} collective-permute-done((f32[480,128]{1,0:T(8,128)S(1)}, f32[480,128]{1,0:T(8,128)S(1)}, u32[]{:S(2)}, u32[]{:S(2)}) %collective-permute-start.16) | collective-permute-done | bytes 245792 | tf_op jit(solution)/shard_map/ppermute | solution.py:457
  159.7 1.3 last_update.1
  161.0 52.4 %all_to_all.15.got_ref = f32[128,8,128]{2,1,0:T(8,128)S(1)} all-to-all(f32[128,8,128]{2,1,0:T(8,128)S(1)} %bitcast.13), channel_id=1, replica_groups=mesh['slab'=128,'rep'=4] {'slab'}, dimensions={0} | all-to-all | bytes 1048576 | tf_op jit(solution)/shard_map/all_to_all | solution.py:460
  213.4 1.2 plane_of.1
  (14 shorter events, 0.0 us)
Async XLA Ops:
  0.0 1.0 copy-start.1
  2.2 20.7 %copy-start = (f32[1280,128]{1,0:T(8,128)S(1)}, f32[1280,128]{1,0:T(8,128)}, u32[]{:S(2)}) copy-start(f32[1280,128]{1,0:T(8,128)} %rows_ref.1) | copy-start | bytes 1966084
  2.2 20.7 %copy-start.3 = (s32[1280]{0:T(1024)S(1)}, s32[1280]{0:T(1024)}, u32[]{:S(2)}) copy-start(s32[1280]{0:T(1024)} %param.9) | copy-start | bytes 15364
  2.2 20.7 %copy-start.4 = (s32[1280]{0:T(1024)S(1)}, s32[1280]{0:T(1024)}, u32[]{:S(2)}) copy-start(s32[1280]{0:T(1024)} %param.10) | copy-start | bytes 15364
  2.2 53.9 %all-to-all-start = ((f32[128,8,128]{2,1,0:T(8,128)}), f32[128,8,128]{2,1,0:T(8,128)S(1)}, u32[]{:S(2)}, u32[]{:S(2)}) async-start(f32[128,8,128]{2,1,0:T(8,128)} %store_tiles.1), calls=%async_computation | async-start | bytes 1048576 | tf_op jit(solution)/shard_map/all_to_all | solution.py:460
  22.9 0.7 copy-start.2
  27.4 10.6 %collective-permute-start = (f32[520,128]{1,0:T(8,128)S(1)}, f32[520,128]{1,0:T(8,128)S(1)}, u32[]{:S(2)}, u32[]{:S(2)}) collective-permute-start(f32[520,128]{1,0:T(8,128)S(1)} %get-tuple-element.36), channel_id=1, source_target_pairs={{0,1},{1,2},{2,3},{3,0},{4,5},{5,6},{6,7},{7,4},{8,9},{9,10},{10,1... | collective-permute-start | bytes 798728 | tf_op jit(solution)/shard_map/ppermute | solution.py:478
  30.6 13.7 %collective-permute-start.1 = (f32[520,128]{1,0:T(8,128)S(1)}, f32[520,128]{1,0:T(8,128)S(1)}, u32[]{:S(2)}, u32[]{:S(2)}) collective-permute-start(f32[520,128]{1,0:T(8,128)S(1)} %get-tuple-element.37), channel_id=1, source_target_pairs={{0,2},{1,3},{2,0},{3,1},{4,6},{5,7},{6,4},{7,5},{8,10},{9,11},{10,... | collective-permute-start | bytes 798728 | tf_op jit(solution)/shard_map/ppermute | solution.py:478
  34.9 10.5 %collective-permute-start.2 = (f32[520,128]{1,0:T(8,128)S(1)}, f32[520,128]{1,0:T(8,128)S(1)}, u32[]{:S(2)}, u32[]{:S(2)}) collective-permute-start(f32[520,128]{1,0:T(8,128)S(1)} %get-tuple-element.38), channel_id=1, source_target_pairs={{0,3},{1,0},{2,1},{3,2},{4,7},{5,4},{6,5},{7,6},{8,11},{9,8},{10,9... | collective-permute-start | bytes 798728 | tf_op jit(solution)/shard_map/ppermute | solution.py:478
  56.1 44.6 %all-to-all-start.1 = ((f32[128,8,128]{2,1,0:T(8,128)}), f32[128,8,128]{2,1,0:T(8,128)S(1)}, u32[]{:S(2)}, u32[]{:S(2)}) async-start(f32[128,8,128]{2,1,0:T(8,128)} %observe.1), calls=%async_computation.1 | async-start | bytes 1048576 | tf_op jit(solution)/shard_map/all_to_all | solution.py:460
  68.1 5.4 %copy-start.6 = (f32[31]{0:T(128)S(1)}, f32[31]{0:T(128)}, u32[]{:S(2)}) copy-start(f32[31]{0:T(128)} %param.12) | copy-start | bytes 376
  68.1 8.1 %collective-permute-start.3 = (f32[480,128]{1,0:T(8,128)S(1)}, f32[480,128]{1,0:T(8,128)S(1)}, u32[]{:S(2)}, u32[]{:S(2)}) collective-permute-start(f32[480,128]{1,0:T(8,128)S(1)} %get-tuple-element.42), channel_id=1, source_target_pairs={{0,128},{1,129},{2,130},{3,131},{132,4},{133,5},{134,6},{135,7},{8... | collective-permute-start | bytes 737288 | tf_op jit(solution)/shard_map/ppermute | solution.py:457
  69.4 10.2 %collective-permute-start.4 = (f32[480,128]{1,0:T(8,128)S(1)}, f32[480,128]{1,0:T(8,128)S(1)}, u32[]{:S(2)}, u32[]{:S(2)}) collective-permute-start(f32[480,128]{1,0:T(8,128)S(1)} %get-tuple-element.43), channel_id=1, source_target_pairs={{128,0},{129,1},{130,2},{131,3},{4,132},{5,133},{6,134},{7,135},{1... | collective-permute-start | bytes 737288 | tf_op jit(solution)/shard_map/ppermute | solution.py:457
  80.7 13.9 %collective-permute-start.5 = (f32[480,128]{1,0:T(8,128)S(1)}, f32[480,128]{1,0:T(8,128)S(1)}, u32[]{:S(2)}, u32[]{:S(2)}) collective-permute-start(f32[480,128]{1,0:T(8,128)S(1)} %get-tuple-element.45), channel_id=1, source_target_pairs={{4,8},{8,4},{12,16},{16,12},{20,24},{24,20},{28,32},{32,28},{36,40... | collective-permute-start | bytes 737288 | tf_op jit(solution)/shard_map/ppermute | solution.py:447
  85.2 2.1 copy-start.5
  85.2 9.4 %collective-permute-start.6 = (f32[480,128]{1,0:T(8,128)S(1)}, f32[480,128]{1,0:T(8,128)S(1)}, u32[]{:S(2)}, u32[]{:S(2)}) collective-permute-start(f32[480,128]{1,0:T(8,128)S(1)} %get-tuple-element.46), channel_id=1, source_target_pairs={{0,4},{4,0},{8,12},{12,8},{16,20},{20,16},{24,28},{28,24},{32,36},... | collective-permute-start | bytes 737288 | tf_op jit(solution)/shard_map/ppermute | solution.py:447
  101.6 10.0 %collective-permute-start.7 = (f32[960,128]{1,0:T(8,128)S(1)}, f32[960,128]{1,0:T(8,128)S(1)}, u32[]{:S(2)}, u32[]{:S(2)}) collective-permute-start(f32[960,128]{1,0:T(8,128)S(1)} %get-tuple-element.48), channel_id=1, source_target_pairs={{0,128},{1,129},{2,130},{3,131},{132,4},{133,5},{134,6},{135,7},{8... | collective-permute-start | bytes 1474568 | tf_op jit(solution)/shard_map/ppermute | solution.py:457
  102.9 14.5 %collective-permute-start.8 = (f32[960,128]{1,0:T(8,128)S(1)}, f32[960,128]{1,0:T(8,128)S(1)}, u32[]{:S(2)}, u32[]{:S(2)}) collective-permute-start(f32[960,128]{1,0:T(8,128)S(1)} %get-tuple-element.49), channel_id=1, source_target_pairs={{128,0},{129,1},{130,2},{131,3},{4,132},{5,133},{6,134},{7,135},{1... | collective-permute-start | bytes 1474568 | tf_op jit(solution)/shard_map/ppermute | solution.py:457
  119.1 10.1 %collective-permute-start.9 = (f32[960,128]{1,0:T(8,128)S(1)}, f32[960,128]{1,0:T(8,128)S(1)}, u32[]{:S(2)}, u32[]{:S(2)}) collective-permute-start(f32[960,128]{1,0:T(8,128)S(1)} %get-tuple-element.51), channel_id=1, source_target_pairs={{4,8},{8,4},{12,16},{16,12},{20,24},{24,20},{28,32},{32,28},{36,40... | collective-permute-start | bytes 1474568 | tf_op jit(solution)/shard_map/ppermute | solution.py:447
  122.3 7.0 %collective-permute-start.10 = (f32[960,128]{1,0:T(8,128)S(1)}, f32[960,128]{1,0:T(8,128)S(1)}, u32[]{:S(2)}, u32[]{:S(2)}) collective-permute-start(f32[960,128]{1,0:T(8,128)S(1)} %get-tuple-element.52), channel_id=1, source_target_pairs={{0,4},{4,0},{8,12},{12,8},{16,20},{20,16},{24,28},{28,24},{32,36},... | collective-permute-start | bytes 1474568 | tf_op jit(solution)/shard_map/ppermute | solution.py:447
  132.2 7.5 %collective-permute-start.11 = (f32[480,128]{1,0:T(8,128)S(1)}, f32[480,128]{1,0:T(8,128)S(1)}, u32[]{:S(2)}, u32[]{:S(2)}) collective-permute-start(f32[480,128]{1,0:T(8,128)S(1)} %get-tuple-element.55), channel_id=1, source_target_pairs={{4,8},{8,4},{12,16},{16,12},{20,24},{24,20},{28,32},{32,28},{36,40... | collective-permute-start | bytes 737288 | tf_op jit(solution)/shard_map/ppermute | solution.py:447
  135.4 4.3 %collective-permute-start.12 = (f32[480,128]{1,0:T(8,128)S(1)}, f32[480,128]{1,0:T(8,128)S(1)}, u32[]{:S(2)}, u32[]{:S(2)}) collective-permute-start(f32[480,128]{1,0:T(8,128)S(1)} %get-tuple-element.56), channel_id=1, source_target_pairs={{0,4},{4,0},{8,12},{12,8},{16,20},{20,16},{24,28},{28,24},{32,36},... | collective-permute-start | bytes 737288 | tf_op jit(solution)/shard_map/ppermute | solution.py:447
  141.2 7.5 %collective-permute-start.13 = (f32[480,128]{1,0:T(8,128)S(1)}, f32[480,128]{1,0:T(8,128)S(1)}, u32[]{:S(2)}, u32[]{:S(2)}) collective-permute-start(f32[480,128]{1,0:T(8,128)S(1)} %get-tuple-element.59), channel_id=1, source_target_pairs={{4,8},{8,4},{12,16},{16,12},{20,24},{24,20},{28,32},{32,28},{36,40... | collective-permute-start | bytes 737288 | tf_op jit(solution)/shard_map/ppermute | solution.py:447
  144.4 4.3 %collective-permute-start.14 = (f32[480,128]{1,0:T(8,128)S(1)}, f32[480,128]{1,0:T(8,128)S(1)}, u32[]{:S(2)}, u32[]{:S(2)}) collective-permute-start(f32[480,128]{1,0:T(8,128)S(1)} %get-tuple-element.60), channel_id=1, source_target_pairs={{0,4},{4,0},{8,12},{12,8},{16,20},{20,16},{24,28},{28,24},{32,36},... | collective-permute-start | bytes 737288 | tf_op jit(solution)/shard_map/ppermute | solution.py:447
  149.8 7.4 %collective-permute-start.15 = (f32[480,128]{1,0:T(8,128)S(1)}, f32[480,128]{1,0:T(8,128)S(1)}, u32[]{:S(2)}, u32[]{:S(2)}) collective-permute-start(f32[480,128]{1,0:T(8,128)S(1)} %get-tuple-element.62), channel_id=1, source_target_pairs={{0,128},{1,129},{2,130},{3,131},{132,4},{133,5},{134,6},{135,7},{8... | collective-permute-start | bytes 737288 | tf_op jit(solution)/shard_map/ppermute | solution.py:457
  151.1 8.6 %collective-permute-start.16 = (f32[480,128]{1,0:T(8,128)S(1)}, f32[480,128]{1,0:T(8,128)S(1)}, u32[]{:S(2)}, u32[]{:S(2)}) collective-permute-start(f32[480,128]{1,0:T(8,128)S(1)} %get-tuple-element.63), channel_id=1, source_target_pairs={{128,0},{129,1},{130,2},{131,3},{4,132},{5,133},{6,134},{7,135},{1... | collective-permute-start | bytes 737288 | tf_op jit(solution)/shard_map/ppermute | solution.py:457

commit v5 on v4

--- a/solution.py
+++ b/solution.py
@@ -262,14 +262,6 @@
     return pl.ds(SIDE * row + lead, 8, stride=SIDE)
 
 
-def along_x(taps_ref, side_ref, part_ref, cross_ref, pair_ref, out_ref, own_ref, other_ref):
-    def store(lead, row, value):
-        out_ref[swapped(lead, row), :] = value
-
-    add_rims(taps_ref, True, side_ref, part_ref, cross_ref, pair_ref, store)
-    store_edges(side_ref, out_ref, own_ref, other_ref)
-
-
 def along_y_first(taps_ref, side_ref, part_ref, near_ref, far_ref, out_ref, cross_ref, pair_ref):
     def store(lead, row, value):
         out_ref[swapped(lead, row), :] = value
@@ -305,14 +297,14 @@
         yield n, total
 
 
-def near_share(taps_ref, side_ref, near_ref, out_ref):
+def near_share(taps_ref, side_ref, rim_ref, out_ref):
     taps = taps_of(taps_ref, True)
     for side in range(2):
 
         @pl.when(side_ref[0] == side)
         def _():
             for row in range(0, SIDE, 8):
-                for n, total in rim_share(taps, side == 1, near_ref, row):
+                for n, total in rim_share(taps, side == 1, rim_ref, row):
                     out_ref[SIDE * n + row : SIDE * n + row + 8, :] = total
 
 
@@ -340,7 +332,17 @@
 
 
 def update_wide(
-    taps_ref, side_ref, part_ref, cross_ref, pair_ref, start_ref, new_ref, out_ref, own_ref, other_ref, turned_ref
+    taps_ref,
+    side_ref,
+    part_ref,
+    cross_ref,
+    pair_ref,
+    start_ref,
+    new_ref,
+    out_ref,
+    cross_out_ref,
+    pair_out_ref,
+    turned_ref,
 ):
     def store(x, e, value):
         spot = slice(WIDE * x + e, WIDE * x + e + 8)
@@ -354,7 +356,7 @@
         out_ref[swapped(y, x), :] = value
 
     correlate(taps_of(taps_ref, False), turned_ref, WIDE, SIDE, SIDE, RIM - MARGIN, store_y)
-    store_edges(side_ref, out_ref, own_ref, other_ref)
+    store_edges(side_ref, out_ref, cross_out_ref, pair_out_ref, rim=2 * RIM)
 
 
 def axial(value, band, back):
@@ -380,22 +382,81 @@
     out_ref[...] = axial(cols_ref[...], band_ref[...], False)
 
 
-def first_ratio(side_ref, got_ref, blurred_ref, band_ref, seen_ref, out_ref, own_ref, other_ref, cols_ref):
+def first_ratio(
+    side_ref,
+    got_ref,
+    blurred_ref,
+    band_ref,
+    seen_ref,
+    cross_ref,
+    pair_ref,
+    out_ref,
+    own_ref,
+    other_ref,
+    cols_ref,
+):
     columns_from(got_ref, seen_ref)
     cols_ref[...] = axial(seen_ref[...] / blurred_ref[...], band_ref[...], True)
     swap_leading(cols_ref, out_ref)
     store_edges(side_ref, out_ref, own_ref, other_ref, rim=2 * RIM)
+    store_edges(side_ref, seen_ref, cross_ref, pair_ref)
+
+
+def extend_x(side_ref, tile_ref, cross_ref, pair_ref, out_ref):
+    ones = jnp.ones((SIDE, Z), F32)
+    out_ref[:SIDE, :] = ones
+    out_ref[SIDE * (WIDE - 1) :, :] = ones
+    out_ref[SIDE * MARGIN : SIDE * (MARGIN + SIDE), :] = tile_ref[...]
+    low_at, high_at = SIDE, SIDE * (MARGIN + SIDE)
+    cross_at = pl.multiple_of(jnp.where(side_ref[0] == 0, low_at, high_at), 8)
+    pair_at = pl.multiple_of(jnp.where(side_ref[0] == 0, high_at, low_at), 8)
+    out_ref[pl.ds(cross_at, RIM * SIDE), :] = cross_ref[...]
+    out_ref[pl.ds(pair_at, RIM * SIDE), :] = pair_ref[...]
 
 
 def blur_ratio(
-    taps_ref, side_ref, part_ref, cross_ref, pair_ref, band_ref, seen_ref, out_ref, own_ref, other_ref, cols_ref
+    taps_ref,
+    side_ref,
+    part_ref,
+    cross_ref,
+    pair_ref,
+    band_ref,
+    seen_ref,
+    out_ref,
+    own_ref,
+    other_ref,
+    cols_ref,
+    ratio_ref,
 ):
-    along_x_last(taps_ref, side_ref, part_ref, cross_ref, pair_ref, cols_ref)
+    taps = taps_of(taps_ref, False)
+    for side in range(2):
+
+        @pl.when(side_ref[0] == side)
+        def _():
+            for row in range(0, SIDE, 8):
+
+                def store(e, total):
+                    spot = slice(SIDE * e + row, SIDE * e + row + 8)
+                    cols_ref[spot, :] = part_ref[spot, :] + total
+
+                low_ref, high_ref = (cross_ref, pair_ref) if side == 0 else (pair_ref, cross_ref)
+                for n, total in rim_share(taps, False, low_ref, row):
+                    store(1 + n, total)
+                for n, total in rim_share(taps, True, high_ref, row):
+                    store(SIDE + 1 + n, total)
+                for e in (0, SIDE - 1, SIDE, WIDE - 1):
+                    store(e, 1.0 if e in (0, WIDE - 1) else 0.0)
+
     band = band_ref[...]
-    for start in range(0, SIDE * SIDE, 256):
+    for start in range(0, WIDE * SIDE, 256):
         spot = slice(start, start + 256)
         ratio = seen_ref[spot, :] / axial(cols_ref[spot, :], band, False)
-        out_ref[spot, :] = axial(ratio, band, True)
+        ratio_ref[spot, :] = axial(ratio, band, True)
+
+    def store_x(x, y, value):
+        out_ref[swapped(x, y), :] = value
+
+    correlate(taps_of(taps_ref, True), ratio_ref, WIDE, SIDE, SIDE, RIM - MARGIN, store_x)
     store_edges(side_ref, out_ref, own_ref, other_ref)
 
 
@@ -495,9 +556,9 @@
         along_y_first, [FLAT, EDGE, EDGE], [], taps, side, own(False, flipped), *start_rims, smem=2
     )
     blurred = call(blur, [FLAT], cols, taps, side, own(False, value), *rims_x(*edges), band, smem=2)[0]
-    seen, back, *edges = call(
+    seen, seen_cross, seen_pair, back, *edges = call(
         first_ratio,
-        [FLAT, FLAT, WIDE_RIM, WIDE_RIM],
+        [FLAT, EDGE, EDGE, FLAT, WIDE_RIM, WIDE_RIM],
         cols,
         side,
         seen_arrived.reshape(Z * 8, LANES),
@@ -505,10 +566,15 @@
         band,
         smem=1,
     )
+
+    def wide_own(flip, value):
+        kernel = functools.partial(own_share, flip, WIDE, SIDE, RIM + MARGIN)
+        return call(kernel, [WIDE_FLAT], [], taps, value, smem=1)[0]
+
     near, far = rims_y(*edges)
-    part = call(
-        functools.partial(own_share, True, WIDE, SIDE, RIM + MARGIN), [WIDE_FLAT], [], taps, back, smem=1
-    )[0]
+    part = wide_own(True, back)
+    seen_cross, seen_pair, part = lax.optimization_barrier((seen_cross, seen_pair, part))
+    near, *seen_rims = lax.optimization_barrier((near, *rims_x(seen_cross, seen_pair)))
     near = call(near_share, [WIDE_RIM], [], taps, side, near, smem=2)[0]
     value, *edges = call(
         wide_rows, [WIDE_FLAT, WIDE_EDGE, WIDE_EDGE], [], taps, side, part, near, far, smem=2
@@ -517,7 +583,7 @@
     wide = call(extend, [WIDE_FLAT], [], side, estimate, *start_rims, smem=1)[0]
     wide, value, *edges = call(
         update_wide,
-        [WIDE_FLAT, FLAT, EDGE, EDGE],
+        [WIDE_FLAT, FLAT, WIDE_RIM, WIDE_RIM],
         [(WIDE_FLAT, F32)],
         taps,
         side,
@@ -527,11 +593,19 @@
         smem=2,
     )
     rims = rims_x(*edges)
-    back, *edges = call(
-        blur_ratio, [FLAT, EDGE, EDGE], cols, taps, side, own(False, value), *rims, band, seen, smem=2
-    )
-    rims = rims_x(*edges)
-    value, *edges = call(along_x, [FLAT, EDGE, EDGE], [], taps, side, own(True, back), *rims, smem=2)
+    seen = call(extend_x, [WIDE_FLAT], [], side, seen, *seen_rims, smem=1)[0]
+    value, *edges = call(
+        blur_ratio,
+        [FLAT, EDGE, EDGE],
+        [(WIDE_FLAT, F32), (WIDE_FLAT, F32)],
+        taps,
+        side,
+        wide_own(False, value),
+        *rims,
+        band,
+        seen,
+        smem=2,
+    )
     rims = rims_y(*edges)
     pieces = call(
         last_update, [(Z * 8, LANES)], cols, taps, side, own(True, value), *rims, wide, smem=2

time: 215 us -> 213 us (level)
  waiting for transfers between devices: 42.5 us -> 38.5 us
    ppermute x6, waiting for transfers between devices: 13.7 us -> 5.03 us  [rims_y(): return (lax.ppermute(other, axes, y_one), lax.ppermute(own, axes, y_two))]
    ppermute x4, waiting for transfers between devices: 9.76 us -> 14.5 us  [rims_x(): lax.ppermute(cross, 'slab', cross_swaps)]
    pallas_call x23 -> x22, Pallas kernels: 35.5 us -> 36.4 us  [call(): pl.pallas_call(kernel, out_shape=outs, in_specs=specs, out_specs=tuple((p...]
  transfers between devices with their start and end apart: 19 -> 19, of which waited for: 13 -> 11; matrix products, arithmetic and copies ran while one was open for 1% -> 1% of each run, Pallas kernels for 11% -> 11%
where the time goes in v5:
time: 213 us; the launch traced here: 212 us
  starting transfers between devices  79.9 us (38%)
  blocking collectives  54.2 us (25%)
  waiting for transfers between devices  38.5 us (18%)
  Pallas kernels  36.4 us (17%)
    all_to_all x1, blocking collectives, turn(): lax.all_to_all(pieces, 'slab', split_axis=0, concat_axis=0, tiled=True)  54.2 us
    pallas_call x22, Pallas kernels, call(): pl.pallas_call(kernel, out_shape=outs, in_specs=specs, out_specs=tuple((p...  36.4 us
    all_to_all x2, starting transfers between devices, turn(): lax.all_to_all(pieces, 'slab', split_axis=0, concat_axis=0, tiled=True)  32.1 us
    ppermute x6, starting transfers between devices, rims_y(): return (lax.ppermute(other, axes, y_one), lax.ppermute(own, axes, y_two))  16.1 us
    ppermute x4, waiting for transfers between devices, rims_x(): lax.ppermute(cross, 'slab', cross_swaps)  14.5 us
    ppermute x4, starting transfers between devices, rims_x(): lax.ppermute(cross, 'slab', cross_swaps)  13.3 us
    all_to_all x2, waiting for transfers between devices, turn(): lax.all_to_all(pieces, 'slab', split_axis=0, concat_axis=0, tiled=True)  11.6 us
    ppermute x3, starting transfers between devices, shards(): lax.ppermute(block, 'rep', [(r, (r + step) % reps) for r in range(reps)])  10.5 us
  transfers between devices with their start and end apart: 19, of which 11 were waited for; matrix products, arithmetic and copies ran while one was open for 1% of the time, Pallas kernels for 11%

profile of v5, /device:TPU:1, one launch (start us, length us, event | category | flops | bytes accessed | tf_op | source)
XLA Modules:
  0.0 212.4 jit_solution(11580407768742075970)
XLA Ops:
  0.0 1.0 copy-done.1
  1.0 1.2 store_tiles.1
  2.2 20.7 %all-to-all-start = ((f32[128,8,128]{2,1,0:T(8,128)}), f32[128,8,128]{2,1,0:T(8,128)S(1)}, u32[]{:S(2)}, u32[]{:S(2)}) async-start(f32[128,8,128]{2,1,0:T(8,128)} %store_tiles.1), calls=%async_computation | async-start | bytes 1048576 | tf_op jit(solution)/shard_map/all_to_all | solution.py:521
  23.0 0.0 copy-start.2
  23.0 0.7 copy-done.2
  23.7 3.8 %pack_rows.1 = (f32[520,128]{1,0:T(8,128)S(1)}, f32[520,128]{1,0:T(8,128)S(1)}, f32[520,128]{1,0:T(8,128)S(1)}, f32[520,128]{1,0:T(8,128)S(1)}) custom-call(s32[1]{0:T(128)} %bitcast.2.rep_ref, f32[1280,128]{1,0:T(8,128)S(1)} %copy-done, f32[10,128]{1,0:T(8,128)S(1)} %bitcast.15, s32[10,128]{1,0:T(8,128)S(1)} %bitcast.16, s32[10,128]{1,0:T(8,128)S(1)} %bitcast.17), custom_call_target="tpu_custom_call" | custom-call | tf_op jit(solution)/shard_map/pack_rows/pallas_call | solution.py:32
  27.5 3.1 %collective-permute-start = (f32[520,128]{1,0:T(8,128)S(1)}, f32[520,128]{1,0:T(8,128)S(1)}, u32[]{:S(2)}, u32[]{:S(2)}) collective-permute-start(f32[520,128]{1,0:T(8,128)S(1)} %get-tuple-element.41), channel_id=1, source_target_pairs={{0,1},{1,2},{2,3},{3,0},{4,5},{5,6},{6,7},{7,4},{8,9},{9,10},{10,1... | collective-permute-start | bytes 798728 | tf_op jit(solution)/shard_map/ppermute | solution.py:539
  30.6 4.4 %collective-permute-start.1 = (f32[520,128]{1,0:T(8,128)S(1)}, f32[520,128]{1,0:T(8,128)S(1)}, u32[]{:S(2)}, u32[]{:S(2)}) collective-permute-start(f32[520,128]{1,0:T(8,128)S(1)} %get-tuple-element.42), channel_id=1, source_target_pairs={{0,2},{1,3},{2,0},{3,1},{4,6},{5,7},{6,4},{7,5},{8,10},{9,11},{10,... | collective-permute-start | bytes 798728 | tf_op jit(solution)/shard_map/ppermute | solution.py:539
  34.9 3.1 %collective-permute-start.2 = (f32[520,128]{1,0:T(8,128)S(1)}, f32[520,128]{1,0:T(8,128)S(1)}, u32[]{:S(2)}, u32[]{:S(2)}) collective-permute-start(f32[520,128]{1,0:T(8,128)S(1)} %get-tuple-element.43), channel_id=1, source_target_pairs={{0,3},{1,0},{2,1},{3,2},{4,7},{5,4},{6,5},{7,6},{8,11},{9,8},{10,9... | collective-permute-start | bytes 798728 | tf_op jit(solution)/shard_map/ppermute | solution.py:539
  38.0 0.0 collective-permute-done.refs_1_
  38.0 6.2 %collective-permute-done.1.refs_2_ = f32[520,128]{1,0:T(8,128)S(1)} collective-permute-done((f32[520,128]{1,0:T(8,128)S(1)}, f32[520,128]{1,0:T(8,128)S(1)}, u32[]{:S(2)}, u32[]{:S(2)}) %collective-permute-start.1) | collective-permute-done | bytes 266272 | tf_op jit(solution)/shard_map/ppermute | solution.py:539
  44.3 1.2 collective-permute-done.2.refs_3_
  45.5 4.1 %observe.1 = f32[128,8,128]{2,1,0:T(8,128)} custom-call(f32[520,128]{1,0:T(8,128)S(1)} %get-tuple-element.40.refs_0_, f32[520,128]{1,0:T(8,128)S(1)} %collective-permute-done.refs_1_, f32[520,128]{1,0:T(8,128)S(1)} %collective-permute-done.1.refs_2_, f32[520,128]{1,0:T(8,128)S(1)} %collective-permute-done.2.refs_3_), custom_call_target="tpu_custom_call" | custom-call | tf_op jit(solution)/shard_map/observe/pallas_call | solution.py:32
  49.6 6.6 %all-to-all-done = f32[128,8,128]{2,1,0:T(8,128)S(1)} async-done(((f32[128,8,128]{2,1,0:T(8,128)}), f32[128,8,128]{2,1,0:T(8,128)S(1)}, u32[]{:S(2)}, u32[]{:S(2)}) %all-to-all-start) | async-done | bytes 524320 | tf_op jit(solution)/shard_map/all_to_all | solution.py:521
  56.2 11.4 %all-to-all-start.1 = ((f32[128,8,128]{2,1,0:T(8,128)}), f32[128,8,128]{2,1,0:T(8,128)S(1)}, u32[]{:S(2)}, u32[]{:S(2)}) async-start(f32[128,8,128]{2,1,0:T(8,128)} %observe.1), calls=%async_computation.1 | async-start | bytes 1048576 | tf_op jit(solution)/shard_map/all_to_all | solution.py:521
  67.5 0.6 arrive.1
  68.1 0.0 copy-start.6
  68.1 1.3 collective-permute-start.3
  69.4 4.0 %collective-permute-start.4 = (f32[480,128]{1,0:T(8,128)S(1)}, f32[480,128]{1,0:T(8,128)S(1)}, u32[]{:S(2)}, u32[]{:S(2)}) collective-permute-start(f32[480,128]{1,0:T(8,128)S(1)} %get-tuple-element.48), channel_id=1, source_target_pairs={{128,0},{129,1},{130,2},{131,3},{4,132},{5,133},{6,134},{7,135},{1... | collective-permute-start | bytes 737288 | tf_op jit(solution)/shard_map/ppermute | solution.py:518
  73.5 0.7 reduce_sum.9
  74.1 0.6 broadcast_divide_fusion.taps_ref
  74.8 1.5 own_share.6.part_ref
  76.3 0.0 collective-permute-done.3.near_ref
  76.3 3.4 %collective-permute-done.4.far_ref = f32[480,128]{1,0:T(8,128)S(1)} collective-permute-done((f32[480,128]{1,0:T(8,128)S(1)}, f32[480,128]{1,0:T(8,128)S(1)}, u32[]{:S(2)}, u32[]{:S(2)}) %collective-permute-start.4) | collective-permute-done | bytes 245792 | tf_op jit(solution)/shard_map/ppermute | solution.py:518
  79.7 1.0 along_y_first.1
  80.7 4.5 %collective-permute-start.5 = (f32[480,128]{1,0:T(8,128)S(1)}, f32[480,128]{1,0:T(8,128)S(1)}, u32[]{:S(2)}, u32[]{:S(2)}) collective-permute-start(f32[480,128]{1,0:T(8,128)S(1)} %get-tuple-element.50), channel_id=1, source_target_pairs={{4,8},{8,4},{12,16},{16,12},{20,24},{24,20},{28,32},{32,28},{36,40... | collective-permute-start | bytes 737288 | tf_op jit(solution)/shard_map/ppermute | solution.py:508
  85.2 0.0 copy-start.5
  85.2 2.1 collective-permute-start.6
  87.3 0.2 axial_band.1.band_ref
  87.5 1.5 own_share.7.part_ref
  89.0 5.6 %collective-permute-done.5.cross_ref = f32[480,128]{1,0:T(8,128)S(1)} collective-permute-done((f32[480,128]{1,0:T(8,128)S(1)}, f32[480,128]{1,0:T(8,128)S(1)}, u32[]{:S(2)}, u32[]{:S(2)}) %collective-permute-start.5) | collective-permute-done | bytes 245792 | tf_op jit(solution)/shard_map/ppermute | solution.py:508
  94.6 0.0 collective-permute-done.6.pair_ref
  94.6 1.1 blur.1.blurred_ref
  95.7 5.0 %all-to-all-done.1 = f32[128,8,128]{2,1,0:T(8,128)S(1)} async-done(((f32[128,8,128]{2,1,0:T(8,128)}), f32[128,8,128]{2,1,0:T(8,128)S(1)}, u32[]{:S(2)}, u32[]{:S(2)}) %all-to-all-start.1) | async-done | bytes 524320 | tf_op jit(solution)/shard_map/all_to_all | solution.py:521
  100.7 0.8 first_ratio.1
  101.6 1.3 collective-permute-start.7
  102.9 4.0 %collective-permute-start.10 = (f32[960,128]{1,0:T(8,128)S(1)}, f32[960,128]{1,0:T(8,128)S(1)}, u32[]{:S(2)}, u32[]{:S(2)}) collective-permute-start(f32[960,128]{1,0:T(8,128)S(1)} %get-tuple-element.60), channel_id=1, source_target_pairs={{128,0},{129,1},{130,2},{131,3},{4,132},{5,133},{6,134},{7,135},{1... | collective-permute-start | bytes 1474568 | tf_op jit(solution)/shard_map/ppermute | solution.py:518
  106.9 1.8 own_share.8.part_ref
  108.7 3.0 %collective-permute-start.8 = (f32[480,128]{1,0:T(8,128)S(1)}, f32[480,128]{1,0:T(8,128)S(1)}, u32[]{:S(2)}, u32[]{:S(2)}) collective-permute-start(f32[480,128]{1,0:T(8,128)S(1)} %get-tuple-element.57), channel_id=1, source_target_pairs={{4,8},{8,4},{12,16},{16,12},{20,24},{24,20},{28,32},{32,28},{36,40... | collective-permute-start | bytes 737288 | tf_op jit(solution)/shard_map/ppermute | solution.py:508
  111.7 1.9 collective-permute-start.9
  113.6 2.9 %collective-permute-done.8.cross_ref = f32[480,128]{1,0:T(8,128)S(1)} collective-permute-done((f32[480,128]{1,0:T(8,128)S(1)}, f32[480,128]{1,0:T(8,128)S(1)}, u32[]{:S(2)}, u32[]{:S(2)}) %collective-permute-start.8) | collective-permute-done | bytes 245792 | tf_op jit(solution)/shard_map/ppermute | solution.py:508
  116.5 0.0 collective-permute-done.9.pair_ref
  116.5 1.1 near_share.1.near_ref
  117.6 1.8 wide_rows.1
  119.4 2.9 %collective-permute-start.11 = (f32[960,128]{1,0:T(8,128)S(1)}, f32[960,128]{1,0:T(8,128)S(1)}, u32[]{:S(2)}, u32[]{:S(2)}) collective-permute-start(f32[960,128]{1,0:T(8,128)S(1)} %get-tuple-element.62), channel_id=1, source_target_pairs={{4,8},{8,4},{12,16},{16,12},{20,24},{24,20},{28,32},{32,28},{36,40... | collective-permute-start | bytes 1474568 | tf_op jit(solution)/shard_map/ppermute | solution.py:508
  122.3 1.9 collective-permute-start.12
  124.3 0.4 extend.1.start_ref
  124.7 2.4 %own_share.9.part_ref = f32[2048,128]{1,0:T(8,128)S(1)} custom-call(f32[31]{0:T(128)S(1)} %broadcast_divide_fusion.taps_ref, f32[2048,128]{1,0:T(8,128)S(1)} %get-tuple-element.61.mid_ref), custom_call_target="tpu_custom_call" | custom-call | tf_op jit(solution)/shard_map/own_share/pallas_call | solution.py:32
  127.1 2.5 %collective-permute-done.11.cross_ref = f32[960,128]{1,0:T(8,128)S(1)} collective-permute-done((f32[960,128]{1,0:T(8,128)S(1)}, f32[960,128]{1,0:T(8,128)S(1)}, u32[]{:S(2)}, u32[]{:S(2)}) %collective-permute-start.11) | collective-permute-done | bytes 491552 | tf_op jit(solution)/shard_map/ppermute | solution.py:508
  129.6 3.0 %update_wide.1 = (f32[2048,128]{1,0:T(8,128)S(1)}, f32[1024,128]{1,0:T(8,128)S(1)}, f32[960,128]{1,0:T(8,128)S(1)}, f32[960,128]{1,0:T(8,128)S(1)}) custom-call(f32[31]{0:T(128)S(1)} %broadcast_divide_fusion.taps_ref, s32[1]{0:T(128)} %bitcast.side_ref, f32[2048,128]{1,0:T(8,128)S(1)} %own_share.9.part_ref, ...), custom_call_target="tpu_custom_call" | custom-call | tf_op jit(solution)/shard_map/update_wide/pallas_call | solution.py:32
  132.5 2.9 %collective-permute-start.13 = (f32[960,128]{1,0:T(8,128)S(1)}, f32[960,128]{1,0:T(8,128)S(1)}, u32[]{:S(2)}, u32[]{:S(2)}) collective-permute-start(f32[960,128]{1,0:T(8,128)S(1)} %get-tuple-element.66), channel_id=1, source_target_pairs={{4,8},{8,4},{12,16},{16,12},{20,24},{24,20},{28,32},{32,28},{36,40... | collective-permute-start | bytes 1474568 | tf_op jit(solution)/shard_map/ppermute | solution.py:508
  135.5 1.9 collective-permute-start.14
  137.4 0.1 extend_x.1.seen_ref
  137.5 1.8 own_share.10.part_ref
  139.3 3.4 %collective-permute-done.13.cross_ref = f32[960,128]{1,0:T(8,128)S(1)} collective-permute-done((f32[960,128]{1,0:T(8,128)S(1)}, f32[960,128]{1,0:T(8,128)S(1)}, u32[]{:S(2)}, u32[]{:S(2)}) %collective-permute-start.13) | collective-permute-done | bytes 491552 | tf_op jit(solution)/shard_map/ppermute | solution.py:508
  142.7 4.4 %blur_ratio.1 = (f32[1024,128]{1,0:T(8,128)S(1)}, f32[480,128]{1,0:T(8,128)S(1)}, f32[480,128]{1,0:T(8,128)S(1)}) custom-call(f32[31]{0:T(128)S(1)} %broadcast_divide_fusion.taps_ref, s32[1]{0:T(128)} %bitcast.side_ref, f32[2048,128]{1,0:T(8,128)S(1)} %own_share.10.part_ref, f32[960,128]{1,0:T(8,128)S(1)} %collective-permute-done.13.cross_ref, ...), custom_call_target="tpu_custom_call" | custom-call | tf_op jit(solution)/shard_map/blur_ratio/pallas_call | solution.py:32
  147.1 1.3 collective-permute-start.15
  148.4 4.2 %collective-permute-start.16 = (f32[480,128]{1,0:T(8,128)S(1)}, f32[480,128]{1,0:T(8,128)S(1)}, u32[]{:S(2)}, u32[]{:S(2)}) collective-permute-start(f32[480,128]{1,0:T(8,128)S(1)} %get-tuple-element.73), channel_id=1, source_target_pairs={{128,0},{129,1},{130,2},{131,3},{4,132},{5,133},{6,134},{7,135},{1... | collective-permute-start | bytes 737288 | tf_op jit(solution)/shard_map/ppermute | solution.py:518
  152.7 1.5 own_share.11.part_ref
  154.1 1.3 collective-permute-done.15.near_ref
  155.4 0.3 collective-permute-done.16.far_ref
  155.8 1.3 last_update.1
  157.0 54.2 %all_to_all.15.got_ref = f32[128,8,128]{2,1,0:T(8,128)S(1)} all-to-all(f32[128,8,128]{2,1,0:T(8,128)S(1)} %bitcast.13), channel_id=1, replica_groups=mesh['slab'=128,'rep'=4] {'slab'}, dimensions={0} | all-to-all | bytes 1048576 | tf_op jit(solution)/shard_map/all_to_all | solution.py:521
  211.2 1.2 plane_of.1
  (13 shorter events, 0.0 us)
Async XLA Ops:
  0.0 1.0 copy-start.1
  2.2 20.7 %copy-start = (f32[1280,128]{1,0:T(8,128)S(1)}, f32[1280,128]{1,0:T(8,128)}, u32[]{:S(2)}) copy-start(f32[1280,128]{1,0:T(8,128)} %rows_ref.1) | copy-start | bytes 1966084
  2.2 20.7 %copy-start.3 = (s32[1280]{0:T(1024)S(1)}, s32[1280]{0:T(1024)}, u32[]{:S(2)}) copy-start(s32[1280]{0:T(1024)} %param.9) | copy-start | bytes 15364
  2.2 20.7 %copy-start.4 = (s32[1280]{0:T(1024)S(1)}, s32[1280]{0:T(1024)}, u32[]{:S(2)}) copy-start(s32[1280]{0:T(1024)} %param.10) | copy-start | bytes 15364
  2.2 53.9 %all-to-all-start = ((f32[128,8,128]{2,1,0:T(8,128)}), f32[128,8,128]{2,1,0:T(8,128)S(1)}, u32[]{:S(2)}, u32[]{:S(2)}) async-start(f32[128,8,128]{2,1,0:T(8,128)} %store_tiles.1), calls=%async_computation | async-start | bytes 1048576 | tf_op jit(solution)/shard_map/all_to_all | solution.py:521
  23.0 0.7 copy-start.2
  27.5 10.6 %collective-permute-start = (f32[520,128]{1,0:T(8,128)S(1)}, f32[520,128]{1,0:T(8,128)S(1)}, u32[]{:S(2)}, u32[]{:S(2)}) collective-permute-start(f32[520,128]{1,0:T(8,128)S(1)} %get-tuple-element.41), channel_id=1, source_target_pairs={{0,1},{1,2},{2,3},{3,0},{4,5},{5,6},{6,7},{7,4},{8,9},{9,10},{10,1... | collective-permute-start | bytes 798728 | tf_op jit(solution)/shard_map/ppermute | solution.py:539
  30.6 13.7 %collective-permute-start.1 = (f32[520,128]{1,0:T(8,128)S(1)}, f32[520,128]{1,0:T(8,128)S(1)}, u32[]{:S(2)}, u32[]{:S(2)}) collective-permute-start(f32[520,128]{1,0:T(8,128)S(1)} %get-tuple-element.42), channel_id=1, source_target_pairs={{0,2},{1,3},{2,0},{3,1},{4,6},{5,7},{6,4},{7,5},{8,10},{9,11},{10,... | collective-permute-start | bytes 798728 | tf_op jit(solution)/shard_map/ppermute | solution.py:539
  34.9 10.5 %collective-permute-start.2 = (f32[520,128]{1,0:T(8,128)S(1)}, f32[520,128]{1,0:T(8,128)S(1)}, u32[]{:S(2)}, u32[]{:S(2)}) collective-permute-start(f32[520,128]{1,0:T(8,128)S(1)} %get-tuple-element.43), channel_id=1, source_target_pairs={{0,3},{1,0},{2,1},{3,2},{4,7},{5,4},{6,5},{7,6},{8,11},{9,8},{10,9... | collective-permute-start | bytes 798728 | tf_op jit(solution)/shard_map/ppermute | solution.py:539
  56.2 44.6 %all-to-all-start.1 = ((f32[128,8,128]{2,1,0:T(8,128)}), f32[128,8,128]{2,1,0:T(8,128)S(1)}, u32[]{:S(2)}, u32[]{:S(2)}) async-start(f32[128,8,128]{2,1,0:T(8,128)} %observe.1), calls=%async_computation.1 | async-start | bytes 1048576 | tf_op jit(solution)/shard_map/all_to_all | solution.py:521
  68.1 5.4 %copy-start.6 = (f32[31]{0:T(128)S(1)}, f32[31]{0:T(128)}, u32[]{:S(2)}) copy-start(f32[31]{0:T(128)} %param.12) | copy-start | bytes 376
  68.1 8.1 %collective-permute-start.3 = (f32[480,128]{1,0:T(8,128)S(1)}, f32[480,128]{1,0:T(8,128)S(1)}, u32[]{:S(2)}, u32[]{:S(2)}) collective-permute-start(f32[480,128]{1,0:T(8,128)S(1)} %get-tuple-element.47), channel_id=1, source_target_pairs={{0,128},{1,129},{2,130},{3,131},{132,4},{133,5},{134,6},{135,7},{8... | collective-permute-start | bytes 737288 | tf_op jit(solution)/shard_map/ppermute | solution.py:518
  69.4 10.2 %collective-permute-start.4 = (f32[480,128]{1,0:T(8,128)S(1)}, f32[480,128]{1,0:T(8,128)S(1)}, u32[]{:S(2)}, u32[]{:S(2)}) collective-permute-start(f32[480,128]{1,0:T(8,128)S(1)} %get-tuple-element.48), channel_id=1, source_target_pairs={{128,0},{129,1},{130,2},{131,3},{4,132},{5,133},{6,134},{7,135},{1... | collective-permute-start | bytes 737288 | tf_op jit(solution)/shard_map/ppermute | solution.py:518
  80.7 13.9 %collective-permute-start.5 = (f32[480,128]{1,0:T(8,128)S(1)}, f32[480,128]{1,0:T(8,128)S(1)}, u32[]{:S(2)}, u32[]{:S(2)}) collective-permute-start(f32[480,128]{1,0:T(8,128)S(1)} %get-tuple-element.50), channel_id=1, source_target_pairs={{4,8},{8,4},{12,16},{16,12},{20,24},{24,20},{28,32},{32,28},{36,40... | collective-permute-start | bytes 737288 | tf_op jit(solution)/shard_map/ppermute | solution.py:508
  85.2 2.1 copy-start.5
  85.2 9.4 %collective-permute-start.6 = (f32[480,128]{1,0:T(8,128)S(1)}, f32[480,128]{1,0:T(8,128)S(1)}, u32[]{:S(2)}, u32[]{:S(2)}) collective-permute-start(f32[480,128]{1,0:T(8,128)S(1)} %get-tuple-element.51), channel_id=1, source_target_pairs={{0,4},{4,0},{8,12},{12,8},{16,20},{20,16},{24,28},{28,24},{32,36},... | collective-permute-start | bytes 737288 | tf_op jit(solution)/shard_map/ppermute | solution.py:508
  101.6 14.9 %collective-permute-start.7 = (f32[960,128]{1,0:T(8,128)S(1)}, f32[960,128]{1,0:T(8,128)S(1)}, u32[]{:S(2)}, u32[]{:S(2)}) collective-permute-start(f32[960,128]{1,0:T(8,128)S(1)} %get-tuple-element.56), channel_id=1, source_target_pairs={{0,128},{1,129},{2,130},{3,131},{132,4},{133,5},{134,6},{135,7},{8... | collective-permute-start | bytes 1474568 | tf_op jit(solution)/shard_map/ppermute | solution.py:518
  102.9 14.7 %collective-permute-start.10 = (f32[960,128]{1,0:T(8,128)S(1)}, f32[960,128]{1,0:T(8,128)S(1)}, u32[]{:S(2)}, u32[]{:S(2)}) collective-permute-start(f32[960,128]{1,0:T(8,128)S(1)} %get-tuple-element.60), channel_id=1, source_target_pairs={{128,0},{129,1},{130,2},{131,3},{4,132},{5,133},{6,134},{7,135},{1... | collective-permute-start | bytes 1474568 | tf_op jit(solution)/shard_map/ppermute | solution.py:518
  108.7 7.8 %collective-permute-start.8 = (f32[480,128]{1,0:T(8,128)S(1)}, f32[480,128]{1,0:T(8,128)S(1)}, u32[]{:S(2)}, u32[]{:S(2)}) collective-permute-start(f32[480,128]{1,0:T(8,128)S(1)} %get-tuple-element.57), channel_id=1, source_target_pairs={{4,8},{8,4},{12,16},{16,12},{20,24},{24,20},{28,32},{32,28},{36,40... | collective-permute-start | bytes 737288 | tf_op jit(solution)/shard_map/ppermute | solution.py:508
  111.7 4.9 %collective-permute-start.9 = (f32[480,128]{1,0:T(8,128)S(1)}, f32[480,128]{1,0:T(8,128)S(1)}, u32[]{:S(2)}, u32[]{:S(2)}) collective-permute-start(f32[480,128]{1,0:T(8,128)S(1)} %get-tuple-element.58), channel_id=1, source_target_pairs={{0,4},{4,0},{8,12},{12,8},{16,20},{20,16},{24,28},{28,24},{32,36},... | collective-permute-start | bytes 737288 | tf_op jit(solution)/shard_map/ppermute | solution.py:508
  119.4 10.1 %collective-permute-start.11 = (f32[960,128]{1,0:T(8,128)S(1)}, f32[960,128]{1,0:T(8,128)S(1)}, u32[]{:S(2)}, u32[]{:S(2)}) collective-permute-start(f32[960,128]{1,0:T(8,128)S(1)} %get-tuple-element.62), channel_id=1, source_target_pairs={{4,8},{8,4},{12,16},{16,12},{20,24},{24,20},{28,32},{32,28},{36,40... | collective-permute-start | bytes 1474568 | tf_op jit(solution)/shard_map/ppermute | solution.py:508
  122.3 7.2 %collective-permute-start.12 = (f32[960,128]{1,0:T(8,128)S(1)}, f32[960,128]{1,0:T(8,128)S(1)}, u32[]{:S(2)}, u32[]{:S(2)}) collective-permute-start(f32[960,128]{1,0:T(8,128)S(1)} %get-tuple-element.63), channel_id=1, source_target_pairs={{0,4},{4,0},{8,12},{12,8},{16,20},{20,16},{24,28},{28,24},{32,36},... | collective-permute-start | bytes 1474568 | tf_op jit(solution)/shard_map/ppermute | solution.py:508
  132.5 10.1 %collective-permute-start.13 = (f32[960,128]{1,0:T(8,128)S(1)}, f32[960,128]{1,0:T(8,128)S(1)}, u32[]{:S(2)}, u32[]{:S(2)}) collective-permute-start(f32[960,128]{1,0:T(8,128)S(1)} %get-tuple-element.66), channel_id=1, source_target_pairs={{4,8},{8,4},{12,16},{16,12},{20,24},{24,20},{28,32},{32,28},{36,40... | collective-permute-start | bytes 1474568 | tf_op jit(solution)/shard_map/ppermute | solution.py:508
  135.5 7.2 %collective-permute-start.14 = (f32[960,128]{1,0:T(8,128)S(1)}, f32[960,128]{1,0:T(8,128)S(1)}, u32[]{:S(2)}, u32[]{:S(2)}) collective-permute-start(f32[960,128]{1,0:T(8,128)S(1)} %get-tuple-element.67), channel_id=1, source_target_pairs={{0,4},{4,0},{8,12},{12,8},{16,20},{20,16},{24,28},{28,24},{32,36},... | collective-permute-start | bytes 1474568 | tf_op jit(solution)/shard_map/ppermute | solution.py:508
  147.1 8.3 %collective-permute-start.15 = (f32[480,128]{1,0:T(8,128)S(1)}, f32[480,128]{1,0:T(8,128)S(1)}, u32[]{:S(2)}, u32[]{:S(2)}) collective-permute-start(f32[480,128]{1,0:T(8,128)S(1)} %get-tuple-element.72), channel_id=1, source_target_pairs={{0,128},{1,129},{2,130},{3,131},{132,4},{133,5},{134,6},{135,7},{8... | collective-permute-start | bytes 737288 | tf_op jit(solution)/shard_map/ppermute | solution.py:518
  148.4 7.3 %collective-permute-start.16 = (f32[480,128]{1,0:T(8,128)S(1)}, f32[480,128]{1,0:T(8,128)S(1)}, u32[]{:S(2)}, u32[]{:S(2)}) collective-permute-start(f32[480,128]{1,0:T(8,128)S(1)} %get-tuple-element.73), channel_id=1, source_target_pairs={{128,0},{129,1},{130,2},{131,3},{4,132},{5,133},{6,134},{7,135},{1... | collective-permute-start | bytes 737288 | tf_op jit(solution)/shard_map/ppermute | solution.py:518

commit v6 on v5

--- a/solution.py
+++ b/solution.py
@@ -161,28 +161,36 @@
         )
 
 
-def observe(*refs):
-    got_refs, (out_ref, hot_ref, plane_ref) = refs[:OWNERS], refs[OWNERS:]
-    total = jnp.zeros((LINES, 2 * LANES), F32)
-    weights = jnp.zeros((LINES, 8), F32)
+def line_sums(got_ref, hot_ref):
     at = lax.broadcasted_iota(jnp.int32, (LINES, LANES), 0)
-    for got_ref in got_refs:
-        meta = got_ref[CAPACITY:, :]
-        where = meta[4:8].astype(jnp.int32)
-        for q in range(4):
-            hot = jnp.where(at == where[q : q + 1, :], 1.0, 0.0)
-            hot_ref[:, q * LANES : (q + 1) * LANES] = hot.astype(BF16)
-        hot = hot_ref[...]
-        high, low = halves(got_ref[:CAPACITY, :])
-        total += jnp.dot(hot, jnp.concatenate([high, low], axis=1), preferred_element_type=F32)
-        weight = jnp.concatenate([meta[q : q + 1] for q in range(4)], axis=1)
-        parts = [p.astype(F32) for p in thirds(weight)]
-        stacked = jnp.concatenate(parts + [jnp.zeros((5, CAPACITY), F32)], axis=0).astype(BF16)
-        weights += lax.dot_general(
-            hot, stacked, (((1,), (1,)), ((), ())), preferred_element_type=F32
-        )
-    weight_sum = weights[:, 0:1] + weights[:, 1:2] + weights[:, 2:3]
-    plane_ref[...] = (total[:, :LANES] + total[:, LANES:]) / weight_sum
+    meta = got_ref[CAPACITY:, :]
+    where = meta[4:8].astype(jnp.int32)
+    for q in range(4):
+        hot = jnp.where(at == where[q : q + 1, :], 1.0, 0.0)
+        hot_ref[:, q * LANES : (q + 1) * LANES] = hot.astype(BF16)
+    hot = hot_ref[...]
+    high, low = halves(got_ref[:CAPACITY, :])
+    rows = jnp.dot(hot, jnp.concatenate([high, low], axis=1), preferred_element_type=F32)
+    weight = jnp.concatenate([meta[q : q + 1] for q in range(4)], axis=1)
+    parts = [p.astype(F32) for p in thirds(weight)]
+    stacked = jnp.concatenate(parts + [jnp.zeros((5, CAPACITY), F32)], axis=0).astype(BF16)
+    weights = lax.dot_general(hot, stacked, (((1,), (1,)), ((), ())), preferred_element_type=F32)
+    return rows[:, :LANES] + rows[:, LANES:], weights[:, 0:1] + weights[:, 1:2] + weights[:, 2:3]
+
+
+def begin_sums(got_ref, total_ref, weight_ref, hot_ref):
+    total_ref[...], weight_ref[...] = line_sums(got_ref, hot_ref)
+
+
+def add_sums(got_ref, before_ref, before_weight_ref, total_ref, weight_ref, hot_ref):
+    rows, weights = line_sums(got_ref, hot_ref)
+    total_ref[...] = before_ref[...] + rows
+    weight_ref[...] = before_weight_ref[...] + weights
+
+
+def observe(got_ref, before_ref, before_weight_ref, out_ref, hot_ref, plane_ref):
+    rows, weights = line_sums(got_ref, hot_ref)
+    plane_ref[...] = (before_ref[...] + rows) / (before_weight_ref[...] + weights)
     store_tiles(plane_ref, out_ref)
 
 
@@ -539,7 +547,11 @@
         block if step == 0 else lax.ppermute(block, "rep", [(r, (r + step) % reps) for r in range(reps)])
         for step, block in enumerate(sent)
     ]
-    seen_pieces = call(observe, [PIECES], [((LINES, CAPACITY), BF16), ((LINES, LANES), F32)], *got)[0]
+    hot = [((LINES, CAPACITY), BF16)]
+    sums = call(begin_sums, [(LINES, LANES), (LINES, 1)], hot, got[0])
+    for block in got[1:-1]:
+        sums = call(add_sums, [(LINES, LANES), (LINES, 1)], hot, block, *sums)
+    seen_pieces = call(observe, [PIECES], hot + [((LINES, LANES), F32)], got[-1], *sums)[0]
     arrived, seen_pieces = lax.optimization_barrier((arrived, seen_pieces))
     estimate, flipped, *edges = call(
         arrive, [FLAT, FLAT, EDGE, EDGE], [], side, arrived.reshape(Z * 8, LANES), smem=1

time: 213 us -> 211 us (level)
  starting transfers between devices: 79.9 us -> 77.7 us
    ppermute x3, waiting for transfers between devices: 7.44 us -> 5.13 us  [shards(): lax.ppermute(block, 'rep', [(r, (r + step) % reps) for r in range(reps)])]
    all_to_all x2, waiting for transfers between devices: 11.6 us -> 13.8 us  [turn(): lax.all_to_all(pieces, 'slab', split_axis=0, concat_axis=0, tiled=True)]
    all_to_all x2, starting transfers between devices: 32.1 us -> 29.9 us  [turn(): lax.all_to_all(pieces, 'slab', split_axis=0, concat_axis=0, tiled=True)]
    pallas_call x22 -> x25, Pallas kernels: 36.4 us -> 36.5 us  [call(): pl.pallas_call(kernel, out_shape=outs, in_specs=specs, out_specs=tuple((p...]
where the time goes in v6:
time: 211 us; the launch traced here: 210 us
  starting transfers between devices  77.7 us (37%)
  blocking collectives  54.2 us (26%)
  waiting for transfers between devices  38.4 us (18%)
  Pallas kernels  36.5 us (17%)
    all_to_all x1, blocking collectives, turn(): lax.all_to_all(pieces, 'slab', split_axis=0, concat_axis=0, tiled=True)  54.2 us
    pallas_call x25, Pallas kernels, call(): pl.pallas_call(kernel, out_shape=outs, in_specs=specs, out_specs=tuple((p...  36.5 us
    all_to_all x2, starting transfers between devices, turn(): lax.all_to_all(pieces, 'slab', split_axis=0, concat_axis=0, tiled=True)  29.9 us
    ppermute x6, starting transfers between devices, rims_y(): return (lax.ppermute(other, axes, y_one), lax.ppermute(own, axes, y_two))  16.3 us
    ppermute x4, waiting for transfers between devices, rims_x(): lax.ppermute(cross, 'slab', cross_swaps)  14.7 us
    all_to_all x2, waiting for transfers between devices, turn(): lax.all_to_all(pieces, 'slab', split_axis=0, concat_axis=0, tiled=True)  13.8 us
    ppermute x4, starting transfers between devices, rims_x(): lax.ppermute(cross, 'slab', cross_swaps)  13.3 us
    ppermute x3, starting transfers between devices, shards(): lax.ppermute(block, 'rep', [(r, (r + step) % reps) for r in range(reps)])  10.5 us
  transfers between devices with their start and end apart: 19, of which 11 were waited for; matrix products, arithmetic and copies ran while one was open for 1% of the time, Pallas kernels for 11%

profile of v6, /device:TPU:1, one launch (start us, length us, event | category | flops | bytes accessed | tf_op | source)
XLA Modules:
  0.0 210.2 jit_solution(2073168016941084618)
XLA Ops:
  0.0 1.0 copy-done.1
  1.0 1.2 store_tiles.1
  2.2 20.7 %all-to-all-start = ((f32[128,8,128]{2,1,0:T(8,128)}), f32[128,8,128]{2,1,0:T(8,128)S(1)}, u32[]{:S(2)}, u32[]{:S(2)}) async-start(f32[128,8,128]{2,1,0:T(8,128)} %store_tiles.1), calls=%async_computation | async-start | bytes 1048576 | tf_op jit(solution)/shard_map/all_to_all | solution.py:529
  22.9 0.0 copy-start.2
  23.0 0.7 copy-done.2
  23.6 3.8 %pack_rows.1 = (f32[520,128]{1,0:T(8,128)S(1)}, f32[520,128]{1,0:T(8,128)S(1)}, f32[520,128]{1,0:T(8,128)S(1)}, f32[520,128]{1,0:T(8,128)S(1)}) custom-call(s32[1]{0:T(128)} %bitcast.2.rep_ref, f32[1280,128]{1,0:T(8,128)S(1)} %copy-done, f32[10,128]{1,0:T(8,128)S(1)} %bitcast.15, s32[10,128]{1,0:T(8,128)S(1)} %bitcast.16, s32[10,128]{1,0:T(8,128)S(1)} %bitcast.17), custom_call_target="tpu_custom_call" | custom-call | tf_op jit(solution)/shard_map/pack_rows/pallas_call | solution.py:32
  27.4 3.1 %collective-permute-start.2 = (f32[520,128]{1,0:T(8,128)S(1)}, f32[520,128]{1,0:T(8,128)S(1)}, u32[]{:S(2)}, u32[]{:S(2)}) collective-permute-start(f32[520,128]{1,0:T(8,128)S(1)} %get-tuple-element.48), channel_id=1, source_target_pairs={{0,1},{1,2},{2,3},{3,0},{4,5},{5,6},{6,7},{7,4},{8,9},{9,10},{10,1... | collective-permute-start | bytes 798728 | tf_op jit(solution)/shard_map/ppermute | solution.py:547
  30.6 4.4 %collective-permute-start.1 = (f32[520,128]{1,0:T(8,128)S(1)}, f32[520,128]{1,0:T(8,128)S(1)}, u32[]{:S(2)}, u32[]{:S(2)}) collective-permute-start(f32[520,128]{1,0:T(8,128)S(1)} %get-tuple-element.47), channel_id=1, source_target_pairs={{0,2},{1,3},{2,0},{3,1},{4,6},{5,7},{6,4},{7,5},{8,10},{9,11},{10,... | collective-permute-start | bytes 798728 | tf_op jit(solution)/shard_map/ppermute | solution.py:547
  34.9 3.1 %collective-permute-start = (f32[520,128]{1,0:T(8,128)S(1)}, f32[520,128]{1,0:T(8,128)S(1)}, u32[]{:S(2)}, u32[]{:S(2)}) collective-permute-start(f32[520,128]{1,0:T(8,128)S(1)} %get-tuple-element.46), channel_id=1, source_target_pairs={{0,3},{1,0},{2,1},{3,2},{4,7},{5,4},{6,5},{7,6},{8,11},{9,8},{10,9... | collective-permute-start | bytes 798728 | tf_op jit(solution)/shard_map/ppermute | solution.py:547
  38.0 0.8 begin_sums.1
  38.8 0.0 collective-permute-done.2.got_ref
  38.8 0.8 add_sums.2
  39.5 4.7 %collective-permute-done.1.got_ref = f32[520,128]{1,0:T(8,128)S(1)} collective-permute-done((f32[520,128]{1,0:T(8,128)S(1)}, f32[520,128]{1,0:T(8,128)S(1)}, u32[]{:S(2)}, u32[]{:S(2)}) %collective-permute-start.1) | collective-permute-done | bytes 266272 | tf_op jit(solution)/shard_map/ppermute | solution.py:547
  44.2 0.8 add_sums.3
  45.0 0.4 collective-permute-done.got_ref
  45.4 2.0 observe.1
  47.4 8.7 %all-to-all-done = f32[128,8,128]{2,1,0:T(8,128)S(1)} async-done(((f32[128,8,128]{2,1,0:T(8,128)}), f32[128,8,128]{2,1,0:T(8,128)S(1)}, u32[]{:S(2)}, u32[]{:S(2)}) %all-to-all-start) | async-done | bytes 524320 | tf_op jit(solution)/shard_map/all_to_all | solution.py:529
  56.1 9.2 %all-to-all-start.1 = ((f32[128,8,128]{2,1,0:T(8,128)}), f32[128,8,128]{2,1,0:T(8,128)S(1)}, u32[]{:S(2)}, u32[]{:S(2)}) async-start(f32[128,8,128]{2,1,0:T(8,128)} %observe.1), calls=%async_computation.1 | async-start | bytes 1048576 | tf_op jit(solution)/shard_map/all_to_all | solution.py:529
  65.4 0.6 arrive.1
  65.9 0.0 copy-start.6
  65.9 1.3 collective-permute-start.3
  67.2 4.2 %collective-permute-start.4 = (f32[480,128]{1,0:T(8,128)S(1)}, f32[480,128]{1,0:T(8,128)S(1)}, u32[]{:S(2)}, u32[]{:S(2)}) collective-permute-start(f32[480,128]{1,0:T(8,128)S(1)} %get-tuple-element.60), channel_id=1, source_target_pairs={{128,0},{129,1},{130,2},{131,3},{4,132},{5,133},{6,134},{7,135},{1... | collective-permute-start | bytes 737288 | tf_op jit(solution)/shard_map/ppermute | solution.py:526
  71.5 0.7 reduce_sum.9
  72.1 0.7 broadcast_divide_fusion.taps_ref
  72.8 1.5 own_share.6.part_ref
  74.3 3.2 %collective-permute-done.4.far_ref = f32[480,128]{1,0:T(8,128)S(1)} collective-permute-done((f32[480,128]{1,0:T(8,128)S(1)}, f32[480,128]{1,0:T(8,128)S(1)}, u32[]{:S(2)}, u32[]{:S(2)}) %collective-permute-start.4) | collective-permute-done | bytes 245792 | tf_op jit(solution)/shard_map/ppermute | solution.py:526
  77.5 1.0 along_y_first.1
  78.5 4.5 %collective-permute-start.5 = (f32[480,128]{1,0:T(8,128)S(1)}, f32[480,128]{1,0:T(8,128)S(1)}, u32[]{:S(2)}, u32[]{:S(2)}) collective-permute-start(f32[480,128]{1,0:T(8,128)S(1)} %get-tuple-element.62), channel_id=1, source_target_pairs={{4,8},{8,4},{12,16},{16,12},{20,24},{24,20},{28,32},{32,28},{36,40... | collective-permute-start | bytes 737288 | tf_op jit(solution)/shard_map/ppermute | solution.py:516
  83.0 0.0 copy-start.5
  83.0 1.9 collective-permute-start.6
  85.0 0.2 axial_band.1.band_ref
  85.1 1.5 own_share.7.part_ref
  86.6 5.8 %collective-permute-done.5.cross_ref = f32[480,128]{1,0:T(8,128)S(1)} collective-permute-done((f32[480,128]{1,0:T(8,128)S(1)}, f32[480,128]{1,0:T(8,128)S(1)}, u32[]{:S(2)}, u32[]{:S(2)}) %collective-permute-start.5) | collective-permute-done | bytes 245792 | tf_op jit(solution)/shard_map/ppermute | solution.py:516
  92.4 1.1 blur.1.blurred_ref
  93.5 5.0 %all-to-all-done.1 = f32[128,8,128]{2,1,0:T(8,128)S(1)} async-done(((f32[128,8,128]{2,1,0:T(8,128)}), f32[128,8,128]{2,1,0:T(8,128)S(1)}, u32[]{:S(2)}, u32[]{:S(2)}) %all-to-all-start.1) | async-done | bytes 524320 | tf_op jit(solution)/shard_map/all_to_all | solution.py:529
  98.6 0.8 first_ratio.1
  99.4 1.3 collective-permute-start.7
  100.7 4.0 %collective-permute-start.10 = (f32[960,128]{1,0:T(8,128)S(1)}, f32[960,128]{1,0:T(8,128)S(1)}, u32[]{:S(2)}, u32[]{:S(2)}) collective-permute-start(f32[960,128]{1,0:T(8,128)S(1)} %get-tuple-element.72), channel_id=1, source_target_pairs={{128,0},{129,1},{130,2},{131,3},{4,132},{5,133},{6,134},{7,135},{1... | collective-permute-start | bytes 1474568 | tf_op jit(solution)/shard_map/ppermute | solution.py:526
  104.7 1.8 own_share.8.part_ref
  106.5 3.0 %collective-permute-start.8 = (f32[480,128]{1,0:T(8,128)S(1)}, f32[480,128]{1,0:T(8,128)S(1)}, u32[]{:S(2)}, u32[]{:S(2)}) collective-permute-start(f32[480,128]{1,0:T(8,128)S(1)} %get-tuple-element.69), channel_id=1, source_target_pairs={{4,8},{8,4},{12,16},{16,12},{20,24},{24,20},{28,32},{32,28},{36,40... | collective-permute-start | bytes 737288 | tf_op jit(solution)/shard_map/ppermute | solution.py:516
  109.5 1.9 collective-permute-start.9
  111.4 2.9 %collective-permute-done.8.cross_ref = f32[480,128]{1,0:T(8,128)S(1)} collective-permute-done((f32[480,128]{1,0:T(8,128)S(1)}, f32[480,128]{1,0:T(8,128)S(1)}, u32[]{:S(2)}, u32[]{:S(2)}) %collective-permute-start.8) | collective-permute-done | bytes 245792 | tf_op jit(solution)/shard_map/ppermute | solution.py:516
  114.3 1.1 near_share.1.near_ref
  115.4 1.8 wide_rows.1
  117.2 2.9 %collective-permute-start.11 = (f32[960,128]{1,0:T(8,128)S(1)}, f32[960,128]{1,0:T(8,128)S(1)}, u32[]{:S(2)}, u32[]{:S(2)}) collective-permute-start(f32[960,128]{1,0:T(8,128)S(1)} %get-tuple-element.74), channel_id=1, source_target_pairs={{4,8},{8,4},{12,16},{16,12},{20,24},{24,20},{28,32},{32,28},{36,40... | collective-permute-start | bytes 1474568 | tf_op jit(solution)/shard_map/ppermute | solution.py:516
  120.2 1.9 collective-permute-start.12
  122.1 0.4 extend.1.start_ref
  122.5 2.4 %own_share.9.part_ref = f32[2048,128]{1,0:T(8,128)S(1)} custom-call(f32[31]{0:T(128)S(1)} %broadcast_divide_fusion.taps_ref, f32[2048,128]{1,0:T(8,128)S(1)} %get-tuple-element.73.mid_ref), custom_call_target="tpu_custom_call" | custom-call | tf_op jit(solution)/shard_map/own_share/pallas_call | solution.py:32
  124.9 2.5 %collective-permute-done.11.cross_ref = f32[960,128]{1,0:T(8,128)S(1)} collective-permute-done((f32[960,128]{1,0:T(8,128)S(1)}, f32[960,128]{1,0:T(8,128)S(1)}, u32[]{:S(2)}, u32[]{:S(2)}) %collective-permute-start.11) | collective-permute-done | bytes 491552 | tf_op jit(solution)/shard_map/ppermute | solution.py:516
  127.4 3.0 %update_wide.1 = (f32[2048,128]{1,0:T(8,128)S(1)}, f32[1024,128]{1,0:T(8,128)S(1)}, f32[960,128]{1,0:T(8,128)S(1)}, f32[960,128]{1,0:T(8,128)S(1)}) custom-call(f32[31]{0:T(128)S(1)} %broadcast_divide_fusion.taps_ref, s32[1]{0:T(128)} %bitcast.side_ref, f32[2048,128]{1,0:T(8,128)S(1)} %own_share.9.part_ref, ...), custom_call_target="tpu_custom_call" | custom-call | tf_op jit(solution)/shard_map/update_wide/pallas_call | solution.py:32
  130.3 2.9 %collective-permute-start.13 = (f32[960,128]{1,0:T(8,128)S(1)}, f32[960,128]{1,0:T(8,128)S(1)}, u32[]{:S(2)}, u32[]{:S(2)}) collective-permute-start(f32[960,128]{1,0:T(8,128)S(1)} %get-tuple-element.78), channel_id=1, source_target_pairs={{4,8},{8,4},{12,16},{16,12},{20,24},{24,20},{28,32},{32,28},{36,40... | collective-permute-start | bytes 1474568 | tf_op jit(solution)/shard_map/ppermute | solution.py:516
  133.3 1.9 collective-permute-start.14
  135.2 0.1 extend_x.1.seen_ref
  135.3 1.8 own_share.10.part_ref
  137.1 3.4 %collective-permute-done.13.cross_ref = f32[960,128]{1,0:T(8,128)S(1)} collective-permute-done((f32[960,128]{1,0:T(8,128)S(1)}, f32[960,128]{1,0:T(8,128)S(1)}, u32[]{:S(2)}, u32[]{:S(2)}) %collective-permute-start.13) | collective-permute-done | bytes 491552 | tf_op jit(solution)/shard_map/ppermute | solution.py:516
  140.5 4.4 %blur_ratio.1 = (f32[1024,128]{1,0:T(8,128)S(1)}, f32[480,128]{1,0:T(8,128)S(1)}, f32[480,128]{1,0:T(8,128)S(1)}) custom-call(f32[31]{0:T(128)S(1)} %broadcast_divide_fusion.taps_ref, s32[1]{0:T(128)} %bitcast.side_ref, f32[2048,128]{1,0:T(8,128)S(1)} %own_share.10.part_ref, f32[960,128]{1,0:T(8,128)S(1)} %collective-permute-done.13.cross_ref, ...), custom_call_target="tpu_custom_call" | custom-call | tf_op jit(solution)/shard_map/blur_ratio/pallas_call | solution.py:32
  144.9 1.3 collective-permute-start.15
  146.2 4.2 %collective-permute-start.16 = (f32[480,128]{1,0:T(8,128)S(1)}, f32[480,128]{1,0:T(8,128)S(1)}, u32[]{:S(2)}, u32[]{:S(2)}) collective-permute-start(f32[480,128]{1,0:T(8,128)S(1)} %get-tuple-element.85), channel_id=1, source_target_pairs={{128,0},{129,1},{130,2},{131,3},{4,132},{5,133},{6,134},{7,135},{1... | collective-permute-start | bytes 737288 | tf_op jit(solution)/shard_map/ppermute | solution.py:526
  150.5 1.5 own_share.11.part_ref
  151.9 1.3 collective-permute-done.15.near_ref
  153.2 0.3 collective-permute-done.16.far_ref
  153.6 1.3 last_update.1
  154.8 54.2 %all_to_all.15.got_ref = f32[128,8,128]{2,1,0:T(8,128)S(1)} all-to-all(f32[128,8,128]{2,1,0:T(8,128)S(1)} %bitcast.13), channel_id=1, replica_groups=mesh['slab'=128,'rep'=4] {'slab'}, dimensions={0} | all-to-all | bytes 1048576 | tf_op jit(solution)/shard_map/all_to_all | solution.py:529
  209.0 1.2 plane_of.1
  (16 shorter events, 0.0 us)
Async XLA Ops:
  0.0 1.0 copy-start.1
  2.2 20.7 %copy-start = (f32[1280,128]{1,0:T(8,128)S(1)}, f32[1280,128]{1,0:T(8,128)}, u32[]{:S(2)}) copy-start(f32[1280,128]{1,0:T(8,128)} %rows_ref.1) | copy-start | bytes 1966084
  2.2 20.7 %copy-start.3 = (s32[1280]{0:T(1024)S(1)}, s32[1280]{0:T(1024)}, u32[]{:S(2)}) copy-start(s32[1280]{0:T(1024)} %param.9) | copy-start | bytes 15364
  2.2 20.7 %copy-start.4 = (s32[1280]{0:T(1024)S(1)}, s32[1280]{0:T(1024)}, u32[]{:S(2)}) copy-start(s32[1280]{0:T(1024)} %param.10) | copy-start | bytes 15364
  2.2 53.9 %all-to-all-start = ((f32[128,8,128]{2,1,0:T(8,128)}), f32[128,8,128]{2,1,0:T(8,128)S(1)}, u32[]{:S(2)}, u32[]{:S(2)}) async-start(f32[128,8,128]{2,1,0:T(8,128)} %store_tiles.1), calls=%async_computation | async-start | bytes 1048576 | tf_op jit(solution)/shard_map/all_to_all | solution.py:529
  22.9 0.7 copy-start.2
  27.4 11.3 %collective-permute-start.2 = (f32[520,128]{1,0:T(8,128)S(1)}, f32[520,128]{1,0:T(8,128)S(1)}, u32[]{:S(2)}, u32[]{:S(2)}) collective-permute-start(f32[520,128]{1,0:T(8,128)S(1)} %get-tuple-element.48), channel_id=1, source_target_pairs={{0,1},{1,2},{2,3},{3,0},{4,5},{5,6},{6,7},{7,4},{8,9},{9,10},{10,1... | collective-permute-start | bytes 798728 | tf_op jit(solution)/shard_map/ppermute | solution.py:547
  30.6 13.7 %collective-permute-start.1 = (f32[520,128]{1,0:T(8,128)S(1)}, f32[520,128]{1,0:T(8,128)S(1)}, u32[]{:S(2)}, u32[]{:S(2)}) collective-permute-start(f32[520,128]{1,0:T(8,128)S(1)} %get-tuple-element.47), channel_id=1, source_target_pairs={{0,2},{1,3},{2,0},{3,1},{4,6},{5,7},{6,4},{7,5},{8,10},{9,11},{10,... | collective-permute-start | bytes 798728 | tf_op jit(solution)/shard_map/ppermute | solution.py:547
  34.9 10.5 %collective-permute-start = (f32[520,128]{1,0:T(8,128)S(1)}, f32[520,128]{1,0:T(8,128)S(1)}, u32[]{:S(2)}, u32[]{:S(2)}) collective-permute-start(f32[520,128]{1,0:T(8,128)S(1)} %get-tuple-element.46), channel_id=1, source_target_pairs={{0,3},{1,0},{2,1},{3,2},{4,7},{5,4},{6,5},{7,6},{8,11},{9,8},{10,9... | collective-permute-start | bytes 798728 | tf_op jit(solution)/shard_map/ppermute | solution.py:547
  56.1 42.4 %all-to-all-start.1 = ((f32[128,8,128]{2,1,0:T(8,128)}), f32[128,8,128]{2,1,0:T(8,128)S(1)}, u32[]{:S(2)}, u32[]{:S(2)}) async-start(f32[128,8,128]{2,1,0:T(8,128)} %observe.1), calls=%async_computation.1 | async-start | bytes 1048576 | tf_op jit(solution)/shard_map/all_to_all | solution.py:529
  65.9 5.5 %copy-start.6 = (f32[31]{0:T(128)S(1)}, f32[31]{0:T(128)}, u32[]{:S(2)}) copy-start(f32[31]{0:T(128)} %param.12) | copy-start | bytes 376
  65.9 8.4 %collective-permute-start.3 = (f32[480,128]{1,0:T(8,128)S(1)}, f32[480,128]{1,0:T(8,128)S(1)}, u32[]{:S(2)}, u32[]{:S(2)}) collective-permute-start(f32[480,128]{1,0:T(8,128)S(1)} %get-tuple-element.59), channel_id=1, source_target_pairs={{0,128},{1,129},{2,130},{3,131},{132,4},{133,5},{134,6},{135,7},{8... | collective-permute-start | bytes 737288 | tf_op jit(solution)/shard_map/ppermute | solution.py:526
  67.2 10.2 %collective-permute-start.4 = (f32[480,128]{1,0:T(8,128)S(1)}, f32[480,128]{1,0:T(8,128)S(1)}, u32[]{:S(2)}, u32[]{:S(2)}) collective-permute-start(f32[480,128]{1,0:T(8,128)S(1)} %get-tuple-element.60), channel_id=1, source_target_pairs={{128,0},{129,1},{130,2},{131,3},{4,132},{5,133},{6,134},{7,135},{1... | collective-permute-start | bytes 737288 | tf_op jit(solution)/shard_map/ppermute | solution.py:526
  78.5 13.9 %collective-permute-start.5 = (f32[480,128]{1,0:T(8,128)S(1)}, f32[480,128]{1,0:T(8,128)S(1)}, u32[]{:S(2)}, u32[]{:S(2)}) collective-permute-start(f32[480,128]{1,0:T(8,128)S(1)} %get-tuple-element.62), channel_id=1, source_target_pairs={{4,8},{8,4},{12,16},{16,12},{20,24},{24,20},{28,32},{32,28},{36,40... | collective-permute-start | bytes 737288 | tf_op jit(solution)/shard_map/ppermute | solution.py:516
  83.0 1.9 copy-start.5
  83.0 9.4 %collective-permute-start.6 = (f32[480,128]{1,0:T(8,128)S(1)}, f32[480,128]{1,0:T(8,128)S(1)}, u32[]{:S(2)}, u32[]{:S(2)}) collective-permute-start(f32[480,128]{1,0:T(8,128)S(1)} %get-tuple-element.63), channel_id=1, source_target_pairs={{0,4},{4,0},{8,12},{12,8},{16,20},{20,16},{24,28},{28,24},{32,36},... | collective-permute-start | bytes 737288 | tf_op jit(solution)/shard_map/ppermute | solution.py:516
  99.4 14.9 %collective-permute-start.7 = (f32[960,128]{1,0:T(8,128)S(1)}, f32[960,128]{1,0:T(8,128)S(1)}, u32[]{:S(2)}, u32[]{:S(2)}) collective-permute-start(f32[960,128]{1,0:T(8,128)S(1)} %get-tuple-element.68), channel_id=1, source_target_pairs={{0,128},{1,129},{2,130},{3,131},{132,4},{133,5},{134,6},{135,7},{8... | collective-permute-start | bytes 1474568 | tf_op jit(solution)/shard_map/ppermute | solution.py:526
  100.7 14.7 %collective-permute-start.10 = (f32[960,128]{1,0:T(8,128)S(1)}, f32[960,128]{1,0:T(8,128)S(1)}, u32[]{:S(2)}, u32[]{:S(2)}) collective-permute-start(f32[960,128]{1,0:T(8,128)S(1)} %get-tuple-element.72), channel_id=1, source_target_pairs={{128,0},{129,1},{130,2},{131,3},{4,132},{5,133},{6,134},{7,135},{1... | collective-permute-start | bytes 1474568 | tf_op jit(solution)/shard_map/ppermute | solution.py:526
  106.5 7.8 %collective-permute-start.8 = (f32[480,128]{1,0:T(8,128)S(1)}, f32[480,128]{1,0:T(8,128)S(1)}, u32[]{:S(2)}, u32[]{:S(2)}) collective-permute-start(f32[480,128]{1,0:T(8,128)S(1)} %get-tuple-element.69), channel_id=1, source_target_pairs={{4,8},{8,4},{12,16},{16,12},{20,24},{24,20},{28,32},{32,28},{36,40... | collective-permute-start | bytes 737288 | tf_op jit(solution)/shard_map/ppermute | solution.py:516
  109.5 4.8 %collective-permute-start.9 = (f32[480,128]{1,0:T(8,128)S(1)}, f32[480,128]{1,0:T(8,128)S(1)}, u32[]{:S(2)}, u32[]{:S(2)}) collective-permute-start(f32[480,128]{1,0:T(8,128)S(1)} %get-tuple-element.70), channel_id=1, source_target_pairs={{0,4},{4,0},{8,12},{12,8},{16,20},{20,16},{24,28},{28,24},{32,36},... | collective-permute-start | bytes 737288 | tf_op jit(solution)/shard_map/ppermute | solution.py:516
  117.2 10.1 %collective-permute-start.11 = (f32[960,128]{1,0:T(8,128)S(1)}, f32[960,128]{1,0:T(8,128)S(1)}, u32[]{:S(2)}, u32[]{:S(2)}) collective-permute-start(f32[960,128]{1,0:T(8,128)S(1)} %get-tuple-element.74), channel_id=1, source_target_pairs={{4,8},{8,4},{12,16},{16,12},{20,24},{24,20},{28,32},{32,28},{36,40... | collective-permute-start | bytes 1474568 | tf_op jit(solution)/shard_map/ppermute | solution.py:516
  120.2 7.2 %collective-permute-start.12 = (f32[960,128]{1,0:T(8,128)S(1)}, f32[960,128]{1,0:T(8,128)S(1)}, u32[]{:S(2)}, u32[]{:S(2)}) collective-permute-start(f32[960,128]{1,0:T(8,128)S(1)} %get-tuple-element.75), channel_id=1, source_target_pairs={{0,4},{4,0},{8,12},{12,8},{16,20},{20,16},{24,28},{28,24},{32,36},... | collective-permute-start | bytes 1474568 | tf_op jit(solution)/shard_map/ppermute | solution.py:516
  130.3 10.1 %collective-permute-start.13 = (f32[960,128]{1,0:T(8,128)S(1)}, f32[960,128]{1,0:T(8,128)S(1)}, u32[]{:S(2)}, u32[]{:S(2)}) collective-permute-start(f32[960,128]{1,0:T(8,128)S(1)} %get-tuple-element.78), channel_id=1, source_target_pairs={{4,8},{8,4},{12,16},{16,12},{20,24},{24,20},{28,32},{32,28},{36,40... | collective-permute-start | bytes 1474568 | tf_op jit(solution)/shard_map/ppermute | solution.py:516
  133.3 7.2 %collective-permute-start.14 = (f32[960,128]{1,0:T(8,128)S(1)}, f32[960,128]{1,0:T(8,128)S(1)}, u32[]{:S(2)}, u32[]{:S(2)}) collective-permute-start(f32[960,128]{1,0:T(8,128)S(1)} %get-tuple-element.79), channel_id=1, source_target_pairs={{0,4},{4,0},{8,12},{12,8},{16,20},{20,16},{24,28},{28,24},{32,36},... | collective-permute-start | bytes 1474568 | tf_op jit(solution)/shard_map/ppermute | solution.py:516
  144.9 8.3 %collective-permute-start.15 = (f32[480,128]{1,0:T(8,128)S(1)}, f32[480,128]{1,0:T(8,128)S(1)}, u32[]{:S(2)}, u32[]{:S(2)}) collective-permute-start(f32[480,128]{1,0:T(8,128)S(1)} %get-tuple-element.84), channel_id=1, source_target_pairs={{0,128},{1,129},{2,130},{3,131},{132,4},{133,5},{134,6},{135,7},{8... | collective-permute-start | bytes 737288 | tf_op jit(solution)/shard_map/ppermute | solution.py:526
  146.2 7.3 %collective-permute-start.16 = (f32[480,128]{1,0:T(8,128)S(1)}, f32[480,128]{1,0:T(8,128)S(1)}, u32[]{:S(2)}, u32[]{:S(2)}) collective-permute-start(f32[480,128]{1,0:T(8,128)S(1)} %get-tuple-element.85), channel_id=1, source_target_pairs={{128,0},{129,1},{130,2},{131,3},{4,132},{5,133},{6,134},{7,135},{1... | collective-permute-start | bytes 737288 | tf_op jit(solution)/shard_map/ppermute | solution.py:526

commit v7 on v6

--- a/solution.py
+++ b/solution.py
@@ -99,8 +99,17 @@
     out_ref[...] = jnp.where(jnp.abs(a - b) <= 31, rolled, 0.0)
 
 
+def split_rows(rows_ref, blend, split_ref):
+    chunks = blend.shape[0]
+    columns = jnp.concatenate([blend, jnp.zeros((LANES - chunks, LANES), F32)], axis=0).T
+    for c in range(chunks):
+        high, low = halves(rows_ref[c * LANES : (c + 1) * LANES, :] * columns[:, c : c + 1])
+        split_ref[c * LANES : (c + 1) * LANES, :LANES] = high
+        split_ref[c * LANES : (c + 1) * LANES, LANES:] = low
+
+
 def pack_rows(rep_ref, rows_ref, blend_ref, route_ref, line_ref, *refs):
-    out_refs, (split_ref, hot_ref) = refs[:OWNERS], refs[OWNERS:]
+    out_refs, (split_ref, hot_ref) = refs[: OWNERS - 1], refs[OWNERS - 1 :]
     chunks = rows_ref.shape[0] // LANES
     blend = blend_ref[...]
     route = route_ref[...]
@@ -121,13 +130,7 @@
         offset = jnp.dot(before, totals, preferred_element_type=F32)
         rank = (upto_here + offset)[:chunks] - 1.0
         key = key + jnp.where(route == owner, rank, 0.0).astype(jnp.int32)
-    square = jnp.concatenate([blend, jnp.zeros((LANES - chunks, LANES), F32)], axis=0)
-    columns = square.T
-    for c in range(chunks):
-        weighted = rows_ref[c * LANES : (c + 1) * LANES, :] * columns[:, c : c + 1]
-        high, low = halves(weighted)
-        split_ref[c * LANES : (c + 1) * LANES, :LANES] = high
-        split_ref[c * LANES : (c + 1) * LANES, LANES:] = low
+    split_rows(rows_ref, blend, split_ref)
     first, second, third = thirds(blend)
     upper = line // 32
     parts = [first, second, third, upper.astype(BF16), (line - upper * 32).astype(BF16)]
@@ -140,7 +143,7 @@
         ],
         axis=1,
     ).astype(BF16)
-    for step, out_ref in enumerate(out_refs):
+    for step, out_ref in enumerate(out_refs, 1):
         owner = (rep_ref[0] + step) % OWNERS
         slot = lax.broadcasted_iota(jnp.int32, (CAPACITY, LANES), 0) + owner * CAPACITY
         for c in range(chunks):
@@ -178,8 +181,24 @@
     return rows[:, :LANES] + rows[:, LANES:], weights[:, 0:1] + weights[:, 1:2] + weights[:, 2:3]
 
 
-def begin_sums(got_ref, total_ref, weight_ref, hot_ref):
-    total_ref[...], weight_ref[...] = line_sums(got_ref, hot_ref)
+def begin_sums(rep_ref, rows_ref, blend_ref, route_ref, line_ref, total_ref, weight_ref, split_ref, hot_ref):
+    blend = blend_ref[...]
+    chunks = blend.shape[0]
+    split_rows(rows_ref, blend, split_ref)
+    where = jnp.where(route_ref[...] == rep_ref[0], line_ref[...], -1)
+    at = lax.broadcasted_iota(jnp.int32, (LINES, LANES), 0)
+    for c in range(chunks):
+        hot = jnp.where(at == where[c : c + 1, :], 1.0, 0.0)
+        hot_ref[:, c * LANES : (c + 1) * LANES] = hot.astype(BF16)
+    hot = hot_ref[...]
+    rows = jnp.dot(hot, split_ref[...], preferred_element_type=F32)
+    parts = [
+        jnp.concatenate([p.astype(F32)[c : c + 1] for c in range(chunks)], axis=1) for p in thirds(blend)
+    ]
+    stacked = jnp.concatenate(parts + [jnp.zeros((5, chunks * LANES), F32)], axis=0).astype(BF16)
+    weights = lax.dot_general(hot, stacked, (((1,), (1,)), ((), ())), preferred_element_type=F32)
+    total_ref[...] = rows[:, :LANES] + rows[:, LANES:]
+    weight_ref[...] = weights[:, 0:1] + weights[:, 1:2] + weights[:, 2:3]
 
 
 def add_sums(got_ref, before_ref, before_weight_ref, total_ref, weight_ref, hot_ref):
@@ -532,24 +551,29 @@
 
     arrived = turn(call(store_tiles, [PIECES], [], start.reshape(LINES, LANES))[0])
     band = call(axial_band, [(Z, LANES)], [((8, LANES), F32)], psf_z[None, :])[0]
-    sent = call(
-        pack_rows,
-        [(CAPACITY + META, LANES)] * OWNERS,
-        [((chunks * LANES, 2 * LANES), BF16), ((CAPACITY, chunks * LANES), BF16)],
+    rows = (
         lax.axis_index("rep").reshape(1),
         camera_rows,
         blend.reshape(chunks, LANES),
         route.reshape(chunks, LANES),
         line.reshape(chunks, LANES),
+    )
+    split = ((chunks * LANES, 2 * LANES), BF16)
+    sent = call(
+        pack_rows,
+        [(CAPACITY + META, LANES)] * (OWNERS - 1),
+        [split, ((CAPACITY, chunks * LANES), BF16)],
+        *rows,
         smem=1,
     )
     got = [
-        block if step == 0 else lax.ppermute(block, "rep", [(r, (r + step) % reps) for r in range(reps)])
-        for step, block in enumerate(sent)
+        lax.ppermute(block, "rep", [(r, (r + step) % reps) for r in range(reps)])
+        for step, block in enumerate(sent, 1)
     ]
     hot = [((LINES, CAPACITY), BF16)]
-    sums = call(begin_sums, [(LINES, LANES), (LINES, 1)], hot, got[0])
-    for block in got[1:-1]:
+    own_hot = ((LINES, chunks * LANES), BF16)
+    sums = call(begin_sums, [(LINES, LANES), (LINES, 1)], [split, own_hot], *rows, smem=1)
+    for block in got[:-1]:
         sums = call(add_sums, [(LINES, LANES), (LINES, 1)], hot, block, *sums)
     seen_pieces = call(observe, [PIECES], hot + [((LINES, LANES), F32)], got[-1], *sums)[0]
     arrived, seen_pieces = lax.optimization_barrier((arrived, seen_pieces))

time: 211 us -> 210 us (level)
  no operation moved by 1% of the time
where the time goes in v7:
time: 210 us; the launch traced here: 209 us
  starting transfers between devices  76.7 us (37%)
  blocking collectives  54.2 us (26%)
  waiting for transfers between devices  38.3 us (18%)
  Pallas kernels  36.5 us (17%)
    all_to_all x1, blocking collectives, turn(): lax.all_to_all(pieces, 'slab', split_axis=0, concat_axis=0, tiled=True)  54.2 us
    pallas_call x25, Pallas kernels, call(): pl.pallas_call(kernel, out_shape=outs, in_specs=specs, out_specs=tuple((p...  36.5 us
    all_to_all x2, starting transfers between devices, turn(): lax.all_to_all(pieces, 'slab', split_axis=0, concat_axis=0, tiled=True)  28.9 us
    ppermute x6, starting transfers between devices, rims_y(): return (lax.ppermute(other, axes, y_one), lax.ppermute(own, axes, y_two))  16.3 us
    all_to_all x2, waiting for transfers between devices, turn(): lax.all_to_all(pieces, 'slab', split_axis=0, concat_axis=0, tiled=True)  14.7 us
    ppermute x4, waiting for transfers between devices, rims_x(): lax.ppermute(cross, 'slab', cross_swaps)  14.7 us
    ppermute x4, starting transfers between devices, rims_x(): lax.ppermute(cross, 'slab', cross_swaps)  13.2 us
    ppermute x3, starting transfers between devices, shards(): lax.ppermute(block, 'rep', [(r, (r + step) % reps) for r in range(reps)])  10.5 us
  transfers between devices with their start and end apart: 19, of which 11 were waited for; matrix products, arithmetic and copies ran while one was open for 1% of the time, Pallas kernels for 11%

profile of v7, /device:TPU:1, one launch (start us, length us, event | category | flops | bytes accessed | tf_op | source)
XLA Modules:
  0.0 209.2 jit_solution(10857078263079000862)
XLA Ops:
  0.0 1.0 copy-done.1
  1.0 1.2 store_tiles.1
  2.2 20.7 %all-to-all-start = ((f32[128,8,128]{2,1,0:T(8,128)}), f32[128,8,128]{2,1,0:T(8,128)S(1)}, u32[]{:S(2)}, u32[]{:S(2)}) async-start(f32[128,8,128]{2,1,0:T(8,128)} %store_tiles.1), calls=%async_computation | async-start | bytes 1048576 | tf_op jit(solution)/shard_map/all_to_all | solution.py:548
  22.9 0.0 copy-start.2
  23.0 0.7 copy-done.2
  23.6 2.8 %pack_rows.1 = (f32[520,128]{1,0:T(8,128)S(1)}, f32[520,128]{1,0:T(8,128)S(1)}, f32[520,128]{1,0:T(8,128)S(1)}) custom-call(s32[1]{0:T(128)} %bitcast.2.rep_ref, f32[1280,128]{1,0:T(8,128)S(1)} %copy-done, f32[10,128]{1,0:T(8,128)S(1)} %bitcast.15, s32[10,128]{1,0:T(8,128)S(1)} %bitcast.17, s32[10,128]{1,0:T(8,128)S(1)} %bitcast.19), custom_call_target="tpu_custom_call" | custom-call | tf_op jit(solution)/shard_map/pack_rows/pallas_call | solution.py:32
  26.5 3.1 %collective-permute-start.2 = (f32[520,128]{1,0:T(8,128)S(1)}, f32[520,128]{1,0:T(8,128)S(1)}, u32[]{:S(2)}, u32[]{:S(2)}) collective-permute-start(f32[520,128]{1,0:T(8,128)S(1)} %get-tuple-element.47), channel_id=1, source_target_pairs={{0,1},{1,2},{2,3},{3,0},{4,5},{5,6},{6,7},{7,4},{8,9},{9,10},{10,1... | collective-permute-start | bytes 798728 | tf_op jit(solution)/shard_map/ppermute | solution.py:570
  29.6 4.4 %collective-permute-start.1 = (f32[520,128]{1,0:T(8,128)S(1)}, f32[520,128]{1,0:T(8,128)S(1)}, u32[]{:S(2)}, u32[]{:S(2)}) collective-permute-start(f32[520,128]{1,0:T(8,128)S(1)} %get-tuple-element.46), channel_id=1, source_target_pairs={{0,2},{1,3},{2,0},{3,1},{4,6},{5,7},{6,4},{7,5},{8,10},{9,11},{10,... | collective-permute-start | bytes 798728 | tf_op jit(solution)/shard_map/ppermute | solution.py:570
  34.0 3.1 %collective-permute-start = (f32[520,128]{1,0:T(8,128)S(1)}, f32[520,128]{1,0:T(8,128)S(1)}, u32[]{:S(2)}, u32[]{:S(2)}) collective-permute-start(f32[520,128]{1,0:T(8,128)S(1)} %get-tuple-element.45), channel_id=1, source_target_pairs={{0,3},{1,0},{2,1},{3,2},{4,7},{5,4},{6,5},{7,6},{8,11},{9,8},{10,9... | collective-permute-start | bytes 798728 | tf_op jit(solution)/shard_map/ppermute | solution.py:570
  37.0 1.8 begin_sums.1
  38.8 0.0 collective-permute-done.2.got_ref
  38.8 0.8 add_sums.2
  39.6 3.7 %collective-permute-done.1.got_ref = f32[520,128]{1,0:T(8,128)S(1)} collective-permute-done((f32[520,128]{1,0:T(8,128)S(1)}, f32[520,128]{1,0:T(8,128)S(1)}, u32[]{:S(2)}, u32[]{:S(2)}) %collective-permute-start.1) | collective-permute-done | bytes 266272 | tf_op jit(solution)/shard_map/ppermute | solution.py:570
  43.3 0.8 add_sums.3
  44.0 0.4 collective-permute-done.got_ref
  44.5 2.0 observe.1
  46.4 9.7 %all-to-all-done = f32[128,8,128]{2,1,0:T(8,128)S(1)} async-done(((f32[128,8,128]{2,1,0:T(8,128)}), f32[128,8,128]{2,1,0:T(8,128)S(1)}, u32[]{:S(2)}, u32[]{:S(2)}) %all-to-all-start) | async-done | bytes 524320 | tf_op jit(solution)/shard_map/all_to_all | solution.py:548
  56.1 8.2 %all-to-all-start.1 = ((f32[128,8,128]{2,1,0:T(8,128)}), f32[128,8,128]{2,1,0:T(8,128)S(1)}, u32[]{:S(2)}, u32[]{:S(2)}) async-start(f32[128,8,128]{2,1,0:T(8,128)} %observe.1), calls=%async_computation.1 | async-start | bytes 1048576 | tf_op jit(solution)/shard_map/all_to_all | solution.py:548
  64.4 0.6 arrive.1
  65.0 0.0 copy-start.6
  65.0 1.3 collective-permute-start.3
  66.3 4.2 %collective-permute-start.4 = (f32[480,128]{1,0:T(8,128)S(1)}, f32[480,128]{1,0:T(8,128)S(1)}, u32[]{:S(2)}, u32[]{:S(2)}) collective-permute-start(f32[480,128]{1,0:T(8,128)S(1)} %get-tuple-element.58), channel_id=1, source_target_pairs={{128,0},{129,1},{130,2},{131,3},{4,132},{5,133},{6,134},{7,135},{1... | collective-permute-start | bytes 737288 | tf_op jit(solution)/shard_map/ppermute | solution.py:545
  70.5 0.7 reduce_sum.9
  71.2 0.7 broadcast_divide_fusion.taps_ref
  71.8 1.5 own_share.6.part_ref
  73.3 3.2 %collective-permute-done.4.far_ref = f32[480,128]{1,0:T(8,128)S(1)} collective-permute-done((f32[480,128]{1,0:T(8,128)S(1)}, f32[480,128]{1,0:T(8,128)S(1)}, u32[]{:S(2)}, u32[]{:S(2)}) %collective-permute-start.4) | collective-permute-done | bytes 245792 | tf_op jit(solution)/shard_map/ppermute | solution.py:545
  76.5 1.0 along_y_first.1
  77.6 4.5 %collective-permute-start.5 = (f32[480,128]{1,0:T(8,128)S(1)}, f32[480,128]{1,0:T(8,128)S(1)}, u32[]{:S(2)}, u32[]{:S(2)}) collective-permute-start(f32[480,128]{1,0:T(8,128)S(1)} %get-tuple-element.60), channel_id=1, source_target_pairs={{4,8},{8,4},{12,16},{16,12},{20,24},{24,20},{28,32},{32,28},{36,40... | collective-permute-start | bytes 737288 | tf_op jit(solution)/shard_map/ppermute | solution.py:535
  82.0 0.0 copy-start.5
  82.0 1.9 collective-permute-start.6
  84.0 0.2 axial_band.1.band_ref
  84.2 1.5 own_share.7.part_ref
  85.6 5.8 %collective-permute-done.5.cross_ref = f32[480,128]{1,0:T(8,128)S(1)} collective-permute-done((f32[480,128]{1,0:T(8,128)S(1)}, f32[480,128]{1,0:T(8,128)S(1)}, u32[]{:S(2)}, u32[]{:S(2)}) %collective-permute-start.5) | collective-permute-done | bytes 245792 | tf_op jit(solution)/shard_map/ppermute | solution.py:535
  91.5 1.1 blur.1.blurred_ref
  92.6 5.0 %all-to-all-done.1 = f32[128,8,128]{2,1,0:T(8,128)S(1)} async-done(((f32[128,8,128]{2,1,0:T(8,128)}), f32[128,8,128]{2,1,0:T(8,128)S(1)}, u32[]{:S(2)}, u32[]{:S(2)}) %all-to-all-start.1) | async-done | bytes 524320 | tf_op jit(solution)/shard_map/all_to_all | solution.py:548
  97.6 0.8 first_ratio.1
  98.4 1.3 collective-permute-start.7
  99.7 4.0 %collective-permute-start.10 = (f32[960,128]{1,0:T(8,128)S(1)}, f32[960,128]{1,0:T(8,128)S(1)}, u32[]{:S(2)}, u32[]{:S(2)}) collective-permute-start(f32[960,128]{1,0:T(8,128)S(1)} %get-tuple-element.70), channel_id=1, source_target_pairs={{128,0},{129,1},{130,2},{131,3},{4,132},{5,133},{6,134},{7,135},{1... | collective-permute-start | bytes 1474568 | tf_op jit(solution)/shard_map/ppermute | solution.py:545
  103.8 1.8 own_share.8.part_ref
  105.6 3.0 %collective-permute-start.8 = (f32[480,128]{1,0:T(8,128)S(1)}, f32[480,128]{1,0:T(8,128)S(1)}, u32[]{:S(2)}, u32[]{:S(2)}) collective-permute-start(f32[480,128]{1,0:T(8,128)S(1)} %get-tuple-element.67), channel_id=1, source_target_pairs={{4,8},{8,4},{12,16},{16,12},{20,24},{24,20},{28,32},{32,28},{36,40... | collective-permute-start | bytes 737288 | tf_op jit(solution)/shard_map/ppermute | solution.py:535
  108.5 1.9 collective-permute-start.9
  110.4 2.9 %collective-permute-done.8.cross_ref = f32[480,128]{1,0:T(8,128)S(1)} collective-permute-done((f32[480,128]{1,0:T(8,128)S(1)}, f32[480,128]{1,0:T(8,128)S(1)}, u32[]{:S(2)}, u32[]{:S(2)}) %collective-permute-start.8) | collective-permute-done | bytes 245792 | tf_op jit(solution)/shard_map/ppermute | solution.py:535
  113.4 1.1 near_share.1.near_ref
  114.5 1.8 wide_rows.1
  116.3 2.9 %collective-permute-start.11 = (f32[960,128]{1,0:T(8,128)S(1)}, f32[960,128]{1,0:T(8,128)S(1)}, u32[]{:S(2)}, u32[]{:S(2)}) collective-permute-start(f32[960,128]{1,0:T(8,128)S(1)} %get-tuple-element.72), channel_id=1, source_target_pairs={{4,8},{8,4},{12,16},{16,12},{20,24},{24,20},{28,32},{32,28},{36,40... | collective-permute-start | bytes 1474568 | tf_op jit(solution)/shard_map/ppermute | solution.py:535
  119.2 1.9 collective-permute-start.12
  121.1 0.4 extend.1.start_ref
  121.5 2.4 %own_share.9.part_ref = f32[2048,128]{1,0:T(8,128)S(1)} custom-call(f32[31]{0:T(128)S(1)} %broadcast_divide_fusion.taps_ref, f32[2048,128]{1,0:T(8,128)S(1)} %get-tuple-element.71.mid_ref), custom_call_target="tpu_custom_call" | custom-call | tf_op jit(solution)/shard_map/own_share/pallas_call | solution.py:32
  123.9 2.5 %collective-permute-done.11.cross_ref = f32[960,128]{1,0:T(8,128)S(1)} collective-permute-done((f32[960,128]{1,0:T(8,128)S(1)}, f32[960,128]{1,0:T(8,128)S(1)}, u32[]{:S(2)}, u32[]{:S(2)}) %collective-permute-start.11) | collective-permute-done | bytes 491552 | tf_op jit(solution)/shard_map/ppermute | solution.py:535
  126.4 3.0 %update_wide.1 = (f32[2048,128]{1,0:T(8,128)S(1)}, f32[1024,128]{1,0:T(8,128)S(1)}, f32[960,128]{1,0:T(8,128)S(1)}, f32[960,128]{1,0:T(8,128)S(1)}) custom-call(f32[31]{0:T(128)S(1)} %broadcast_divide_fusion.taps_ref, s32[1]{0:T(128)} %bitcast.side_ref, f32[2048,128]{1,0:T(8,128)S(1)} %own_share.9.part_ref, ...), custom_call_target="tpu_custom_call" | custom-call | tf_op jit(solution)/shard_map/update_wide/pallas_call | solution.py:32
  129.4 2.9 %collective-permute-start.13 = (f32[960,128]{1,0:T(8,128)S(1)}, f32[960,128]{1,0:T(8,128)S(1)}, u32[]{:S(2)}, u32[]{:S(2)}) collective-permute-start(f32[960,128]{1,0:T(8,128)S(1)} %get-tuple-element.76), channel_id=1, source_target_pairs={{4,8},{8,4},{12,16},{16,12},{20,24},{24,20},{28,32},{32,28},{36,40... | collective-permute-start | bytes 1474568 | tf_op jit(solution)/shard_map/ppermute | solution.py:535
  132.3 1.9 collective-permute-start.14
  134.2 0.1 extend_x.1.seen_ref
  134.3 1.8 own_share.10.part_ref
  136.1 3.4 %collective-permute-done.13.cross_ref = f32[960,128]{1,0:T(8,128)S(1)} collective-permute-done((f32[960,128]{1,0:T(8,128)S(1)}, f32[960,128]{1,0:T(8,128)S(1)}, u32[]{:S(2)}, u32[]{:S(2)}) %collective-permute-start.13) | collective-permute-done | bytes 491552 | tf_op jit(solution)/shard_map/ppermute | solution.py:535
  139.5 4.4 %blur_ratio.1 = (f32[1024,128]{1,0:T(8,128)S(1)}, f32[480,128]{1,0:T(8,128)S(1)}, f32[480,128]{1,0:T(8,128)S(1)}) custom-call(f32[31]{0:T(128)S(1)} %broadcast_divide_fusion.taps_ref, s32[1]{0:T(128)} %bitcast.side_ref, f32[2048,128]{1,0:T(8,128)S(1)} %own_share.10.part_ref, f32[960,128]{1,0:T(8,128)S(1)} %collective-permute-done.13.cross_ref, ...), custom_call_target="tpu_custom_call" | custom-call | tf_op jit(solution)/shard_map/blur_ratio/pallas_call | solution.py:32
  144.0 1.3 collective-permute-start.15
  145.3 4.2 %collective-permute-start.16 = (f32[480,128]{1,0:T(8,128)S(1)}, f32[480,128]{1,0:T(8,128)S(1)}, u32[]{:S(2)}, u32[]{:S(2)}) collective-permute-start(f32[480,128]{1,0:T(8,128)S(1)} %get-tuple-element.83), channel_id=1, source_target_pairs={{128,0},{129,1},{130,2},{131,3},{4,132},{5,133},{6,134},{7,135},{1... | collective-permute-start | bytes 737288 | tf_op jit(solution)/shard_map/ppermute | solution.py:545
  149.5 1.5 own_share.11.part_ref
  151.0 1.3 collective-permute-done.15.near_ref
  152.3 0.3 collective-permute-done.16.far_ref
  152.6 1.3 last_update.1
  153.9 54.2 %all_to_all.15.got_ref = f32[128,8,128]{2,1,0:T(8,128)S(1)} all-to-all(f32[128,8,128]{2,1,0:T(8,128)S(1)} %bitcast.13), channel_id=1, replica_groups=mesh['slab'=128,'rep'=4] {'slab'}, dimensions={0} | all-to-all | bytes 1048576 | tf_op jit(solution)/shard_map/all_to_all | solution.py:548
  208.0 1.2 plane_of.1
  (16 shorter events, 0.0 us)
Async XLA Ops:
  0.0 1.0 copy-start.1
  2.2 20.7 %copy-start = (f32[1280,128]{1,0:T(8,128)S(1)}, f32[1280,128]{1,0:T(8,128)}, u32[]{:S(2)}) copy-start(f32[1280,128]{1,0:T(8,128)} %rows_ref.3) | copy-start | bytes 1966084
  2.2 20.7 %copy-start.3 = (s32[1280]{0:T(1024)S(1)}, s32[1280]{0:T(1024)}, u32[]{:S(2)}) copy-start(s32[1280]{0:T(1024)} %param.9) | copy-start | bytes 15364
  2.2 20.7 %copy-start.4 = (s32[1280]{0:T(1024)S(1)}, s32[1280]{0:T(1024)}, u32[]{:S(2)}) copy-start(s32[1280]{0:T(1024)} %param.10) | copy-start | bytes 15364
  2.2 53.9 %all-to-all-start = ((f32[128,8,128]{2,1,0:T(8,128)}), f32[128,8,128]{2,1,0:T(8,128)S(1)}, u32[]{:S(2)}, u32[]{:S(2)}) async-start(f32[128,8,128]{2,1,0:T(8,128)} %store_tiles.1), calls=%async_computation | async-start | bytes 1048576 | tf_op jit(solution)/shard_map/all_to_all | solution.py:548
  22.9 0.7 copy-start.2
  26.5 12.3 %collective-permute-start.2 = (f32[520,128]{1,0:T(8,128)S(1)}, f32[520,128]{1,0:T(8,128)S(1)}, u32[]{:S(2)}, u32[]{:S(2)}) collective-permute-start(f32[520,128]{1,0:T(8,128)S(1)} %get-tuple-element.47), channel_id=1, source_target_pairs={{0,1},{1,2},{2,3},{3,0},{4,5},{5,6},{6,7},{7,4},{8,9},{9,10},{10,1... | collective-permute-start | bytes 798728 | tf_op jit(solution)/shard_map/ppermute | solution.py:570
  29.6 13.7 %collective-permute-start.1 = (f32[520,128]{1,0:T(8,128)S(1)}, f32[520,128]{1,0:T(8,128)S(1)}, u32[]{:S(2)}, u32[]{:S(2)}) collective-permute-start(f32[520,128]{1,0:T(8,128)S(1)} %get-tuple-element.46), channel_id=1, source_target_pairs={{0,2},{1,3},{2,0},{3,1},{4,6},{5,7},{6,4},{7,5},{8,10},{9,11},{10,... | collective-permute-start | bytes 798728 | tf_op jit(solution)/shard_map/ppermute | solution.py:570
  34.0 10.5 %collective-permute-start = (f32[520,128]{1,0:T(8,128)S(1)}, f32[520,128]{1,0:T(8,128)S(1)}, u32[]{:S(2)}, u32[]{:S(2)}) collective-permute-start(f32[520,128]{1,0:T(8,128)S(1)} %get-tuple-element.45), channel_id=1, source_target_pairs={{0,3},{1,0},{2,1},{3,2},{4,7},{5,4},{6,5},{7,6},{8,11},{9,8},{10,9... | collective-permute-start | bytes 798728 | tf_op jit(solution)/shard_map/ppermute | solution.py:570
  56.1 41.5 %all-to-all-start.1 = ((f32[128,8,128]{2,1,0:T(8,128)}), f32[128,8,128]{2,1,0:T(8,128)S(1)}, u32[]{:S(2)}, u32[]{:S(2)}) async-start(f32[128,8,128]{2,1,0:T(8,128)} %observe.1), calls=%async_computation.1 | async-start | bytes 1048576 | tf_op jit(solution)/shard_map/all_to_all | solution.py:548
  65.0 5.5 %copy-start.6 = (f32[31]{0:T(128)S(1)}, f32[31]{0:T(128)}, u32[]{:S(2)}) copy-start(f32[31]{0:T(128)} %param.12) | copy-start | bytes 376
  65.0 8.4 %collective-permute-start.3 = (f32[480,128]{1,0:T(8,128)S(1)}, f32[480,128]{1,0:T(8,128)S(1)}, u32[]{:S(2)}, u32[]{:S(2)}) collective-permute-start(f32[480,128]{1,0:T(8,128)S(1)} %get-tuple-element.57), channel_id=1, source_target_pairs={{0,128},{1,129},{2,130},{3,131},{132,4},{133,5},{134,6},{135,7},{8... | collective-permute-start | bytes 737288 | tf_op jit(solution)/shard_map/ppermute | solution.py:545
  66.3 10.2 %collective-permute-start.4 = (f32[480,128]{1,0:T(8,128)S(1)}, f32[480,128]{1,0:T(8,128)S(1)}, u32[]{:S(2)}, u32[]{:S(2)}) collective-permute-start(f32[480,128]{1,0:T(8,128)S(1)} %get-tuple-element.58), channel_id=1, source_target_pairs={{128,0},{129,1},{130,2},{131,3},{4,132},{5,133},{6,134},{7,135},{1... | collective-permute-start | bytes 737288 | tf_op jit(solution)/shard_map/ppermute | solution.py:545
  77.6 13.9 %collective-permute-start.5 = (f32[480,128]{1,0:T(8,128)S(1)}, f32[480,128]{1,0:T(8,128)S(1)}, u32[]{:S(2)}, u32[]{:S(2)}) collective-permute-start(f32[480,128]{1,0:T(8,128)S(1)} %get-tuple-element.60), channel_id=1, source_target_pairs={{4,8},{8,4},{12,16},{16,12},{20,24},{24,20},{28,32},{32,28},{36,40... | collective-permute-start | bytes 737288 | tf_op jit(solution)/shard_map/ppermute | solution.py:535
  82.0 1.9 copy-start.5
  82.0 9.4 %collective-permute-start.6 = (f32[480,128]{1,0:T(8,128)S(1)}, f32[480,128]{1,0:T(8,128)S(1)}, u32[]{:S(2)}, u32[]{:S(2)}) collective-permute-start(f32[480,128]{1,0:T(8,128)S(1)} %get-tuple-element.61), channel_id=1, source_target_pairs={{0,4},{4,0},{8,12},{12,8},{16,20},{20,16},{24,28},{28,24},{32,36},... | collective-permute-start | bytes 737288 | tf_op jit(solution)/shard_map/ppermute | solution.py:535
  98.4 14.9 %collective-permute-start.7 = (f32[960,128]{1,0:T(8,128)S(1)}, f32[960,128]{1,0:T(8,128)S(1)}, u32[]{:S(2)}, u32[]{:S(2)}) collective-permute-start(f32[960,128]{1,0:T(8,128)S(1)} %get-tuple-element.66), channel_id=1, source_target_pairs={{0,128},{1,129},{2,130},{3,131},{132,4},{133,5},{134,6},{135,7},{8... | collective-permute-start | bytes 1474568 | tf_op jit(solution)/shard_map/ppermute | solution.py:545
  99.7 14.7 %collective-permute-start.10 = (f32[960,128]{1,0:T(8,128)S(1)}, f32[960,128]{1,0:T(8,128)S(1)}, u32[]{:S(2)}, u32[]{:S(2)}) collective-permute-start(f32[960,128]{1,0:T(8,128)S(1)} %get-tuple-element.70), channel_id=1, source_target_pairs={{128,0},{129,1},{130,2},{131,3},{4,132},{5,133},{6,134},{7,135},{1... | collective-permute-start | bytes 1474568 | tf_op jit(solution)/shard_map/ppermute | solution.py:545
  105.6 7.8 %collective-permute-start.8 = (f32[480,128]{1,0:T(8,128)S(1)}, f32[480,128]{1,0:T(8,128)S(1)}, u32[]{:S(2)}, u32[]{:S(2)}) collective-permute-start(f32[480,128]{1,0:T(8,128)S(1)} %get-tuple-element.67), channel_id=1, source_target_pairs={{4,8},{8,4},{12,16},{16,12},{20,24},{24,20},{28,32},{32,28},{36,40... | collective-permute-start | bytes 737288 | tf_op jit(solution)/shard_map/ppermute | solution.py:535
  108.5 4.9 %collective-permute-start.9 = (f32[480,128]{1,0:T(8,128)S(1)}, f32[480,128]{1,0:T(8,128)S(1)}, u32[]{:S(2)}, u32[]{:S(2)}) collective-permute-start(f32[480,128]{1,0:T(8,128)S(1)} %get-tuple-element.68), channel_id=1, source_target_pairs={{0,4},{4,0},{8,12},{12,8},{16,20},{20,16},{24,28},{28,24},{32,36},... | collective-permute-start | bytes 737288 | tf_op jit(solution)/shard_map/ppermute | solution.py:535
  116.3 10.1 %collective-permute-start.11 = (f32[960,128]{1,0:T(8,128)S(1)}, f32[960,128]{1,0:T(8,128)S(1)}, u32[]{:S(2)}, u32[]{:S(2)}) collective-permute-start(f32[960,128]{1,0:T(8,128)S(1)} %get-tuple-element.72), channel_id=1, source_target_pairs={{4,8},{8,4},{12,16},{16,12},{20,24},{24,20},{28,32},{32,28},{36,40... | collective-permute-start | bytes 1474568 | tf_op jit(solution)/shard_map/ppermute | solution.py:535
  119.2 7.2 %collective-permute-start.12 = (f32[960,128]{1,0:T(8,128)S(1)}, f32[960,128]{1,0:T(8,128)S(1)}, u32[]{:S(2)}, u32[]{:S(2)}) collective-permute-start(f32[960,128]{1,0:T(8,128)S(1)} %get-tuple-element.73), channel_id=1, source_target_pairs={{0,4},{4,0},{8,12},{12,8},{16,20},{20,16},{24,28},{28,24},{32,36},... | collective-permute-start | bytes 1474568 | tf_op jit(solution)/shard_map/ppermute | solution.py:535
  129.4 10.1 %collective-permute-start.13 = (f32[960,128]{1,0:T(8,128)S(1)}, f32[960,128]{1,0:T(8,128)S(1)}, u32[]{:S(2)}, u32[]{:S(2)}) collective-permute-start(f32[960,128]{1,0:T(8,128)S(1)} %get-tuple-element.76), channel_id=1, source_target_pairs={{4,8},{8,4},{12,16},{16,12},{20,24},{24,20},{28,32},{32,28},{36,40... | collective-permute-start | bytes 1474568 | tf_op jit(solution)/shard_map/ppermute | solution.py:535
  132.3 7.2 %collective-permute-start.14 = (f32[960,128]{1,0:T(8,128)S(1)}, f32[960,128]{1,0:T(8,128)S(1)}, u32[]{:S(2)}, u32[]{:S(2)}) collective-permute-start(f32[960,128]{1,0:T(8,128)S(1)} %get-tuple-element.77), channel_id=1, source_target_pairs={{0,4},{4,0},{8,12},{12,8},{16,20},{20,16},{24,28},{28,24},{32,36},... | collective-permute-start | bytes 1474568 | tf_op jit(solution)/shard_map/ppermute | solution.py:535
  144.0 8.3 %collective-permute-start.15 = (f32[480,128]{1,0:T(8,128)S(1)}, f32[480,128]{1,0:T(8,128)S(1)}, u32[]{:S(2)}, u32[]{:S(2)}) collective-permute-start(f32[480,128]{1,0:T(8,128)S(1)} %get-tuple-element.82), channel_id=1, source_target_pairs={{0,128},{1,129},{2,130},{3,131},{132,4},{133,5},{134,6},{135,7},{8... | collective-permute-start | bytes 737288 | tf_op jit(solution)/shard_map/ppermute | solution.py:545
  145.3 7.3 %collective-permute-start.16 = (f32[480,128]{1,0:T(8,128)S(1)}, f32[480,128]{1,0:T(8,128)S(1)}, u32[]{:S(2)}, u32[]{:S(2)}) collective-permute-start(f32[480,128]{1,0:T(8,128)S(1)} %get-tuple-element.83), channel_id=1, source_target_pairs={{128,0},{129,1},{130,2},{131,3},{4,132},{5,133},{6,134},{7,135},{1... | collective-permute-start | bytes 737288 | tf_op jit(solution)/shard_map/ppermute | solution.py:545
